TPU v7x, 128 devices: a whole 4x4x4 slice. The times are simulated.
128 devices in a mesh: wide: 32 (over y_hi, z, x), tp: 4 (over y_lo, core).
Axes of the slice: x: 4, y: 4 (y_hi: 2, y_lo: 2; y = y_hi * 2 + y_lo), z: 4, core: 2. Of those that a mesh axis runs over, the one named last changes fastest.
Arguments:
- inputs: bfloat16 [16384, 2048], P(('wide', 'tp')), may hold values from -24 to 24
- positions: int32 [16384], P('wide'), may hold values from 0 to 2047, as said below
- attn_gain: bfloat16 [2048], P('wide'), may hold values from 0.5 to 1.5
- query_weight: bfloat16 [2048, 2048], P('wide', 'tp'), may hold values from -0.125 to 0.125
- key_weight: bfloat16 [2048, 256], P('wide', 'tp'), may hold values from -0.125 to 0.125
- value_weight: bfloat16 [2048, 256], P('wide', 'tp'), may hold values from -0.125 to 0.125
- out_weight: bfloat16 [2048, 2048], P('tp', 'wide'), may hold values from -2 to 2
- mlp_gain: bfloat16 [2048], P('wide'), may hold values from 0.5 to 1.5
- gate_weight: bfloat16 [2048, 5632], P('wide', 'tp'), may hold values from -0.125 to 0.125
- up_weight: bfloat16 [2048, 5632], P('wide', 'tp'), may hold values from -0.125 to 0.125
- down_weight: bfloat16 [5632, 2048], P('tp', 'wide'), may hold values from -0.078125 to 0.078125
- cotangent: bfloat16 [16384, 2048], P(('wide', 'tp')), may hold values from -24 to 24
Outputs:
- output: bfloat16 [16384, 2048], P(('wide', 'tp'))
- input_grad: float32 [16384, 2048], P(('wide', 'tp'))
- attn_gain_grad: float32 [2048], P('wide')
- query_weight_grad: float32 [2048, 2048], P('wide', 'tp')
- key_weight_grad: float32 [2048, 256], P('wide', 'tp')
- value_weight_grad: float32 [2048, 256], P('wide', 'tp')
- out_weight_grad: float32 [2048, 2048], P('tp', 'wide')
- mlp_gain_grad: float32 [2048], P('wide')
- gate_weight_grad: float32 [2048, 5632], P('wide', 'tp')
- up_weight_grad: float32 [2048, 5632], P('wide', 'tp')
- down_weight_grad: float32 [5632, 2048], P('tp', 'wide')
Inputs may be any that keep to these rules, and one draw needn't show every extreme that they name: positions[t] is the index of token t within its document; every sequence of 2048 tokens begins a document at its first token and holds one to four documents; exactly one sequence, drawn from the seed, is a single document.
All inputs are finite; a program needn't handle non-finite values.
Results may differ from a plain program's by a relative error of at most 0.03.
Values may be sent and summed in bfloat16 or wider, within the bound.
No kernel may reach another device: no remote copies, remote signals or barrier semaphores. Data moves between devices by JAX's collectives and lax.ppermute only.
A program may use at most 256 MiB of HBM per device.

v0:
```python
from functools import reduce
import math

import jax
import jax.numpy as jnp
from jax import lax
from jax.sharding import PartitionSpec as P

HEADS = 32
KV = 4
HD = 64
SEQ_DEVS = 4


epsilon = 1e-05
masked_fill = -1e30


def from_behind(block, axis, distance):
    devices = range(lax.axis_size(axis))
    route = [(i - distance, i) for i in devices if i - distance in devices]
    return lax.ppermute(block, axis, route)


def rotate(values, positions, sign):
    half = HD // 2
    heads = values.shape[1] // HD
    freqs = 10000.0 ** (-(jnp.arange(half, dtype=jnp.float32) * 2.0) / HD)
    angles = positions.astype(jnp.float32)[:, None] * freqs[None, :]
    cosine = jnp.cos(angles)[:, None, :]
    sine = sign * jnp.sin(angles)[:, None, :]
    shaped = values.reshape(values.shape[0], heads, HD)
    first = shaped[..., :half]
    second = shaped[..., half:]
    turned = jnp.concatenate([first * cosine - second * sine, second * cosine + first * sine], -1)
    return turned.reshape(values.shape)


def norm_rows(rows):
    values = rows.astype(jnp.float32)
    factor = lax.rsqrt(jnp.mean(values * values, -1, keepdims=True) + epsilon)
    return (values * factor, factor)


def norm_back(grad_normed, normed, factor):
    inner = jnp.mean(grad_normed * normed, -1, keepdims=True)
    return factor * (grad_normed - normed * inner)


def gather_rows(rows):
    return lax.all_gather(rows, "tp", axis=0, tiled=True)


def contract_last(left, right):
    return lax.dot_general(
        left, right, (((1,), (1,)), ((), ())), preferred_element_type=jnp.float32
    )


def contract_first(left, right):
    return lax.dot_general(
        left, right, (((0,), (0,)), ((), ())), preferred_element_type=jnp.float32
    )


def project_in(normed, matrix, gain):
    piece_matrix = lax.all_gather(matrix, "wide", axis=0, tiled=True)
    piece_gain = lax.all_gather(gain, "wide", axis=0, tiled=True)
    gain_piece = piece_gain.astype(jnp.float32)
    scaled_piece = (normed * gain_piece).astype(jnp.bfloat16)
    total = jnp.dot(scaled_piece, piece_matrix, preferred_element_type=jnp.float32)
    return (total, gain_piece, matrix)


def back_in(grad_out, source, normed, gain_all, factor):
    grad_normed = contract_last(grad_out, lax.all_gather(source, "wide", axis=0, tiled=True))
    scaled = (normed * gain_all).astype(jnp.bfloat16)
    grad_gain = jnp.sum(grad_normed * normed, 0)
    grad_matrix = contract_first(scaled, grad_out)
    grad_matrix, grad_gain = (
        lax.psum_scatter(
            grad_matrix.astype(jnp.bfloat16), "wide", scatter_dimension=0, tiled=True
        ).astype(jnp.float32),
        lax.psum_scatter(
            grad_gain.astype(jnp.bfloat16), "wide", scatter_dimension=0, tiled=True
        ).astype(jnp.float32),
    )
    partial_rows = norm_back(grad_normed * gain_all, normed, factor)
    return (
        lax.psum_scatter(
            partial_rows.astype(jnp.bfloat16), "tp", scatter_dimension=0, tiled=True
        ).astype(jnp.float32),
        grad_matrix,
        grad_gain,
    )


def project_out(mixed, matrix):
    whole = lax.all_gather(matrix, "wide", axis=1, tiled=True)
    return (
        lax.psum_scatter(
            jnp.dot(mixed, whole, preferred_element_type=jnp.float32).astype(jnp.bfloat16),
            "tp",
            scatter_dimension=0,
            tiled=True,
        ).astype(jnp.float32),
        whole,
    )


def back_out(grad_rows, mixed, matrix):
    grad_all = gather_rows(grad_rows)
    grad_mixed = contract_last(grad_all, lax.all_gather(matrix, "wide", axis=1, tiled=True))
    grad_matrix = contract_first(mixed, grad_all)
    grad_matrix = lax.psum_scatter(
        grad_matrix.astype(jnp.bfloat16), "wide", scatter_dimension=1, tiled=True
    ).astype(jnp.float32)
    return (grad_mixed, grad_matrix)


def per_device(
    inputs,
    positions,
    attn_gain,
    query_weight,
    key_weight,
    value_weight,
    out_weight,
    mlp_gain,
    gate_weight,
    up_weight,
    down_weight,
    cotangent,
):
    width_q = query_weight.shape[1]
    width_k = key_weight.shape[1]
    hidden_width = gate_weight.shape[1]
    kv_heads = width_k // HD
    groups = HEADS // KV
    span = positions.shape[0]
    scale = 1.0 / math.sqrt(HD)
    normed_in, factor_in = norm_rows(gather_rows(inputs))
    attn_matrix = jnp.concatenate([query_weight, key_weight, value_weight], 1)
    projected, gain_in, source_in = project_in(normed_in, attn_matrix, attn_gain)
    queries = (
        rotate(projected[:, :width_q], positions, 1.0)
        .astype(jnp.bfloat16)
        .reshape(span, kv_heads, groups, HD)
    )
    keys_own = rotate(projected[:, width_q : width_q + width_k], positions, 1.0).astype(
        jnp.bfloat16
    )
    values_own = projected[:, width_q + width_k :].astype(jnp.bfloat16)
    kv_block = jnp.concatenate([keys_own, values_own], 1)
    group = lax.axis_index("wide") % SEQ_DEVS
    places = jnp.arange(span, dtype=jnp.int32)
    query_place = group * span + places
    blocks = [kv_block]
    current = kv_block
    for distance in range(1, SEQ_DEVS):
        current = from_behind(current, "wide", 1)
        blocks.append(current)
    masked = []
    maxima = []
    for distance in range(SEQ_DEVS):
        keys_block = blocks[distance][:, :width_k].reshape(span, kv_heads, HD)
        key_place = (group - distance) * span + places
        visible = (
            (key_place[None, :] <= query_place[:, None])
            & (query_place[:, None] - key_place[None, :] <= positions[:, None])
            & (group >= distance)
        )
        raw = (
            jnp.einsum("qkgd,ckd->kgqc", queries, keys_block, preferred_element_type=jnp.float32)
            * scale
        )
        scores = jnp.where(visible[None, None], raw, masked_fill)
        masked.append(scores)
        maxima.append(jnp.max(scores, -1))
    top = reduce(jnp.maximum, maxima)
    total = jnp.zeros_like(top)
    for scores in masked:
        total = total + jnp.sum(jnp.exp(scores - top[..., None]), -1)
    log_total = top + jnp.log(total)
    mixed = jnp.zeros((span, kv_heads, groups, HD), jnp.float32)
    prob_list = []
    for distance in range(SEQ_DEVS):
        probs = jnp.exp(masked[distance] - log_total[..., None])
        values_block = blocks[distance][:, width_k:].reshape(span, kv_heads, HD)
        mixed = mixed + jnp.einsum(
            "kgqc,ckd->qkgd",
            probs.astype(jnp.bfloat16),
            values_block,
            preferred_element_type=jnp.float32,
        )
        prob_list.append(probs)
    mixed_low = mixed.astype(jnp.bfloat16).reshape(span, width_q)
    attn_rows, out_whole = project_out(mixed_low, out_weight)
    middle = inputs.astype(jnp.float32) + attn_rows
    normed_mid, factor_mid = norm_rows(gather_rows(middle.astype(jnp.bfloat16)))
    mlp_matrix = jnp.concatenate([gate_weight, up_weight], 1)
    gate_up, gain_mid, source_mid = project_in(normed_mid, mlp_matrix, mlp_gain)
    gate = gate_up[:, :hidden_width]
    up = gate_up[:, hidden_width:]
    sigmoid_gate = jax.nn.sigmoid(gate)
    hidden = (gate * sigmoid_gate * up).astype(jnp.bfloat16)
    mlp_rows, down_whole = project_out(hidden, down_weight)
    output = (middle + mlp_rows).astype(jnp.bfloat16)
    grad_hidden, down_grad = back_out(cotangent, hidden, down_weight)
    grad_gate = (grad_hidden * up * sigmoid_gate * (1.0 + gate * (1.0 - sigmoid_gate))).astype(
        jnp.bfloat16
    )
    grad_up = (grad_hidden * (gate * sigmoid_gate)).astype(jnp.bfloat16)
    mid_part, mlp_matrix_grad, mlp_gain_part = back_in(
        jnp.concatenate([grad_gate, grad_up], 1), source_mid, normed_mid, gain_mid, factor_mid
    )
    grad_middle = cotangent.astype(jnp.float32) + mid_part
    grad_mixed, out_grad = back_out(grad_middle.astype(jnp.bfloat16), mixed_low, out_weight)
    grad_heads = grad_mixed.astype(jnp.bfloat16).reshape(span, kv_heads, groups, HD)
    prob_grads = []
    delta = jnp.zeros_like(top)
    for distance in range(SEQ_DEVS):
        values_block = blocks[distance][:, width_k:].reshape(span, kv_heads, HD)
        prob_grad = jnp.einsum(
            "qkgd,ckd->kgqc", grad_heads, values_block, preferred_element_type=jnp.float32
        )
        delta = delta + jnp.sum(prob_list[distance] * prob_grad, -1)
        prob_grads.append(prob_grad)
    query_grad = jnp.zeros((span, kv_heads, groups, HD), jnp.float32)
    block_grads = []
    for distance in range(SEQ_DEVS):
        probs = prob_list[distance]
        keys_block = blocks[distance][:, :width_k].reshape(span, kv_heads, HD)
        raw_grad = (scale * probs * (prob_grads[distance] - delta[..., None])).astype(jnp.bfloat16)
        query_grad = query_grad + jnp.einsum(
            "kgqc,ckd->qkgd", raw_grad, keys_block, preferred_element_type=jnp.float32
        )
        key_grad = jnp.einsum(
            "kgqc,qkgd->ckd", raw_grad, queries, preferred_element_type=jnp.float32
        )
        value_grad = jnp.einsum(
            "kgqc,qkgd->ckd",
            probs.astype(jnp.bfloat16),
            grad_heads,
            preferred_element_type=jnp.float32,
        )
        block_grads.append(
            jnp.concatenate([key_grad.reshape(span, width_k), value_grad.reshape(span, width_k)], 1)
        )
    carried = block_grads[SEQ_DEVS - 1]
    for distance in range(SEQ_DEVS - 2, -1, -1):
        carried = (
            from_behind(carried.astype(jnp.bfloat16), "wide", -1).astype(carried.dtype)
            + block_grads[distance]
        )
    query_raw_grad = rotate(query_grad.reshape(span, width_q), positions, -1.0).astype(jnp.bfloat16)
    key_raw_grad = rotate(carried[:, :width_k], positions, -1.0).astype(jnp.bfloat16)
    value_raw_grad = carried[:, width_k:].astype(jnp.bfloat16)
    grad_projected = jnp.concatenate([query_raw_grad, key_raw_grad, value_raw_grad], 1)
    in_part, attn_matrix_grad, attn_gain_part = back_in(
        grad_projected, source_in, normed_in, gain_in, factor_in
    )
    input_grad = grad_middle + in_part
    attn_gain_grad, mlp_gain_grad = lax.psum((attn_gain_part, mlp_gain_part), "tp")
    return (
        output,
        input_grad,
        attn_gain_grad,
        attn_matrix_grad[:, :width_q],
        attn_matrix_grad[:, width_q : width_q + width_k],
        attn_matrix_grad[:, width_q + width_k :],
        out_grad,
        mlp_gain_grad,
        mlp_matrix_grad[:, :hidden_width],
        mlp_matrix_grad[:, hidden_width:],
        down_grad,
    )


def solution(mesh):
    return jax.shard_map(
        per_device,
        mesh=mesh,
        in_specs=(
            P(("wide", "tp"), None),
            P("wide"),
            P("wide"),
            P("wide", "tp"),
            P("wide", "tp"),
            P("wide", "tp"),
            P("tp", "wide"),
            P("wide"),
            P("wide", "tp"),
            P("wide", "tp"),
            P("tp", "wide"),
            P(("wide", "tp"), None),
        ),
        out_specs=(
            P(("wide", "tp"), None),
            P(("wide", "tp"), None),
            P("wide"),
            P("wide", "tp"),
            P("wide", "tp"),
            P("wide", "tp"),
            P("tp", "wide"),
            P("wide"),
            P("wide", "tp"),
            P("wide", "tp"),
            P("tp", "wide"),
        ),
        check_vma=False,
    )
```

profile of v0, /device:TPU:1, one launch (start us, length us, event | category | flops | bytes accessed | tf_op | source)
XLA Modules:
  0.0 1413.8 jit_solution(16325552124145338294)
XLA Ops:
  8.0 1.6 pad_maximum_fusion.11
  14.8 85.9 %all-reduce.6 = (bf16[2048]{0:T(1024)(128)(2,1)S(1)}, bf16[2048]{0:T(1024)(128)(2,1)S(1)}) all-reduce(bf16[2048]{0:T(1024)(128)(2,1)S(1)} %dynamic-update-slice, bf16[2048]{0:T(1024)(128)(2,1)S(1)} %dynamic-update-slice.1), channel_id=1, replica_groups=mesh['wide'=32,'tp'=4] {'wide'}, use_global_device_ids=true, to_apply=%add | all-reduce | flops 4096 | bytes 16384
  101.7 1.9 fusion.61
  103.7 2.3 fusion.34
  106.1 11.8 all-gather.11.cloned.1.call-done
  117.9 4.2 fusion.72
  127.5 2.6 collective-permute-start
  133.0 3.4 collective-permute-start.1
  136.4 4.7 fusion.25
  141.1 3.3 collective-permute-start.2
  144.5 4.7 fusion.26
  149.2 4.7 fusion.27
  153.9 11.9 exponential_reduce_fusion.2
  165.9 2.5 fusion.96
  168.4 5.9 convolution_add_fusion.5
  174.4 2.2 convolution_add_fusion.4
  176.6 2.2 fusion.53
  178.8 9.9 all-gather.13.cloned.1.call-done
  188.7 4.3 convolution_convert_fusion.4
  193.1 32.3 %reduce-scatter.9.cloned.1.call-done = bf16[128,2048]{1,0:T(8,128)(2,1)} async-done(((bf16[512,2048]{1,0:T(8,128)(2,1)}), bf16[128,2048]{1,0:T(8,128)(2,1)}) %reduce-scatter.9.cloned.1.call-update) | async-done | bytes 524304 | tf_op jit(solution)/shard_map/reduce_scatter | solution.py:101
  225.4 2.0 fusion.66
  229.8 28.1 %all-gather.15.cloned.1.call-done = bf16[512,2048]{1,0:T(8,128)(2,1)} async-done(((bf16[128,2048]{1,0:T(8,128)(2,1)}), bf16[512,2048]{1,0:T(8,128)(2,1)}) %all-gather.15.cloned.1.call-update) | async-done | bytes 2097168 | tf_op jit(solution)/shard_map/all_gather | solution.py:51
  257.8 2.1 fusion.41
  259.9 124.6 %all-gather.17.cloned.1.call-done = bf16[2048,2816]{1,0:T(8,128)(2,1)} async-done(((bf16[64,2816]{1,0:T(8,128)(2,1)}), bf16[2048,2816]{1,0:T(8,128)(2,1)}) %all-gather.17.cloned.1.call-update) | async-done | bytes 11534352 | tf_op jit(solution)/shard_map/all_gather | solution.py:67
  384.5 13.1 fusion.69
  397.6 16.3 %all-gather.21.cloned.1.call-done = bf16[512,2048]{1,0:T(8,128)(2,1)} async-done(((bf16[128,2048]{1,0:T(8,128)(2,1)}), bf16[512,2048]{1,0:T(8,128)(2,1)}) %all-gather.21.cloned.1.call-update) | async-done | bytes 2097168 | tf_op jit(solution)/shard_map/all_gather | solution.py:51
  413.9 92.6 %all-gather.19.cloned.1.call-done = bf16[1408,2048]{0,1:T(8,128)(2,1)} async-done(((bf16[1408,64]{0,1:T(8,128)(2,1)}), bf16[1408,2048]{0,1:T(8,128)(2,1)}) %all-gather.19.cloned.1.call-update) | async-done | bytes 5767184 | tf_op jit(solution)/shard_map/all_gather | solution.py:99
  506.5 11.4 multiply_convert_fusion.1
  517.9 8.2 fusion.40
  526.1 2.4 fusion.39
  528.6 26.7 %reduce-scatter.13.cloned.1.call-done = bf16[128,2048]{1,0:T(8,128)(2,1)} async-done(((bf16[512,2048]{1,0:T(8,128)(2,1)}), bf16[128,2048]{1,0:T(8,128)(2,1)}) %reduce-scatter.13.cloned.1.call-update) | async-done | bytes 524304 | tf_op jit(solution)/shard_map/reduce_scatter | solution.py:90
  555.3 2.0 fusion.67
  557.4 7.3 convolution_convert_fusion.5
  564.8 22.9 %all-gather.23.cloned.1.call-done = bf16[512,2048]{1,0:T(8,128)(2,1)} async-done(((bf16[128,2048]{1,0:T(8,128)(2,1)}), bf16[512,2048]{1,0:T(8,128)(2,1)}) %all-gather.23.cloned.1.call-update) | async-done | bytes 2097168 | tf_op jit(solution)/shard_map/all_gather | solution.py:51
  587.7 4.4 convolution_convert_fusion.3
  592.2 6.9 convolution_convert_fusion.1
  599.2 3.6 convolution_convert_fusion.6
  605.5 4.9 fusion.102
  611.3 19.7 %fusion.6 = (f32[8,512]{1,0:T(8,128)S(1)}, f32[8,512]{1,0:T(8,128)S(1)}, f32[8,512]{1,0:T(8,128)S(1)}, f32[8,512]{1,0:T(8,128)S(1)}, f32[512,512,8]{1,0,2:T(8,128)}) fusion(f32[512,512,8]{1,0,2:T(8,128)} %get-tuple-element.64, f32[8,512]{1,0:T(8,128)S(1)} %log_add_fusion, pred[512,512]{0,1:T(8,128)(4,1)S(1)} %copy-done.12, f32[512,512,8]{1,0,2:T(8,128)S(1)} %fusion.94, ...), kind=kOutput, calls=%fused_computation.17 | convolution fusion | flops 310362112 | bytes 68829184 | tf_op jit(solution)/shard_map/qkgd,ckd->kgqc/dot_general | solution.py:224
  631.0 27.5 %fusion.49 = (bf16[8,512,512]{1,2,0:T(8,128)(2,1)}, bf16[8,512,512]{1,2,0:T(8,128)(2,1)}, bf16[8,512,512]{1,2,0:T(8,128)(2,1)}, bf16[8,512,512]{1,2,0:T(8,128)(2,1)}) fusion(f32[512,512,8]{1,0,2:T(8,128)} %copy-done, f32[512,512,8]{1,0,2:T(8,128)} %get-tuple-element.58, f32[8,512]{1,0:T(8,128)S(1)} %add_add_fusion, f32[8,512]{1,0:T(8,128)S(1)} %log_add_fusion, ...), kind=kLoop, calls=%fused_computation.75 | loop fusion | flops 58720256 | bytes 84967424 | tf_op jit(solution)/shard_map/reshape.101
  658.5 3.6 fusion.57
  662.1 5.6 fusion.56
  667.8 1.8 collective-permute-start.3
  674.1 1.6 copy-done.4
  677.1 2.7 convolution_bitcast_fusion
  679.9 2.1 convolution_bitcast_fusion.2
  682.3 2.1 convolution_bitcast_fusion.4
  688.9 5.9 collective-permute-done.4
  694.8 1.6 collective-permute-start.5
  696.7 4.6 collective-permute-done.5
  701.7 2.8 fusion.33
  704.5 2.5 fusion.32
  707.1 3.5 convolution_convert_fusion.2
  710.7 11.2 convolution_convert_fusion
  723.1 2.1 add_convert_fusion
  725.2 84.5 %all-reduce.5 = (bf16[2048]{0:T(1024)(128)(2,1)S(1)}, bf16[2048]{0:T(1024)(128)(2,1)S(1)}) all-reduce(bf16[2048]{0:T(1024)(128)(2,1)S(1)} %get-tuple-element.13, bf16[2048]{0:T(1024)(128)(2,1)S(1)} %get-tuple-element.11), channel_id=6, replica_groups=mesh['wide'=32,'tp'=4] {'wide'}, use_global_device_ids=true, to_apply=%region_21.22.clone | all-reduce | flops 4096 | bytes 16384
  809.8 19.0 %all-reduce.4 = (f32[64]{0:T(128)}, f32[64]{0:T(128)}) all-reduce(f32[64]{0:T(128)S(1)} %dynamic-slice_convert_fusion.1, f32[64]{0:T(128)S(1)} %dynamic-slice_convert_fusion), channel_id=1, replica_groups=mesh['wide'=32,'tp'=4] {'tp'}, use_global_device_ids=true, to_apply=%region_22.23 | all-reduce | flops 128 | bytes 1024 | tf_op jit(solution)/shard_map/psum | solution.py:264
  830.3 149.8 %reduce-scatter.23.cloned.1.call-done = bf16[1408,64]{0,1:T(8,128)(2,1)} async-done(((bf16[1408,2048]{0,1:T(8,128)(2,1)}), bf16[1408,64]{0,1:T(8,128)(2,1)}) %reduce-scatter.23.cloned.1.call-update) | async-done | bytes 180240 | tf_op jit(solution)/shard_map/reduce_scatter | solution.py:115
  980.2 1.7 convert_element_type.240
  981.9 46.6 %reduce-scatter.15.cloned.1.call-done = bf16[128,2048]{1,0:T(8,128)(2,1)} async-done(((bf16[512,2048]{1,0:T(8,128)(2,1)}), bf16[128,2048]{1,0:T(8,128)(2,1)}) %reduce-scatter.15.cloned.1.call-update) | async-done | bytes 524304 | tf_op jit(solution)/shard_map/reduce_scatter | solution.py:90
  1028.5 2.2 convert_add_fusion
  1030.7 164.9 %reduce-scatter.17.cloned.1.call-done = bf16[64,640]{1,0:T(8,128)(2,1)} async-done(((bf16[2048,640]{1,0:T(8,128)(2,1)}), bf16[64,640]{1,0:T(8,128)(2,1)}) %reduce-scatter.17.cloned.1.call-update) | async-done | bytes 81936 | tf_op jit(solution)/shard_map/reduce_scatter | solution.py:81
  1198.6 206.3 %reduce-scatter.21.cloned.1.call-done = bf16[64,2816]{1,0:T(8,128)(2,1)} async-done(((bf16[2048,2816]{1,0:T(8,128)(2,1)}), bf16[64,2816]{1,0:T(8,128)(2,1)}) %reduce-scatter.21.cloned.1.call-update) | async-done | bytes 360464 | tf_op jit(solution)/shard_map/reduce_scatter | solution.py:81
  1404.8 1.9 fusion.120
  (221 shorter events, 37.2 us)
Async XLA Ops:
  7.2 96.5 %all-gather.9.cloned.1.call-start = ((), (), s32[]{:S(2)}) async-start(), calls=%async_computation.8 | async-start | bytes 2621440 | tf_op jit(solution)/shard_map/all_gather | solution.py:51
  7.9 110.0 %all-gather.11.cloned.1.call-start = ((), (), s32[]{:S(2)}) async-start(), calls=%async_computation.9 | async-start | bytes 2703360 | tf_op jit(solution)/shard_map/all_gather | solution.py:67
  9.6 179.1 %all-gather.13.cloned.1.call-start = ((), (), s32[]{:S(2)}) async-start(), calls=%async_computation.10 | async-start | bytes 2162688 | tf_op jit(solution)/shard_map/all_gather | solution.py:99
  10.3 215.1 %reduce-scatter.9.cloned.1.call-start = ((), (), s32[]{:S(2)}) async-start(), calls=%async_computation.11 | async-start | bytes 2621440 | tf_op jit(solution)/shard_map/reduce_scatter | solution.py:101
  10.4 115.4 %copy-start.44 = (f32[32]{0:T(128)}, f32[32]{0:T(128)S(1)}, u32[]{:S(2)}) copy-start(f32[32]{0:T(128)S(1)} %multiply_power_fusion) | copy-start | bytes 388
  11.1 114.7 %copy-start.38 = (f32[512]{0:T(512)}, f32[512]{0:T(512)S(1)}, u32[]{:S(2)}) copy-start(f32[512]{0:T(512)S(1)} %convert_element_type.192) | copy-start | bytes 6148
  100.7 21.4 %copy-start.40 = (f32[2048]{0:T(1024)}, f32[2048]{0:T(1024)S(1)}, u32[]{:S(2)}) copy-start(f32[2048]{0:T(1024)S(1)} %convert_element_type.190) | copy-start | bytes 24580
  101.7 28.4 %copy-start.19 = (f32[512,32]{0,1:T(8,128)}, f32[512,32]{0,1:T(8,128)S(1)}, u32[]{:S(2)}) copy-start(f32[512,32]{0,1:T(8,128)S(1)} %get-tuple-element.54) | copy-start | bytes 196612
  103.7 62.2 %copy-start.13 = (pred[512,512]{0,1:T(8,128)(4,1)}, pred[512,512]{0,1:T(8,128)(4,1)S(1)}, u32[]{:S(2)}) copy-start(pred[512,512]{0,1:T(8,128)(4,1)S(1)} %get-tuple-element.51) | copy-start | bytes 786436
  103.7 64.7 %copy-start.11 = (pred[512,512]{0,1:T(8,128)(4,1)}, pred[512,512]{0,1:T(8,128)(4,1)S(1)}, u32[]{:S(2)}) copy-start(pred[512,512]{0,1:T(8,128)(4,1)S(1)} %get-tuple-element.48) | copy-start | bytes 786436
  103.7 72.9 %copy-start.15 = (pred[512,512]{0,1:T(8,128)(4,1)}, pred[512,512]{0,1:T(8,128)(4,1)S(1)}, u32[]{:S(2)}) copy-start(pred[512,512]{0,1:T(8,128)(4,1)S(1)} %get-tuple-element.50) | copy-start | bytes 786436
  106.1 16.0 %copy-start.42 = (f32[512]{0:T(512)}, f32[512]{0:T(512)S(1)}, u32[]{:S(2)}) copy-start(f32[512]{0:T(512)S(1)} %add_rsqrt_fusion.1) | copy-start | bytes 6148
  126.1 6.9 copy-start.23
  126.1 6.9 copy-start.25
  127.5 5.5 collective-permute-start
  133.0 32.9 %copy-start.1 = (f32[512,512,8]{1,0,2:T(8,128)}, f32[512,512,8]{1,0,2:T(8,128)S(1)}, u32[]{:S(2)}) copy-start(f32[512,512,8]{1,0,2:T(8,128)S(1)} %get-tuple-element.62) | copy-start | bytes 25165828
  133.0 35.3 %copy-start.30 = (bf16[512,128]{0,1:T(8,128)(2,1)}, bf16[512,128]{0,1:T(8,128)(2,1)S(1)}, u32[]{:S(2)}) copy-start(bf16[512,128]{0,1:T(8,128)(2,1)S(1)} %collective-permute-done) | copy-start | bytes 393220
  133.0 8.1 collective-permute-start.1
  141.1 33.2 %copy-start.32 = (bf16[512,128]{0,1:T(8,128)(2,1)}, bf16[512,128]{0,1:T(8,128)(2,1)S(1)}, u32[]{:S(2)}) copy-start(bf16[512,128]{0,1:T(8,128)(2,1)S(1)} %collective-permute-done.1) | copy-start | bytes 393220
  141.1 8.1 collective-permute-start.2
  149.2 27.4 %copy-start.34 = (bf16[512,128]{0,1:T(8,128)(2,1)}, bf16[512,128]{0,1:T(8,128)(2,1)S(1)}, u32[]{:S(2)}) copy-start(bf16[512,128]{0,1:T(8,128)(2,1)S(1)} %collective-permute-done.2) | copy-start | bytes 393220
  165.9 8.5 slice-start.4
  168.4 6.0 slice-start.5
  168.4 8.2 slice-start.8
  178.8 9.9 copy-start.49
  188.7 36.6 %copy-start.9 = (bf16[128,2048]{1,0:T(8,128)(2,1)S(1)}, bf16[128,2048]{1,0:T(8,128)(2,1)}, u32[]{:S(2)}) copy-start(bf16[128,2048]{1,0:T(8,128)(2,1)} %param.12) | copy-start | bytes 1572868
  193.0 34.4 %copy-start.28 = (bf16[64,1408]{1,0:T(8,128)(2,1)S(1)}, bf16[64,1408]{1,0:T(8,128)(2,1)}, u32[]{:S(2)}) copy-start(bf16[64,1408]{1,0:T(8,128)(2,1)} %param.21) | copy-start | bytes 540676
  193.0 34.4 %copy-start.29 = (bf16[64,1408]{1,0:T(8,128)(2,1)S(1)}, bf16[64,1408]{1,0:T(8,128)(2,1)}, u32[]{:S(2)}) copy-start(bf16[64,1408]{1,0:T(8,128)(2,1)} %param.20) | copy-start | bytes 540676
  193.1 64.8 %all-gather.15.cloned.1.call-start = ((), (), s32[]{:S(2)}) async-start(), calls=%async_computation.12 | async-start | bytes 2621440 | tf_op jit(solution)/shard_map/all_gather | solution.py:51
  227.4 157.1 %all-gather.17.cloned.1.call-start = ((), (), s32[]{:S(2)}) async-start(), calls=%async_computation.13 | async-start | bytes 11894784 | tf_op jit(solution)/shard_map/all_gather | solution.py:67
  228.2 185.7 %all-gather.21.cloned.1.call-start = ((), (), s32[]{:S(2)}) async-start(), calls=%async_computation.16 | async-start | bytes 2621440 | tf_op jit(solution)/shard_map/all_gather | solution.py:51
  229.0 277.5 %all-gather.19.cloned.1.call-start = ((), (), s32[]{:S(2)}) async-start(), calls=%async_computation.14 | async-start | bytes 5947392 | tf_op jit(solution)/shard_map/all_gather | solution.py:99
  229.7 325.6 %reduce-scatter.13.cloned.1.call-start = ((), (), s32[]{:S(2)}) async-start(), calls=%async_computation.17 | async-start | bytes 2621440 | tf_op jit(solution)/shard_map/reduce_scatter | solution.py:90
  397.6 120.3 %copy-start.7 = (bf16[512,2048]{1,0:T(8,128)(2,1)S(1)}, bf16[512,2048]{1,0:T(8,128)(2,1)}, u32[]{:S(2)}) copy-start(bf16[512,2048]{1,0:T(8,128)(2,1)} %all-gather.15.cloned.1.call-done) | copy-start | bytes 6291460
  506.5 11.4 copy-start.46
  526.1 29.2 %copy-start.8 = (bf16[128,2048]{1,0:T(8,128)(2,1)S(1)}, bf16[128,2048]{1,0:T(8,128)(2,1)}, u32[]{:S(2)}) copy-start(bf16[128,2048]{1,0:T(8,128)(2,1)} %param.23) | copy-start | bytes 1572868
  528.5 28.8 %copy-start.50 = (bf16[512,1408]{1,0:T(8,128)(2,1)S(1)}, bf16[512,1408]{1,0:T(8,128)(2,1)}, u32[]{:S(2)}) copy-start(bf16[512,1408]{1,0:T(8,128)(2,1)} %get-tuple-element.31) | copy-start | bytes 4325380
  528.6 59.1 %all-gather.23.cloned.1.call-start = ((), (), s32[]{:S(2)}) async-start(), calls=%async_computation.18 | async-start | bytes 2621440 | tf_op jit(solution)/shard_map/all_gather | solution.py:51
  557.3 165.4 %reduce-scatter.11.cloned.1.call-start = ((), (), s32[]{:S(2)}) async-start(), calls=%async_computation.15 | async-start | bytes 2621440 | tf_op jit(solution)/shard_map/reduce_scatter | solution.py:101
  564.7 27.4 %copy-start.48 = (bf16[512,2048]{1,0:T(8,128)(2,1)S(1)}, bf16[512,2048]{1,0:T(8,128)(2,1)}, u32[]{:S(2)}) copy-start(bf16[512,2048]{1,0:T(8,128)(2,1)} %all-gather.21.cloned.1.call-done) | copy-start | bytes 6291460
  564.7 264.1 %reduce-scatter.19.cloned.1.call-start = ((), (), s32[]{:S(2)}) async-start(), calls=%async_computation.21 | async-start | bytes 2162688 | tf_op jit(solution)/shard_map/reduce_scatter | solution.py:115
  592.1 388.1 %reduce-scatter.23.cloned.1.call-start = ((), (), s32[]{:S(2)}) async-start(), calls=%async_computation.23 | async-start | bytes 5947392 | tf_op jit(solution)/shard_map/reduce_scatter | solution.py:115
  599.1 429.3 %reduce-scatter.15.cloned.1.call-start = ((), (), s32[]{:S(2)}) async-start(), calls=%async_computation.19 | async-start | bytes 2621440 | tf_op jit(solution)/shard_map/reduce_scatter | solution.py:90
  605.4 5.8 copy-start
  605.4 5.8 copy-start.12
  605.4 5.8 copy-start.14
  605.5 5.8 copy-start.16
  662.1 7.5 copy-start.5
  667.8 18.0 %collective-permute-start.3 = (bf16[512,128]{0,1:T(8,128)(2,1)S(1)}, bf16[512,128]{0,1:T(8,128)(2,1)S(1)}, u32[]{:S(2)}, u32[]{:S(2)}) collective-permute-start(bf16[512,128]{0,1:T(8,128)(2,1)S(1)} %pad_maximum_fusion.10), channel_id=1, source_target_pairs={{4,0},{8,4},{12,8},{16,12},{20,16},{24,20},{28,24},{32,28},{36,32}... | collective-permute-start | bytes 393224 | tf_op jit(solution)/shard_map/ppermute | solution.py:22
  684.4 12.0 copy-start.20
  684.4 12.0 copy-start.27
  685.9 15.4 %copy-start.37 = (f32[512,64]{0,1:T(8,128)S(1)}, f32[512,64]{0,1:T(8,128)}, u32[]{:S(2)}) copy-start(f32[512,64]{0,1:T(8,128)} %convolution_bitcast_fusion) | copy-start | bytes 393220
  685.9 15.5 %copy-start.39 = (f32[512]{0:T(512)S(1)}, f32[512]{0:T(512)}, u32[]{:S(2)}) copy-start(f32[512]{0:T(512)} %copy-done.38) | copy-start | bytes 6148
  685.9 15.5 %copy-start.45 = (f32[32]{0:T(128)S(1)}, f32[32]{0:T(128)}, u32[]{:S(2)}) copy-start(f32[32]{0:T(128)} %copy-done.44) | copy-start | bytes 388
  685.9 15.8 %copy-start.6 = (bf16[512,2048]{1,0:T(8,128)(2,1)S(1)}, bf16[512,2048]{1,0:T(8,128)(2,1)}, u32[]{:S(2)}) copy-start(bf16[512,2048]{1,0:T(8,128)(2,1)} %all-gather.9.cloned.1.call-done) | copy-start | bytes 6291460
  685.9 15.8 %copy-start.41 = (f32[2048]{0:T(1024)S(1)}, f32[2048]{0:T(1024)}, u32[]{:S(2)}) copy-start(f32[2048]{0:T(1024)} %copy-done.40) | copy-start | bytes 24580
  685.9 15.8 %copy-start.43 = (f32[512]{0:T(512)S(1)}, f32[512]{0:T(512)}, u32[]{:S(2)}) copy-start(f32[512]{0:T(512)} %copy-done.42) | copy-start | bytes 6148
  685.9 15.8 %copy-start.47 = (bf16[2048,640]{1,0:T(8,128)(2,1)S(1)}, bf16[2048,640]{1,0:T(8,128)(2,1)}, u32[]{:S(2)}) copy-start(bf16[2048,640]{1,0:T(8,128)(2,1)} %all-gather.11.cloned.1.call-done) | copy-start | bytes 7864324
  685.9 8.9 collective-permute-start.4
  694.8 6.4 collective-permute-start.5
  696.7 7.8 copy-start.21
  707.0 488.5 %reduce-scatter.17.cloned.1.call-start = ((), (), s32[]{:S(2)}) async-start(), calls=%async_computation.20 | async-start | bytes 2703360 | tf_op jit(solution)/shard_map/reduce_scatter | solution.py:81
  710.6 694.2 %reduce-scatter.21.cloned.1.call-start = ((), (), s32[]{:S(2)}) async-start(), calls=%async_computation.22 | async-start | bytes 11894784 | tf_op jit(solution)/shard_map/reduce_scatter | solution.py:81
  721.9 306.6 %copy-start.17 = (bf16[128,2048]{1,0:T(8,128)(2,1)S(1)}, bf16[128,2048]{1,0:T(8,128)(2,1)}, u32[]{:S(2)}) copy-start(bf16[128,2048]{1,0:T(8,128)(2,1)} %reduce-scatter.13.cloned.1.call-done) | copy-start | bytes 1572868
  (19 other events, 56.1 us)
Sparse Core Ops, SparseCore 0:
  9.7 32.7 all-gather.8
  46.1 71.7 all-gather.10
  120.9 67.8 all-gather.12
  193.2 32.1 reduce-scatter.8
  227.6 30.2 all-gather.14
  261.8 122.6 all-gather.16
  386.3 27.6 all-gather.20
  417.4 89.0 all-gather.18
  528.7 26.5 reduce-scatter.12
  557.4 30.2 all-gather.22
  590.1 28.9 reduce-scatter.10
  621.4 164.5 reduce-scatter.18
  788.4 191.7 reduce-scatter.22
  982.4 45.9 reduce-scatter.14
  1030.8 164.7 reduce-scatter.16
  1198.0 206.7 reduce-scatter.20
where the time goes:
time: 1440 us; the launch traced here: 1410 us
  waiting for transfers between devices  946 us (66%)
  blocking collectives  189 us (13%)
  matrix products  160 us (11%)
  other arithmetic  68.7 us (5%)
  local copies, waits for them, and re-layouts  17.5 us (1%)
  between operations  17 us (1%)
  starting transfers between devices  15 us (1%)
    reduce_scatter x2, waiting for transfers between devices, back_in(): lax.psum_scatter(grad_matrix.astype(jnp.bfloat16), 'wide', scatter_dimens...  371 us
    unnamed x2, blocking collectives  170 us
    reduce_scatter x2, waiting for transfers between devices, back_out(): lax.psum_scatter(grad_matrix.astype(jnp.bfloat16), 'wide', scatter_dimens...  150 us
    all_gather x2, waiting for transfers between devices, project_in(): piece_matrix = lax.all_gather(matrix, 'wide', axis=0, tiled=True)  136 us
    all_gather x2, waiting for transfers between devices, project_out(): whole = lax.all_gather(matrix, 'wide', axis=1, tiled=True)  102 us
    reduce_scatter x2, waiting for transfers between devices, back_in(): lax.psum_scatter(partial_rows.astype(jnp.bfloat16), 'tp', scatter_dimensi...  73.3 us
    all_gather x4, waiting for transfers between devices, gather_rows(): return lax.all_gather(rows, 'tp', axis=0, tiled=True)  67.3 us
    reduce_scatter x2, waiting for transfers between devices, project_out(): lax.psum_scatter(jnp.dot(mixed, whole, preferred_element_type=jnp.float32...  32.3 us
  transfers between devices with their start and end apart: 22, of which 15 were waited for; matrix products, arithmetic and copies ran while one was open for 15% of the time, Pallas kernels for 0%

commit v1 on v0

v1 whole, which is shorter than its diff:
```python
import functools

import jax
import jax.numpy as jnp
from jax import lax
from jax.experimental import pallas as pl
from jax.experimental.pallas import tpu as pltpu
from jax.sharding import Mesh, PartitionSpec as P

HEADS = 32
KV = 4
HD = 64
SEQ_DEVS = 4
WIDE = ("yh", "z", "x")
TP = ("yl", "core")
BF = jnp.bfloat16
F32 = jnp.float32

epsilon = 1e-05
masked_fill = -1e30
VMEM_LIMIT = 56 * 1024 * 1024


def after(value, *earlier):
    return lax.optimization_barrier((value, earlier))[0]


def shift(block, axis, distance):
    n = lax.axis_size(axis)
    return lax.ppermute(block, axis, [(i, (i + distance) % n) for i in range(n)])


def swap(block, axis):
    return shift(block, axis, 1)


def place(axis, step=0):
    n = lax.axis_size(axis)
    return ((lax.axis_index(axis) + (step + n)) & (n - 1)).astype(jnp.uint32)


def pick(array, index, dim):
    return lax.dynamic_index_in_dim(array, index, dim, keepdims=False)


def gather_stage(block, axis, dim, hold=()):
    n = lax.axis_size(axis)
    order = (0, 1, n - 1, *range(2, n - 1))
    arrived = [block] + [after(shift(block, axis, d), *hold) for d in order[1:]]
    out = jnp.zeros(block.shape[:dim] + (n,) + block.shape[dim:], block.dtype)
    for d, piece in zip(order, arrived):
        out = lax.dynamic_update_index_in_dim(out, piece, place(axis, -d), dim)
    return out


def join_sides(shard, other):
    first = lax.axis_index("yh") == 0
    return jnp.concatenate([jnp.where(first, shard, other), jnp.where(first, other, shard)], 0)


def flat(blocks):
    return blocks.reshape(-1, blocks.shape[-1])


def to_inner(rows):
    t, d = rows.shape
    return rows.reshape(t, 2, 16, d // 32).transpose(0, 2, 1, 3).reshape(t, d)


def from_inner(rows):
    t, d = rows.shape
    return rows.reshape(t, 16, 2, d // 32).transpose(0, 2, 1, 3).reshape(t, d)


def gather_rows(rows):
    across = swap(rows, "yl")
    return [rows, swap(rows, "core"), across, swap(across, "core")]


def scatter_rows(partial):
    n = partial.shape[0] // 4
    low = partial.astype(BF)
    far = swap(low[3 * n :], "core").astype(F32)
    near = swap(low[n : 2 * n], "core").astype(F32)
    other = partial[2 * n : 3 * n].astype(F32) + far
    mine = partial[:n].astype(F32) + near
    return mine + swap(other.astype(BF), "yl").astype(F32)


def contract_last(left, right):
    return lax.dot_general(left, right, (((1,), (1,)), ((), ())), preferred_element_type=F32)


def contract_first(left, right):
    return lax.dot_general(left, right, (((0,), (0,)), ((), ())), preferred_element_type=F32)


def columns_of(rows, axis, index):
    t, d = rows.shape
    blocks = rows.reshape(t, 4, 4, d // 16)
    return pick(blocks, index, {"z": 1, "x": 2}[axis]).reshape(t, d // 4)


def exchange_sum(parts, axis, hold=()):
    n = len(parts)
    total = parts[0].astype(F32)
    for d in (1, n - 1, *range(2, n - 1))[: n - 1]:
        total = total + after(shift(parts[d].astype(BF), axis, d), *hold).astype(F32)
    return total


def sides_sum(part, hold=()):
    half = part.reshape(2, part.shape[0] // 2, part.shape[1])
    return exchange_sum([pick(half, place("yh"), 0), pick(half, place("yh", 1), 0)], "yh", hold)


def wide_parts(left, right, axis):
    return [
        contract_first(columns_of(left, axis, place(axis, d)), right).astype(BF)
        for d in range(lax.axis_size(axis))
    ]


def wide_sum_next(part, axis, hold=()):
    n = lax.axis_size(axis)
    part = part.reshape(n, part.shape[0] // n, part.shape[1])
    pieces = [pick(part, place(axis, d), 0) for d in range(n)]
    return exchange_sum(pieces, axis, hold).astype(BF)


def mm(left, right):
    return jnp.dot(left, right, preferred_element_type=F32)


def mm_last(left, right):
    return lax.dot_general(left, right, (((1,), (1,)), ((), ())), preferred_element_type=F32)


def normed_rows(piece):
    values = piece.astype(F32)
    factor = lax.rsqrt(jnp.mean(values * values, -1, keepdims=True) + epsilon)
    return values * factor, factor


def scale_rows(piece_refs, gain, scaled_ref):
    for n, ref in enumerate(piece_refs):
        for at in range(0, ref.shape[0], 32):
            normed, _ = normed_rows(ref[at : at + 32, :])
            rows = n * ref.shape[0] + at
            scaled_ref[rows : rows + 32, :] = (normed * gain).astype(BF)


def project_kernel(*refs):
    piece_refs, (w_ref, last_ref, cos_ref, sin_ref, q_ref, kv_ref, scaled_ref, gains_ref) = refs[:4], refs[4:]
    width_q = q_ref.shape[0]
    half = HD // 2
    cos, sin = cos_ref[...], sin_ref[...]
    tiles = [(w, at) for w in (w_ref, last_ref) for at in range(0, w.shape[1], 128)]

    def turned(block):
        a, b = block[:half], block[half:]
        return jnp.concatenate([a * cos - b * sin, b * cos + a * sin], 0)

    w, at = tiles[-1]
    gains_ref[...] = w[:, at : at + 128].T[:8].astype(F32)
    scale_rows(piece_refs, gains_ref[0:1, :], scaled_ref)
    x = scaled_ref[...]
    for n in range(width_q // 128):
        w, at = tiles[n]
        piece = mm(x, w[:, at : at + 128]).T
        for sub in range(0, 128, HD):
            low = turned(piece[sub : sub + HD]).astype(BF)
            q_ref[n * 128 + sub : n * 128 + sub + HD, :] = low * 0.125
    w, at = tiles[width_q // 128]
    piece = mm(x, w[:, at : at + 128]).T
    kv = jnp.concatenate([turned(piece[:HD]), piece[HD:]], 0)
    kv_ref[...] = kv.T.astype(BF)


def hidden_kernel(*refs):
    pieces, cots, (gain_ref, gate_ref, up_ref, down_ref, hidden_ref, dgate_ref, dup_ref, scaled_ref, cot_ref) = (
        refs[:4], refs[4:8], refs[8:],
    )

    @pl.when(pl.program_id(0) == 0)
    def _():
        scale_rows(pieces, gain_ref[1:2, :], scaled_ref)
        for n, ref in enumerate(cots):
            cot_ref[n * ref.shape[0] : (n + 1) * ref.shape[0], :] = ref[...]

    tile = gate_ref.shape[1]
    both = mm(scaled_ref[...], jnp.concatenate([gate_ref[...], up_ref[...]], 1))
    grad = mm(cot_ref[...], down_ref[...])
    gate, up = both[:, :tile], both[:, tile:]
    sigmoid = 1.0 / (1.0 + jnp.exp(-gate))
    gated = gate * sigmoid
    hidden_ref[...] = (gated * up).astype(BF)
    dgate_ref[...] = (grad * up * sigmoid * (1.0 + gate * (1.0 - sigmoid))).astype(BF)
    dup_ref[...] = (grad * gated).astype(BF)


def rows_grad_kernel(count, gain_row, *refs):
    grads, weights, pieces = refs[:count], refs[count : 2 * count], refs[2 * count : 2 * count + 4]
    gain_ref, out_ref, sum_ref = refs[2 * count + 4 :]
    step = pl.program_id(0)
    tile = weights[0].shape[0]
    total = None
    for g_ref, w_ref in zip(grads, weights):
        part = mm_last(g_ref[...], w_ref[...])
        total = part if total is None else total + part
    columns = pl.ds(pl.multiple_of(step * tile, tile), tile)
    sum_ref[:, columns] = total * gain_ref[gain_row : gain_row + 1, columns]

    @pl.when(step == pl.num_programs(0) - 1)
    def _():
        for n, ref in enumerate(pieces):
            for at in range(0, ref.shape[0], 32):
                normed, factor = normed_rows(ref[at : at + 32, :])
                rows = slice(n * ref.shape[0] + at, n * ref.shape[0] + at + 32)
                scaled = sum_ref[rows, :]
                inner = jnp.mean(scaled * normed, -1, keepdims=True)
                out_ref[rows, :] = (factor * (scaled - normed * inner)).astype(BF)


def fill_bias(bias_ref, me_ref, pos_ref, span, distances):
    step = 64
    quarter = span // 4
    me = me_ref[0, 0]
    at = lax.broadcasted_iota(jnp.int32, (1, span), 1)
    query = (((at // quarter) ^ me) * quarter) + (at & (quarter - 1))
    first = query - pos_ref[...]

    @pl.loop(0, span // step)
    def _(i):
        block = (i * step) // quarter
        start = (block ^ me) * quarter + i * step - block * quarter
        key = start + lax.broadcasted_iota(jnp.int32, (step, span), 0)
        for n, d in enumerate(distances):
            seen = (key - d * span <= query) & (key - d * span >= first)
            bias_ref[pl.ds(pl.multiple_of(n * span + i * step, step), step), :] = jnp.where(
                seen, 0.0, masked_fill
            ).astype(F32)


def attend_kernel(q_ref, *refs):
    blocks = len(refs) - 7
    kv_refs = refs[:blocks]
    me_ref, pos_ref, mix_ref, lse_ref, bias_ref, s_ref, vt_ref = refs[blocks:]
    span = q_ref.shape[1]
    fill_bias(bias_ref, me_ref, pos_ref, span, range(blocks))
    for d in range(blocks):
        vt_ref[:, d * span : (d + 1) * span] = kv_refs[d][...].T[HD:]

    @pl.loop(0, q_ref.shape[0] // 128)
    def _(pair):
        outs = []
        for sub in range(2):
            q = q_ref[pl.ds(pl.multiple_of(pair * 128 + sub * HD, HD), HD), :]
            top = None
            for d in range(blocks):
                rows = slice(d * span, (d + 1) * span)
                s = mm(kv_refs[d][:, :HD], q) + bias_ref[rows, :]
                s_ref[rows, :] = s
                high = jnp.max(s, 0, keepdims=True)
                top = high if top is None else jnp.maximum(top, high)
            total = jnp.zeros_like(top)
            out = jnp.zeros((HD, span), F32)
            for d in range(blocks):
                rows = slice(d * span, (d + 1) * span)
                p = jnp.exp(s_ref[rows, :] - top)
                total = total + jnp.sum(p, 0, keepdims=True)
                out = out + mm(vt_ref[:, rows], p.astype(BF))
            outs.append(out / total)
            lse_ref[pl.ds(pair * 2 + sub, 1), :] = top + jnp.log(total)
        mix_ref[:, pl.ds(pl.multiple_of(pair * 128, 128), 128)] = (
            jnp.concatenate(outs, 0).T.astype(BF)
        )


def attend_back_kernel(distances, first, last, q_ref, *refs):
    blocks = len(distances)
    refs = list(refs)

    def take(count):
        got, refs[:count] = refs[:count], []
        return got

    kv_refs = take(blocks)
    me_ref, pos_ref, lse_ref = take(3)
    if first:
        mix_ref, grad_ref = take(2)
    else:
        gt_ref, delta_ref, part_ref = take(3)
    if last:
        cos_ref, sin_ref = take(2)
        (dq_ref,) = take(1)
    else:
        (sum_ref,) = take(1)
    (dkv_ref,) = take(1)
    if first:
        gt_ref, delta_ref = take(2)
    bias_ref, v_ref, kt_ref, dk_ref, dv_ref = take(5)
    span = q_ref.shape[1]
    half = HD // 2
    heads = q_ref.shape[0] // HD
    fill_bias(bias_ref, me_ref, pos_ref, span, distances)
    for n in range(blocks):
        rows = slice(n * span, (n + 1) * span)
        both = kv_refs[n][...].T
        kt_ref[:, rows] = both[:HD]
        v_ref[rows, :] = both[HD:].T
    dk_ref[...] = jnp.zeros_like(dk_ref)
    dv_ref[...] = jnp.zeros_like(dv_ref)
    if first:
        for at in range(0, heads * HD, 128):
            gt = grad_ref[:, at : at + 128].T
            mt = mix_ref[:, at : at + 128].T
            gt_ref[at : at + 128, :] = gt
            prod = gt.astype(F32) * mt.astype(F32)
            for sub in range(2):
                h = at // HD + sub
                delta_ref[h : h + 1, :] = jnp.sum(prod[sub * HD : (sub + 1) * HD], 0, keepdims=True)

    @pl.loop(0, heads // 2)
    def _(pair):
        outs = []
        for sub in range(2):
            rows_h = pl.ds(pl.multiple_of(pair * 128 + sub * HD, HD), HD)
            q, g = q_ref[rows_h, :], gt_ref[rows_h, :]
            lse = lse_ref[pl.ds(pair * 2 + sub, 1), :]
            delta = delta_ref[pl.ds(pair * 2 + sub, 1), :]
            dq = jnp.zeros((HD, span), F32) if first else part_ref[rows_h, :]
            for n in range(blocks):
                rows = slice(n * span, (n + 1) * span)
                s = mm(kv_refs[n][:, :HD], q) + bias_ref[rows, :]
                p = jnp.exp(s - lse)
                ds = (p * (mm(v_ref[rows, :], g) - delta)).astype(BF)
                dv_ref[rows, :] += mm_last(p.astype(BF), g)
                dk_ref[rows, :] += mm_last(ds, q)
                dq = dq + mm(kt_ref[:, rows], ds)
            if last:
                dq = dq * 0.125
                a, b = dq[:half], dq[half:]
                cos, sin = cos_ref[...], sin_ref[...]
                outs += [a * cos + b * sin, b * cos - a * sin]
            else:
                sum_ref[rows_h, :] = dq
        if last:
            dq_ref[:, pl.ds(pl.multiple_of(pair * 128, 128), 128)] = (
                jnp.concatenate(outs, 0).T.astype(BF)
            )

    for n in range(blocks):
        rows = slice(n * span, (n + 1) * span)
        dkv_ref[rows, :] = jnp.concatenate([dk_ref[rows, :], dv_ref[rows, :]], 1).astype(dkv_ref.dtype)


def weight_grads_kernel(left_ref, *refs):
    out_ref = refs[-1]
    turned = left_ref[...].T
    at = 0
    for ref in refs[:-1]:
        for c in range(0, ref.shape[1], 256):
            size = min(256, ref.shape[1] - c)
            out_ref[:, at + c : at + c + size] = mm(turned, ref[:, c : c + size]).astype(BF)
        at += ref.shape[1]


def params():
    return pltpu.CompilerParams(vmem_limit_bytes=VMEM_LIMIT)


def whole(count):
    return [pl.BlockSpec(memory_space=pltpu.VMEM)] * count


def cost(products, moved):
    return pl.CostEstimate(flops=2 * products, bytes_accessed=moved, transcendentals=0)


def project(pieces, w, last, cos, sin, width_q):
    span, d = 4 * pieces[0].shape[0], pieces[0].shape[1]
    return pl.pallas_call(
        project_kernel,
        out_shape=(
            jax.ShapeDtypeStruct((width_q, span), BF),
            jax.ShapeDtypeStruct((span, 2 * HD), BF),
            jax.ShapeDtypeStruct((span, d), BF),
            jax.ShapeDtypeStruct((8, d), F32),
        ),
        in_specs=whole(8),
        out_specs=tuple(whole(4)),
        compiler_params=params(),
        cost_estimate=cost(span * d * (width_q + 2 * HD), 8 << 20),
        name="project",
    )(*pieces, w, last, cos, sin)


def hidden_units(pieces, cots, gains, weights, width):
    span, d = 4 * pieces[0].shape[0], pieces[0].shape[1]
    tile = 128
    tiles = width // tile

    def fixed(array):
        return pl.BlockSpec(array.shape, lambda i: (0, 0))

    def columns(base):
        return pl.BlockSpec((d, tile), lambda i: (0, i + base))

    out = pl.BlockSpec((span, tile), lambda i: (0, i))
    return pl.pallas_call(
        hidden_kernel,
        grid=(tiles,),
        out_shape=(jax.ShapeDtypeStruct((span, width), BF),) * 3
        + (jax.ShapeDtypeStruct((span, d), BF),) * 2,
        in_specs=[fixed(a) for a in (*pieces, *cots, gains)]
        + [columns(0), columns(tiles), columns(2 * tiles)],
        out_specs=(out,) * 3 + (pl.BlockSpec((span, d), lambda i: (0, 0)),) * 2,
        compiler_params=params(),
        cost_estimate=cost(3 * span * d * width, 6 * d * width),
        name="hidden_units",
    )(*pieces, *cots, gains, weights, weights, weights)


def rows_grad(grads, weights, pieces, gains, gain_row):
    span, d = 4 * pieces[0].shape[0], pieces[0].shape[1]
    tile = 256

    def fixed(array):
        return pl.BlockSpec(array.shape, lambda i: (0, 0))

    def rows(grad, index):
        return pl.BlockSpec((tile, grad.shape[1]), lambda i: (i, index))

    return pl.pallas_call(
        functools.partial(rows_grad_kernel, len(grads), gain_row),
        grid=(d // tile,),
        out_shape=jax.ShapeDtypeStruct((span, d), BF),
        in_specs=[fixed(g) for g in grads]
        + [rows(g, w[1]) for g, w in zip(grads, weights)]
        + [fixed(a) for a in (*pieces, gains)],
        out_specs=pl.BlockSpec((span, d), lambda i: (0, 0)),
        scratch_shapes=[pltpu.VMEM((span, d), F32)],
        compiler_params=params(),
        cost_estimate=cost(sum(span * d * g.shape[1] for g in grads), 8 << 20),
        name="rows_grad",
    )(*grads, *[w[0] for w in weights], *pieces, gains)


def window_specs():
    return [pl.BlockSpec(memory_space=pltpu.SMEM)] + whole(1)


def attend(q, kvs, window):
    n = len(kvs)
    width, span = q.shape
    heads = width // HD
    return pl.pallas_call(
        attend_kernel,
        out_shape=(
            jax.ShapeDtypeStruct((span, width), BF),
            jax.ShapeDtypeStruct((heads, span), F32),
        ),
        in_specs=whole(n + 1) + window_specs(),
        out_specs=tuple(whole(2)),
        scratch_shapes=[
            pltpu.VMEM((n * span, span), F32),
            pltpu.VMEM((n * span, span), F32),
            pltpu.VMEM((HD, n * span), BF),
        ],
        compiler_params=params(),
        cost_estimate=pl.CostEstimate(flops=16 * span * width * n * span, bytes_accessed=2 << 20, transcendentals=heads * n * span * span),
        name="attend",
    )(q, *kvs, *window)


def attend_back(distances, q, kvs, window, lse, prepared, mixed=None, grad=None, turn=None):
    n = len(kvs)
    width, span = q.shape
    heads = width // HD
    first, last = prepared is None, turn is not None
    operands = [q, *kvs, *window, lse]
    operands += [mixed, grad] if first else list(prepared)
    shapes = []
    if last:
        operands += turn
        shapes.append(jax.ShapeDtypeStruct((span, width), BF))
    else:
        shapes.append(jax.ShapeDtypeStruct((width, span), F32))
    shapes.append(jax.ShapeDtypeStruct((n * span, 2 * HD), F32 if last else BF))
    if first:
        shapes.append(jax.ShapeDtypeStruct((width, span), BF))
        shapes.append(jax.ShapeDtypeStruct((heads, span), F32))
    return pl.pallas_call(
        functools.partial(attend_back_kernel, distances, first, last),
        out_shape=tuple(shapes),
        in_specs=whole(n + 1) + window_specs() + whole(len(operands) - n - 3),
        out_specs=tuple(whole(len(shapes))),
        scratch_shapes=[
            pltpu.VMEM((n * span, span), F32),
            pltpu.VMEM((n * span, HD), BF),
            pltpu.VMEM((HD, n * span), BF),
            pltpu.VMEM((n * span, HD), F32),
            pltpu.VMEM((n * span, HD), F32),
        ],
        compiler_params=params(),
        cost_estimate=pl.CostEstimate(flops=40 * span * width * n * span, bytes_accessed=4 << 20, transcendentals=heads * n * span * span),
        name="attend_back",
    )(*operands)


def weight_grads(left, *rights):
    t, d = left.shape
    tile = 256
    width = sum(right.shape[1] for right in rights)
    return pl.pallas_call(
        weight_grads_kernel,
        grid=(d // tile,),
        out_shape=jax.ShapeDtypeStruct((d, width), BF),
        in_specs=[pl.BlockSpec((t, tile), lambda i: (0, i))]
        + [pl.BlockSpec(right.shape, lambda i: (0, 0)) for right in rights],
        out_specs=pl.BlockSpec((tile, width), lambda i: (i, 0)),
        compiler_params=params(),
        cost_estimate=cost(t * d * width, 2 * d * width + 4 * t * d),
        name="weight_grads",
    )(left, *rights)


def per_device(
    inputs,
    positions,
    attn_gain,
    query_weight,
    key_weight,
    value_weight,
    out_weight,
    mlp_gain,
    gate_weight,
    up_weight,
    down_weight,
    cotangent,
):
    width_q = query_weight.shape[1]
    width_k = key_weight.shape[1]
    hidden_width = gate_weight.shape[1]
    span = positions.shape[0]
    quarter = span // 4
    cut = 3 * width_q // 4

    inputs = to_inner(inputs)
    cotangent = to_inner(cotangent)

    pad = jnp.zeros((attn_gain.shape[0], 126), BF)
    shard_a = query_weight[:, :cut]
    shard_b = jnp.concatenate(
        [query_weight[:, cut:], key_weight, value_weight, attn_gain[:, None], mlp_gain[:, None], pad], 1
    )
    width_b = width_q - cut + 2 * width_k
    shard_mlp = jnp.concatenate([gate_weight, up_weight, down_weight.T], 1)
    other_a, other_b = swap(shard_a, "yh"), swap(shard_b, "yh")
    other_mlp = swap(shard_mlp, "yh")
    rows_in = gather_rows(inputs)

    part_b = gather_stage(join_sides(shard_b, other_b), "x", 0)
    part_a = gather_stage(join_sides(shard_a, other_a), "z", 0)
    out_turned = after(out_weight.T, part_a, part_b)
    other_out = swap(out_turned, "yh")
    mlp_pair = join_sides(shard_mlp, after(other_mlp, other_out))
    mlp_whole = lax.all_gather(mlp_pair, ("z", "x"), axis=0, tiled=True)
    whole_b = flat(gather_stage(part_b, "z", 0))
    whole_a = flat(gather_stage(part_a, "x", 1))
    pair_out = join_sides(out_turned, other_out)

    me = (lax.axis_index("yl") * 2 + lax.axis_index("core")).astype(jnp.int32)
    blocked = jnp.arange(4, dtype=jnp.int32) ^ me
    positions = jnp.take(positions.reshape(4, quarter), blocked, axis=0, mode="clip").reshape(1, span)
    freqs = 10000.0 ** (-(jnp.arange(HD // 2, dtype=F32) * 2.0) / HD)
    angles = freqs[:, None] * positions.astype(F32)
    cos, sin = jnp.cos(angles), jnp.sin(angles)
    window = (me.reshape(1, 1), positions)

    queries, kv_block, scaled_in, gains = project(rows_in, whole_a, whole_b, cos, sin, width_q)
    blocks = [kv_block] + [shift(kv_block, "x", d) for d in range(1, SEQ_DEVS)]
    part_out = gather_stage(pair_out, "x", 0, hold=[kv_block])
    cotangents = gather_rows(after(cotangent, kv_block))
    mixed, log_total = attend(queries, blocks, window)
    out_whole = flat(gather_stage(part_out, "z", 0, hold=[log_total]))

    middle = inputs.astype(F32) + scatter_rows(contract_last(mixed, out_whole))
    rows_mid = gather_rows(middle.astype(BF))
    hidden, grad_gate, grad_up, scaled_mid, cotangent_all = hidden_units(
        rows_mid, cotangents, gains, mlp_whole, hidden_width
    )
    mid_partial = rows_grad(
        [grad_gate, grad_up], [(mlp_whole, 0), (mlp_whole, 1)], rows_mid, gains, 1
    )
    mid_part = scatter_rows(mid_partial)
    grad_middle = cotangent.astype(F32) + mid_part
    grad_middle_all = jnp.concatenate(gather_rows(grad_middle.astype(BF)), 0)

    gate_up_sum = weight_grads(after(scaled_mid, mid_partial), grad_gate, grad_up)
    gate_up_sum = lax.psum_scatter(gate_up_sum, ("z", "x"), scatter_dimension=0, tiled=True)
    down_parts = wide_parts(after(cotangent_all, mid_partial), hidden, "z")
    mlp_partial = contract_last(after(hidden, down_parts), mlp_whole[:, 2 * hidden_width :])

    grad_mixed = jnp.dot(grad_middle_all, out_whole, preferred_element_type=F32).astype(BF)
    out_parts = wide_parts(grad_middle_all, mixed, "x")
    down_sum = exchange_sum(down_parts, "z", hold=[grad_middle_all]).astype(BF)
    query_part, far_grads, grad_turned, delta = attend_back(
        (1, 2, 3), queries, blocks[1:], window, log_total, None, mixed, after(grad_mixed, out_parts)
    )
    mlp_rows = scatter_rows(after(mlp_partial, grad_middle_all))
    output = (middle + mlp_rows).astype(BF)
    arriving = [
        shift(far_grads[(d - 1) * span : d * span], "x", -d) for d in range(1, SEQ_DEVS)
    ]
    out_sum = exchange_sum(out_parts, "x", hold=[query_part]).astype(BF)
    down_sum = wide_sum_next(down_sum, "x", hold=[query_part])
    query_raw_grad, carried = attend_back(
        (0,), queries, blocks[:1], window, log_total, (grad_turned, delta, query_part), turn=[cos, sin]
    )
    out_sum = wide_sum_next(out_sum, "z", hold=[query_raw_grad])
    outer = jnp.concatenate([down_sum, out_sum], 1)
    for piece in arriving:
        carried = carried + piece.astype(F32)

    a_sum = exchange_sum(wide_parts(scaled_in, query_raw_grad[:, :cut], "x"), "x").astype(BF)
    turned = carried[:, :width_k]
    first, second = turned[:, : HD // 2], turned[:, HD // 2 :]
    key_raw_grad = jnp.concatenate(
        [first * cos.T + second * sin.T, second * cos.T - first * sin.T], 1
    ).astype(BF)
    grad_b = jnp.concatenate(
        [query_raw_grad[:, cut:], key_raw_grad, carried[:, width_k:].astype(BF)], 1
    )
    in_part = scatter_rows(
        rows_grad([query_raw_grad[:, :cut], grad_b], [(whole_a, 0), (whole_b, 0)], rows_in, gains, 0)
    )
    input_grad = grad_middle + in_part
    b_sum = exchange_sum(wide_parts(scaled_in, grad_b, "z"), "z").astype(BF)
    a_sum, b_sum = wide_sum_next(a_sum, "z"), wide_sum_next(b_sum, "x")
    attn_sum = sides_sum(jnp.concatenate([a_sum, b_sum], 1))
    a_grad, b_grad = attn_sum[:, :cut], attn_sum[:, cut:]
    outer_grad = sides_sum(outer, hold=[b_sum]).T
    down_grad, out_grad = outer_grad[:hidden_width], outer_grad[hidden_width:]
    mlp_grad = sides_sum(after(gate_up_sum, query_raw_grad))
    gate_grad, up_grad = mlp_grad[:, :hidden_width], mlp_grad[:, hidden_width:]

    attn_gain_part = jnp.sum(shard_a.astype(F32) * a_grad, 1) + jnp.sum(
        shard_b[:, :width_b].astype(F32) * b_grad, 1
    )
    mlp_gain_part = jnp.sum(
        gate_weight.astype(F32) * gate_grad + up_weight.astype(F32) * up_grad, 1
    )
    attn_gain_grad, mlp_gain_grad = lax.psum((attn_gain_part, mlp_gain_part), TP)
    own = width_q - cut
    return (
        from_inner(output),
        from_inner(input_grad),
        attn_gain_grad / attn_gain.astype(F32),
        jnp.concatenate([a_grad, b_grad[:, :own]], 1),
        b_grad[:, own : own + width_k],
        b_grad[:, own + width_k :],
        out_grad,
        mlp_gain_grad / mlp_gain.astype(F32),
        gate_grad,
        up_grad,
        down_grad,
    )


def solution(mesh):
    split = Mesh(mesh.devices.reshape(2, 4, 4, 2, 2), WIDE + TP)
    rows = P(WIDE + TP, None)
    inward = P(WIDE, TP)
    outward = P(TP, WIDE)
    gain = P(WIDE)
    return jax.shard_map(
        per_device,
        mesh=split,
        in_specs=(
            rows, gain, gain, inward, inward, inward, outward, gain, inward, inward, outward, rows,
        ),
        out_specs=(
            rows, rows, gain, inward, inward, inward, outward, gain, inward, inward, outward,
        ),
        check_vma=False,
    )
```

time: 1440 us -> 552 us (0.38); the launches traced: 1410 us -> 543 us
  waiting for transfers between devices: 946 us -> 129 us
  blocking collectives: 189 us -> 7.11 us
  matrix products: 160 us -> 31.9 us
  Pallas kernels: 0 us -> 113 us
  starting transfers between devices: 15 us -> 126 us
  local copies, waits for them, and re-layouts: 17.5 us -> 90.7 us
  other arithmetic: 68.7 us -> 28.2 us
    reduce_scatter x8 -> x1, waiting for transfers between devices: 627 us -> 0.01 us  [per_device(): lax.psum_scatter(gate_up_sum, ('z', 'x'), scatter_dimension=0, tiled=True)]
    all_gather x8 -> x1, waiting for transfers between devices: 306 us -> 0.01 us  [per_device(): mlp_whole = lax.all_gather(mlp_pair, ('z', 'x'), axis=0, tiled=True)]
    unnamed x2 -> x0, blocking collectives: 170 us -> none
    ppermute x6 -> x79, waiting for transfers between devices: 10.5 us -> 129 us  [shift(): lax.ppermute(block, axis, [(i, (i + distance) % n) for i in range(n)])]
    pallas_call x0 -> x8, Pallas kernels: none -> 113 us  [the longest x2 30.6 us: attend_back(): pl.pallas_call(functools.partial(attend_back_kernel, distances, first, la...]
    ppermute x6 -> x79, starting transfers between devices: 14.3 us -> 126 us  [shift(): lax.ppermute(block, axis, [(i, (i + distance) % n) for i in range(n)])]
    dot_general x28 -> x1, matrix products: 108 us -> 2.05 us  [per_device(): jnp.dot(grad_middle_all, out_whole, preferred_element_type=F32).astype(BF)]
    another operation x5 -> x1, other arithmetic: 29.7 us -> 1.22 us
  transfers between devices with their start and end apart: 22 -> 81, of which waited for: 15 -> 26; matrix products, arithmetic and copies ran while one was open for 15% -> 25% of each run, Pallas kernels for 0% -> 12%
where the time goes in v1:
time: 552 us; the launch traced here: 543 us
  waiting for transfers between devices  129 us (23%)
  starting transfers between devices  126 us (23%)
  Pallas kernels  113 us (20%)
  local copies, waits for them, and re-layouts  90.7 us (16%)
  matrix products  31.9 us (6%)
  other arithmetic  28.2 us (5%)
  between operations  16 us (3%)
  blocking collectives  7.11 us (1%)
    ppermute x79, waiting for transfers between devices, shift(): lax.ppermute(block, axis, [(i, (i + distance) % n) for i in range(n)])  129 us
    ppermute x79, starting transfers between devices, shift(): lax.ppermute(block, axis, [(i, (i + distance) % n) for i in range(n)])  126 us
    unnamed x192, local copies, waits for them, and re-layouts  37.6 us
    pallas_call x2, Pallas kernels, attend_back(): pl.pallas_call(functools.partial(attend_back_kernel, distances, first, la...  30.6 us
    pallas_call x2, Pallas kernels, rows_grad(): pl.pallas_call(functools.partial(rows_grad_kernel, len(grads), gain_row),...  24.7 us
    dot_general x16, matrix products, contract_first(): lax.dot_general(left, right, (((0,), (0,)), ((), ())), preferred_element_...  21 us
    pallas_call x1, Pallas kernels, hidden_units(): pl.pallas_call(hidden_kernel, grid=(tiles,), out_shape=(jax.ShapeDtypeStr...  20.1 us
    pallas_call x1, Pallas kernels, attend(): pl.pallas_call(attend_kernel, out_shape=(jax.ShapeDtypeStruct((span, widt...  18.4 us
  transfers between devices with their start and end apart: 81, of which 26 were waited for; matrix products, arithmetic and copies ran while one was open for 25% of the time, Pallas kernels for 12%

profile of v1, /device:TPU:1, one launch (start us, length us, event | category | flops | bytes accessed | tf_op | source)
XLA Modules:
  0.0 542.8 jit_solution(13824551249729707209)
XLA Ops:
  8.0 3.7 collective-permute-start.3
  16.2 3.0 collective-permute-start.36
  21.8 2.2 collective-permute-start.5
  30.5 4.3 collective-permute-done.13
  34.9 4.6 collective-permute-done.20
  43.3 2.7 collective-permute-start.8
  47.4 9.5 %collective-permute-done.7 = bf16[4,128,384]{2,1,0:T(8,128)(2,1)S(1)} collective-permute-done((bf16[4,128,384]{2,1,0:T(8,128)(2,1)S(1)}, bf16[4,128,384]{2,1,0:T(8,128)(2,1)S(1)}, u32[]{:S(2)}, u32[]{:S(2)}) %collective-permute-start.7) | collective-permute-done | bytes 393248 | tf_op jit(solution)/shard_map/ppermute | solution.py:30
  56.9 11.6 %collective-permute-start = (bf16[128,2048]{1,0:T(8,128)(2,1)S(1)}, bf16[128,2048]{1,0:T(8,128)(2,1)S(1)}, u32[]{:S(2)}, u32[]{:S(2)}) collective-permute-start(bf16[128,2048]{1,0:T(8,128)(2,1)S(1)} %copy.68.refs_0_.refs_4_), channel_id=1, source_target_pairs={{0,1},{1,0},{2,3},{3,2},{4,5},{5,4},{6,7},{7,6},{8,9},{9,8},{10,11... | collective-permute-start | bytes 1572872 | tf_op jit(solution)/shard_map/ppermute | solution.py:30
  68.8 9.6 %collective-permute-start.2 = (bf16[128,2048]{1,0:T(8,128)(2,1)S(1)}, bf16[128,2048]{1,0:T(8,128)(2,1)S(1)}, u32[]{:S(2)}, u32[]{:S(2)}) collective-permute-start(bf16[128,2048]{1,0:T(8,128)(2,1)S(1)} %collective-permute-done.1.refs_2_.refs_6_), channel_id=1, source_target_pairs={{0,1},{1,0},{2,3},{3,2},{4,5},{5,4},{6,7},{7,6},{8,9},{9,8},{10,11... | collective-permute-start | bytes 1572872 | tf_op jit(solution)/shard_map/ppermute | solution.py:30
  78.7 6.3 %collective-permute-done.15 = bf16[4,128,384]{2,1,0:T(8,128)(2,1)S(1)} collective-permute-done((bf16[4,128,384]{2,1,0:T(8,128)(2,1)S(1)}, bf16[4,128,384]{2,1,0:T(8,128)(2,1)S(1)}, u32[]{:S(2)}, u32[]{:S(2)}) %collective-permute-start.15) | collective-permute-done | bytes 393248 | tf_op jit(solution)/shard_map/ppermute | solution.py:30
  86.8 7.5 %project.1 = (bf16[512,512]{1,0:T(8,128)(2,1)}, bf16[512,128]{1,0:T(8,128)(2,1)}, bf16[512,2048]{1,0:T(8,128)(2,1)}, f32[8,2048]{1,0:T(8,128)}) custom-call(bf16[128,2048]{1,0:T(8,128)(2,1)} %copy-done.6, bf16[128,2048]{1,0:T(8,128)(2,1)} %copy-done.36, bf16[128,2048]{1,0:T(8,128)(2,1)} %copy-done.35, bf16[128,2048]{1,0:T(8,128)(2,1)} %copy-done.37, ...), custom_call_target="tpu_custom_call" | custom-call | flops 1342177280 | bytes 8388608 | tf_op jit(solution)/shard_map/project/pallas_call | solution.py:383
  95.7 3.6 collective-permute-start.18
  99.4 8.1 %collective-permute-start.24 = (bf16[4,128,512]{2,1,0:T(8,128)(2,1)S(1)}, bf16[4,128,512]{2,1,0:T(8,128)(2,1)S(1)}, u32[]{:S(2)}, u32[]{:S(2)}) collective-permute-start(bf16[4,128,512]{2,1,0:T(8,128)(2,1)S(1)} %bitcast_dynamic-update-slice_fusion.12), channel_id=1, source_target_pairs={{0,16},{16,32},{32,48},{48,0},{1,17},{17,33},{33,49},{49,1},{2,18}... | collective-permute-start | bytes 1572872 | tf_op jit(solution)/shard_map/ppermute | solution.py:30
  107.5 2.8 collective-permute-start.25
  112.5 18.4 %attend.1 = (bf16[512,512]{1,0:T(8,128)(2,1)}, f32[8,512]{1,0:T(8,128)}) custom-call(bf16[512,512]{1,0:T(8,128)(2,1)} %get-tuple-element.56.q_ref, bf16[512,128]{1,0:T(8,128)(2,1)} %get-tuple-element.57.refs_0_, bf16[512,128]{1,0:T(8,128)(2,1)} %copy-done.87, bf16[512,128]{1,0:T(8,128)(2,1)} %copy-done.88, bf16[512,128]{1,0:T(8,128)(2,1)} %copy-done.89, ...), custom_call_target="tpu_custom_call" | custom-call | flops 8589934592 | bytes 2097152 | tf_op jit(solution)/shard_map/attend/pallas_call | solution.py:458
  130.9 2.4 collective-permute-done.24
  133.3 23.4 %collective-permute-done.26 = bf16[4,128,512]{2,1,0:T(8,128)(2,1)S(1)} collective-permute-done((bf16[4,128,512]{2,1,0:T(8,128)(2,1)S(1)}, bf16[4,128,512]{2,1,0:T(8,128)(2,1)S(1)}, u32[]{:S(2)}, u32[]{:S(2)}) %collective-permute-start.26) | collective-permute-done | bytes 524320 | tf_op jit(solution)/shard_map/ppermute | solution.py:30
  159.2 2.8 collective-permute-start.28
  162.0 2.3 collective-permute-done.28
  167.6 11.0 %collective-permute-done.29 = bf16[128,2048]{1,0:T(8,128)(2,1)S(1)} collective-permute-done((bf16[128,2048]{1,0:T(8,128)(2,1)}, bf16[128,2048]{1,0:T(8,128)(2,1)S(1)}, u32[]{:S(2)}, u32[]{:S(2)}) %collective-permute-start.29) | collective-permute-done | bytes 524320 | tf_op jit(solution)/shard_map/ppermute | solution.py:30
  183.9 5.9 %collective-permute-done.34.refs_6_ = bf16[128,2048]{1,0:T(8,128)(2,1)S(1)} collective-permute-done((bf16[128,2048]{1,0:T(8,128)(2,1)S(1)}, bf16[128,2048]{1,0:T(8,128)(2,1)S(1)}, u32[]{:S(2)}, u32[]{:S(2)}) %collective-permute-start.34) | collective-permute-done | bytes 524320 | tf_op jit(solution)/shard_map/ppermute | solution.py:30
  191.9 9.1 %collective-permute-done.31.refs_2_.refs_6_ = bf16[128,2048]{1,0:T(8,128)(2,1)S(1)} collective-permute-done((bf16[128,2048]{1,0:T(8,128)(2,1)S(1)}, bf16[128,2048]{1,0:T(8,128)(2,1)S(1)}, u32[]{:S(2)}, u32[]{:S(2)}) %collective-permute-start.31) | collective-permute-done | bytes 524320 | tf_op jit(solution)/shard_map/ppermute | solution.py:30
  204.6 20.1 %hidden_units.1 = (bf16[512,1408]{1,0:T(8,128)(2,1)}, bf16[512,1408]{1,0:T(8,128)(2,1)}, bf16[512,1408]{1,0:T(8,128)(2,1)}, bf16[512,2048]{1,0:T(8,128)(2,1)}, bf16[512,2048]{1,0:T(8,128)(2,1)}) custom-call(bf16[128,2048]{1,0:T(8,128)(2,1)} %copy-done.15, bf16[128,2048]{1,0:T(8,128)(2,1)} %copy-done.20, bf16[128,2048]{1,0:T(8,128)(2,1)} %copy-done.19, ...), custom_call_target="tpu_custom_call" | custom-call | flops 8858370048 | bytes 17301504 | tf_op jit(solution)/shard_map/hidden_units/pallas_call | solution.py:411
  224.7 14.8 %rows_grad.2 = bf16[512,2048]{1,0:T(8,128)(2,1)} custom-call(bf16[512,1408]{1,0:T(8,128)(2,1)} %get-tuple-element.72.refs_0_, bf16[512,1408]{1,0:T(8,128)(2,1)} %get-tuple-element.73.refs_1_, bf16[2048,4224]{1,0:T(8,128)(2,1)} %all-gather.2.cloned.1.call-done.refs_9_.refs_10_.refs_11_.refs_2_.refs_3_, ...), custom_call_target="tpu_custom_call" | custom-call | flops 5905580032 | bytes 8388608 | tf_op jit(solution)/shard_map/rows_grad/pallas_call | solution.py:435
  239.5 11.7 %weight_grads.1 = bf16[2048,2816]{1,0:T(8,128)(2,1)} custom-call(bf16[512,2048]{1,0:T(8,128)(2,1)} %get-tuple-element.99.left_ref, bf16[512,1408]{1,0:T(8,128)(2,1)} %get-tuple-element.72.refs_0_, bf16[512,1408]{1,0:T(8,128)(2,1)} %get-tuple-element.73.refs_1_), custom_call_target="tpu_custom_call" | custom-call | flops 5905580032 | bytes 15728640 | tf_op jit(solution)/shard_map/weight_grads/pallas_call | solution.py:516
  255.5 3.4 reshape.231
  258.9 5.5 %constant_dynamic-slice_fusion.7 = (bf16[512,4,1,128]{3,2,1,0:T(2,128)(2,1)}, bf16[512,4,1,128]{3,2,1,0:T(2,128)(2,1)}, bf16[512,4,1,128]{3,2,1,0:T(2,128)(2,1)}, bf16[512,4,1,128]{3,2,1,0:T(2,128)(2,1)}) fusion(bf16[512,4,4,128]{3,2,1,0:T(4,128)(2,1)S(1)} %reshape.231, u32[]{:T(128)S(6)} %convert_element_type.430, u32[]{:T(128)S(6)} %convert_element_type.469, ...), kind=kLoop, calls=%fused_computation.156 | loop fusion | bytes 4194320 | tf_op jit(solution)/shard_map/jit(dynamic_index_in_dim)/dynamic_slice | solution.py:43
  264.4 3.5 copy.107
  267.9 3.5 copy.106
  271.4 3.5 copy.105
  274.9 3.5 copy.104
  278.4 4.4 reshape.217
  283.3 4.8 constant_dynamic-slice_fusion.2
  295.0 3.3 collective-permute-start.66
  298.3 4.6 collective-permute-done.39
  311.1 4.8 collective-permute-done.41
  317.8 7.6 %fusion = f32[512,2048]{1,0:T(8,128)} fusion(bf16[512,1408]{1,0:T(8,128)(2,1)S(1)} %copy-done.83, bf16[2048,4224]{1,0:T(8,128)(2,1)} %all-gather.2.cloned.1.call-done.refs_9_.refs_10_.refs_11_.refs_2_.refs_3_), kind=kOutput, calls=%fused_computation.1 | convolution fusion | flops 2952790016 | bytes 11403264 | tf_op jit(solution)/shard_map/dot_general | solution.py:91
  328.5 3.2 reshape.224
  331.7 5.5 %constant_dynamic-slice_fusion.8 = (bf16[512,4,1,128]{3,2,1,0:T(2,128)(2,1)}, bf16[512,4,1,128]{3,2,1,0:T(2,128)(2,1)}, bf16[512,4,1,128]{3,2,1,0:T(2,128)(2,1)}, bf16[512,4,1,128]{3,2,1,0:T(2,128)(2,1)}) fusion(bf16[512,4,4,128]{3,2,1,0:T(4,128)(2,1)S(1)} %reshape.224, u32[]{:T(128)S(6)} %convert_element_type.469, u32[]{:T(128)S(6)} %convert_element_type.467, ...), kind=kLoop, calls=%fused_computation.157 | loop fusion | bytes 4194320 | tf_op jit(solution)/shard_map/jit(dynamic_index_in_dim)/dynamic_slice | solution.py:43
  337.2 3.6 copy.100
  340.9 3.5 copy.101
  344.3 2.3 copy.102
  346.6 2.3 copy.103
  355.5 21.0 %attend_back.2 = (f32[512,512]{1,0:T(8,128)}, bf16[1536,128]{1,0:T(8,128)(2,1)}, bf16[512,512]{1,0:T(8,128)(2,1)}, f32[8,512]{1,0:T(8,128)}) custom-call(bf16[512,512]{1,0:T(8,128)(2,1)} %get-tuple-element.56.q_ref, bf16[512,128]{1,0:T(8,128)(2,1)} %copy-done.87, bf16[512,128]{1,0:T(8,128)(2,1)} %copy-done.88, bf16[512,128]{1,0:T(8,128)(2,1)} %copy-done.89, ...), custom_call_target="tpu_custom_call" | custom-call | flops 16106127360 | bytes 4194304 | tf_op jit(solution)/shard_map/attend_back/pallas_call | solution.py:494
  376.5 9.6 %attend_back.3 = (bf16[512,512]{1,0:T(8,128)(2,1)}, f32[512,128]{1,0:T(8,128)}) custom-call(bf16[512,512]{1,0:T(8,128)(2,1)} %get-tuple-element.56.q_ref, bf16[512,128]{1,0:T(8,128)(2,1)} %get-tuple-element.57.refs_0_, s32[1,1]{1,0:T(1,128)} %bitcast.30.refs_4_.refs_3_.refs_1_, s32[1,512]{1,0:T(1,128)} %bitcast.270, ...), custom_call_target="tpu_custom_call" | custom-call | flops 5368709120 | bytes 4194304 | tf_op jit(solution)/shard_map/attend_back/pallas_call | solution.py:494
  390.2 2.4 collective-permute-start.46
  392.6 3.0 add_convert_fusion
  396.7 2.4 collective-permute-start.70
  408.8 3.2 collective-permute-start.59
  412.1 9.9 %rows_grad.3 = bf16[512,2048]{1,0:T(8,128)(2,1)} custom-call(bf16[512,384]{1,0:T(8,128)(2,1)} %slice.132.refs_0_, bf16[512,256]{1,0:T(8,128)(2,1)} %copy-done.43, bf16[2048,384]{1,0:T(8,128)(2,1)} %bitcast.220, bf16[2048,384]{1,0:T(8,128)(2,1)} %bitcast.222, bf16[128,2048]{1,0:T(8,128)(2,1)} %copy-done.6, bf16[128,2048]{1,0:T(8,128)(2,1)} %copy-done.36, ...), custom_call_target="tpu_custom_call" | custom-call | flops 1342177280 | bytes 8388608 | tf_op jit(solution)/shard_map/rows_grad/pallas_call | solution.py:435
  428.6 2.3 collective-permute-start.73
  433.1 2.5 collective-permute-done.54
  437.8 9.2 %collective-permute-done.53 = bf16[512,384]{1,0:T(8,128)(2,1)S(1)} collective-permute-done((bf16[512,384]{1,0:T(8,128)(2,1)S(1)}, bf16[512,384]{1,0:T(8,128)(2,1)S(1)}, u32[]{:S(2)}, u32[]{:S(2)}) %collective-permute-start.53) | collective-permute-done | bytes 393248 | tf_op jit(solution)/shard_map/ppermute | solution.py:30
  452.9 3.8 collective-permute-done.63
  460.8 2.7 collective-permute-start.56
  465.1 3.3 collective-permute-start.44
  468.4 3.6 collective-permute-start.43
  472.3 2.2 collective-permute-start.64
  480.3 3.2 collective-permute-start.49
  487.5 16.1 %collective-permute-done.77 = bf16[64,1920]{1,0:T(8,128)(2,1)S(1)} collective-permute-done((bf16[64,1920]{1,0:T(8,128)(2,1)S(1)}, bf16[64,1920]{1,0:T(8,128)(2,1)S(1)}, u32[]{:S(2)}, u32[]{:S(2)}) %collective-permute-start.77) | collective-permute-done | bytes 245792 | tf_op jit(solution)/shard_map/ppermute | solution.py:30
  505.2 2.6 add_convert_fusion.3
  515.4 3.1 add_add_fusion
  521.6 3.7 collective-permute-done.78
  527.4 7.1 %all-reduce = (f32[64]{0:T(128)S(1)}, f32[64]{0:T(128)S(1)}) all-reduce(f32[64]{0:T(128)S(1)} %add.300, f32[64]{0:T(128)S(1)} %get-tuple-element.125), channel_id=1, replica_groups=mesh['yh'=2,'z'=4,'x'=4,'yl'=2,'core'=2] {'yl','core'}, use_global_device_ids=true, to_apply=%region_2.3 | all-reduce | flops 128 | bytes 1024 | tf_op jit(solution)/shard_map/psum | solution.py:655
  (436 shorter events, 135.7 us)
Async XLA Ops:
  7.2 196.6 %all-gather.2.cloned.1.call-start = ((), (), s32[]{:S(2)}) async-start(), calls=%async_computation.1 | async-start | bytes 18382848 | tf_op jit(solution)/shard_map/all_gather | solution.py:569
  8.0 11.2 %collective-permute-start.3 = (bf16[64,384]{1,0:T(8,128)(2,1)S(1)}, bf16[64,384]{1,0:T(8,128)(2,1)S(1)}, u32[]{:S(2)}, u32[]{:S(2)}) collective-permute-start(bf16[64,384]{1,0:T(8,128)(2,1)S(1)} %slice.117), channel_id=1, source_target_pairs={{0,64},{64,0},{1,65},{65,1},{2,66},{66,2},{3,67},{67,3},{4,68},{68... | collective-permute-start | bytes 147464 | tf_op jit(solution)/shard_map/ppermute | solution.py:30
  14.9 10.3 %collective-permute-start.10 = (bf16[64,384]{1,0:T(8,128)(2,1)S(1)}, bf16[64,384]{1,0:T(8,128)(2,1)S(1)}, u32[]{:S(2)}, u32[]{:S(2)}) collective-permute-start(bf16[64,384]{1,0:T(8,128)(2,1)S(1)} %concatenate.40), channel_id=1, source_target_pairs={{0,64},{64,0},{1,65},{65,1},{2,66},{66,2},{3,67},{67,3},{4,68},{68... | collective-permute-start | bytes 147464 | tf_op jit(solution)/shard_map/ppermute | solution.py:30
  16.2 23.3 %collective-permute-start.36 = (bf16[64,4224]{1,0:T(8,128)(2,1)S(1)}, bf16[64,4224]{1,0:T(8,128)(2,1)S(1)}, u32[]{:S(2)}, u32[]{:S(2)}) collective-permute-start(bf16[64,4224]{1,0:T(8,128)(2,1)S(1)} %pad_maximum_fusion.2), channel_id=1, source_target_pairs={{0,64},{64,0},{1,65},{65,1},{2,66},{66,2},{3,67},{67,3},{4,68},{68... | collective-permute-start | bytes 1622024 | tf_op jit(solution)/shard_map/ppermute | solution.py:30
  41.0 472.9 %reduce-scatter.2.cloned.1.call-start = ((), (), s32[]{:S(2)}) async-start(), calls=%async_computation.2 | async-start | bytes 12255232 | tf_op jit(solution)/shard_map/reduce_scatter | solution.py:602
  41.6 27.2 %collective-permute-start.1 = (bf16[128,2048]{1,0:T(8,128)(2,1)S(1)}, bf16[128,2048]{1,0:T(8,128)(2,1)S(1)}, u32[]{:S(2)}, u32[]{:S(2)}) collective-permute-start(bf16[128,2048]{1,0:T(8,128)(2,1)S(1)} %copy.68.refs_0_.refs_4_), channel_id=1, source_target_pairs={{0,2},{2,0},{1,3},{3,1},{4,6},{6,4},{5,7},{7,5},{8,10},{10,8},{9,1... | collective-permute-start | bytes 1572872 | tf_op jit(solution)/shard_map/ppermute | solution.py:30
  43.3 13.6 %collective-permute-start.7 = (bf16[4,128,384]{2,1,0:T(8,128)(2,1)S(1)}, bf16[4,128,384]{2,1,0:T(8,128)(2,1)S(1)}, u32[]{:S(2)}, u32[]{:S(2)}) collective-permute-start(bf16[4,128,384]{2,1,0:T(8,128)(2,1)S(1)} %bitcast_dynamic-update-slice_fusion.20), channel_id=1, source_target_pairs={{0,4},{4,8},{8,12},{12,0},{1,5},{5,9},{9,13},{13,1},{2,6},{6,10},{... | collective-permute-start | bytes 1179656 | tf_op jit(solution)/shard_map/ppermute | solution.py:30
  43.3 25.1 %collective-permute-start.8 = (bf16[4,128,384]{2,1,0:T(8,128)(2,1)S(1)}, bf16[4,128,384]{2,1,0:T(8,128)(2,1)S(1)}, u32[]{:S(2)}, u32[]{:S(2)}) collective-permute-start(bf16[4,128,384]{2,1,0:T(8,128)(2,1)S(1)} %bitcast_dynamic-update-slice_fusion.20), channel_id=1, source_target_pairs={{0,12},{4,0},{8,4},{12,8},{1,13},{5,1},{9,5},{13,9},{2,14},{6,2},{... | collective-permute-start | bytes 1179656 | tf_op jit(solution)/shard_map/ppermute | solution.py:30
  46.0 22.5 %collective-permute-start.9 = (bf16[4,128,384]{2,1,0:T(8,128)(2,1)S(1)}, bf16[4,128,384]{2,1,0:T(8,128)(2,1)S(1)}, u32[]{:S(2)}, u32[]{:S(2)}) collective-permute-start(bf16[4,128,384]{2,1,0:T(8,128)(2,1)S(1)} %bitcast_dynamic-update-slice_fusion.20), channel_id=1, source_target_pairs={{0,8},{4,12},{8,0},{12,4},{1,9},{5,13},{9,1},{13,5},{2,10},{6,14},... | collective-permute-start | bytes 1179656 | tf_op jit(solution)/shard_map/ppermute | solution.py:30
  46.0 22.7 %collective-permute-start.14 = (bf16[4,128,384]{2,1,0:T(8,128)(2,1)S(1)}, bf16[4,128,384]{2,1,0:T(8,128)(2,1)S(1)}, u32[]{:S(2)}, u32[]{:S(2)}) collective-permute-start(bf16[4,128,384]{2,1,0:T(8,128)(2,1)S(1)} %bitcast_dynamic-update-slice_fusion.16), channel_id=1, source_target_pairs={{0,16},{16,32},{32,48},{48,0},{1,17},{17,33},{33,49},{49,1},{2,18}... | collective-permute-start | bytes 1179656 | tf_op jit(solution)/shard_map/ppermute | solution.py:30
  56.9 28.4 %collective-permute-start = (bf16[128,2048]{1,0:T(8,128)(2,1)S(1)}, bf16[128,2048]{1,0:T(8,128)(2,1)S(1)}, u32[]{:S(2)}, u32[]{:S(2)}) collective-permute-start(bf16[128,2048]{1,0:T(8,128)(2,1)S(1)} %copy.68.refs_0_.refs_4_), channel_id=1, source_target_pairs={{0,1},{1,0},{2,3},{3,2},{4,5},{5,4},{6,7},{7,6},{8,9},{9,8},{10,11... | collective-permute-start | bytes 1572872 | tf_op jit(solution)/shard_map/ppermute | solution.py:30
  68.5 16.5 %collective-permute-start.15 = (bf16[4,128,384]{2,1,0:T(8,128)(2,1)S(1)}, bf16[4,128,384]{2,1,0:T(8,128)(2,1)S(1)}, u32[]{:S(2)}, u32[]{:S(2)}) collective-permute-start(bf16[4,128,384]{2,1,0:T(8,128)(2,1)S(1)} %bitcast_dynamic-update-slice_fusion.16), channel_id=1, source_target_pairs={{0,48},{16,0},{32,16},{48,32},{1,49},{17,1},{33,17},{49,33},{2,50}... | collective-permute-start | bytes 1179656 | tf_op jit(solution)/shard_map/ppermute | solution.py:30
  68.5 16.5 %collective-permute-start.16 = (bf16[4,128,384]{2,1,0:T(8,128)(2,1)S(1)}, bf16[4,128,384]{2,1,0:T(8,128)(2,1)S(1)}, u32[]{:S(2)}, u32[]{:S(2)}) collective-permute-start(bf16[4,128,384]{2,1,0:T(8,128)(2,1)S(1)} %bitcast_dynamic-update-slice_fusion.16), channel_id=1, source_target_pairs={{0,32},{16,48},{32,0},{48,16},{1,33},{17,49},{33,1},{49,17},{2,34}... | collective-permute-start | bytes 1179656 | tf_op jit(solution)/shard_map/ppermute | solution.py:30
  68.7 30.6 %collective-permute-start.21 = (bf16[128,512]{1,0:T(8,128)(2,1)S(1)}, bf16[128,512]{1,0:T(8,128)(2,1)S(1)}, u32[]{:S(2)}, u32[]{:S(2)}) collective-permute-start(bf16[128,512]{1,0:T(8,128)(2,1)S(1)} %pad_maximum_fusion.6), channel_id=1, source_target_pairs={{0,4},{4,8},{8,12},{12,0},{1,5},{5,9},{9,13},{13,1},{2,6},{6,10},{... | collective-permute-start | bytes 393224 | tf_op jit(solution)/shard_map/ppermute | solution.py:30
  68.8 16.6 %collective-permute-start.2 = (bf16[128,2048]{1,0:T(8,128)(2,1)S(1)}, bf16[128,2048]{1,0:T(8,128)(2,1)S(1)}, u32[]{:S(2)}, u32[]{:S(2)}) collective-permute-start(bf16[128,2048]{1,0:T(8,128)(2,1)S(1)} %collective-permute-done.1.refs_2_.refs_6_), channel_id=1, source_target_pairs={{0,1},{1,0},{2,3},{3,2},{4,5},{5,4},{6,7},{7,6},{8,9},{9,8},{10,11... | collective-permute-start | bytes 1572872 | tf_op jit(solution)/shard_map/ppermute | solution.py:30
  85.0 14.3 %collective-permute-start.22 = (bf16[128,512]{1,0:T(8,128)(2,1)S(1)}, bf16[128,512]{1,0:T(8,128)(2,1)S(1)}, u32[]{:S(2)}, u32[]{:S(2)}) collective-permute-start(bf16[128,512]{1,0:T(8,128)(2,1)S(1)} %pad_maximum_fusion.6), channel_id=1, source_target_pairs={{0,12},{4,0},{8,4},{12,8},{1,13},{5,1},{9,5},{13,9},{2,14},{6,2},{... | collective-permute-start | bytes 393224 | tf_op jit(solution)/shard_map/ppermute | solution.py:30
  85.0 14.3 %collective-permute-start.23 = (bf16[128,512]{1,0:T(8,128)(2,1)S(1)}, bf16[128,512]{1,0:T(8,128)(2,1)S(1)}, u32[]{:S(2)}, u32[]{:S(2)}) collective-permute-start(bf16[128,512]{1,0:T(8,128)(2,1)S(1)} %pad_maximum_fusion.6), channel_id=1, source_target_pairs={{0,8},{4,12},{8,0},{12,4},{1,9},{5,13},{9,1},{13,5},{2,10},{6,14},... | collective-permute-start | bytes 393224 | tf_op jit(solution)/shard_map/ppermute | solution.py:30
  94.3 16.3 %collective-permute-start.17 = (bf16[512,128]{1,0:T(8,128)(2,1)}, bf16[512,128]{1,0:T(8,128)(2,1)S(1)}, u32[]{:S(2)}, u32[]{:S(2)}) collective-permute-start(bf16[512,128]{1,0:T(8,128)(2,1)} %get-tuple-element.57.refs_0_), channel_id=1, source_target_pairs={{0,4},{4,8},{8,12},{12,0},{1,5},{5,9},{9,13},{13,1},{2,6},{6,10},{... | collective-permute-start | bytes 393224 | tf_op jit(solution)/shard_map/ppermute | solution.py:30
  95.7 16.1 %collective-permute-start.18 = (bf16[512,128]{1,0:T(8,128)(2,1)}, bf16[512,128]{1,0:T(8,128)(2,1)S(1)}, u32[]{:S(2)}, u32[]{:S(2)}) collective-permute-start(bf16[512,128]{1,0:T(8,128)(2,1)} %get-tuple-element.57.refs_0_), channel_id=1, source_target_pairs={{0,8},{4,12},{8,0},{12,4},{1,9},{5,13},{9,1},{13,5},{2,10},{6,14},... | collective-permute-start | bytes 393224 | tf_op jit(solution)/shard_map/ppermute | solution.py:30
  99.3 12.5 %collective-permute-start.19 = (bf16[512,128]{1,0:T(8,128)(2,1)}, bf16[512,128]{1,0:T(8,128)(2,1)S(1)}, u32[]{:S(2)}, u32[]{:S(2)}) collective-permute-start(bf16[512,128]{1,0:T(8,128)(2,1)} %get-tuple-element.57.refs_0_), channel_id=1, source_target_pairs={{0,12},{4,0},{8,4},{12,8},{1,13},{5,1},{9,5},{13,9},{2,14},{6,2},{... | collective-permute-start | bytes 393224 | tf_op jit(solution)/shard_map/ppermute | solution.py:30
  99.4 33.9 %collective-permute-start.24 = (bf16[4,128,512]{2,1,0:T(8,128)(2,1)S(1)}, bf16[4,128,512]{2,1,0:T(8,128)(2,1)S(1)}, u32[]{:S(2)}, u32[]{:S(2)}) collective-permute-start(bf16[4,128,512]{2,1,0:T(8,128)(2,1)S(1)} %bitcast_dynamic-update-slice_fusion.12), channel_id=1, source_target_pairs={{0,16},{16,32},{32,48},{48,0},{1,17},{17,33},{33,49},{49,1},{2,18}... | collective-permute-start | bytes 1572872 | tf_op jit(solution)/shard_map/ppermute | solution.py:30
  107.5 25.8 %collective-permute-start.25 = (bf16[4,128,512]{2,1,0:T(8,128)(2,1)S(1)}, bf16[4,128,512]{2,1,0:T(8,128)(2,1)S(1)}, u32[]{:S(2)}, u32[]{:S(2)}) collective-permute-start(bf16[4,128,512]{2,1,0:T(8,128)(2,1)S(1)} %bitcast_dynamic-update-slice_fusion.12), channel_id=1, source_target_pairs={{0,48},{16,0},{32,16},{48,32},{1,49},{17,1},{33,17},{49,33},{2,50}... | collective-permute-start | bytes 1572872 | tf_op jit(solution)/shard_map/ppermute | solution.py:30
  110.6 46.2 %collective-permute-start.26 = (bf16[4,128,512]{2,1,0:T(8,128)(2,1)S(1)}, bf16[4,128,512]{2,1,0:T(8,128)(2,1)S(1)}, u32[]{:S(2)}, u32[]{:S(2)}) collective-permute-start(bf16[4,128,512]{2,1,0:T(8,128)(2,1)S(1)} %bitcast_dynamic-update-slice_fusion.12), channel_id=1, source_target_pairs={{0,32},{16,48},{32,0},{48,16},{1,33},{17,49},{33,1},{49,17},{2,34}... | collective-permute-start | bytes 1572872 | tf_op jit(solution)/shard_map/ppermute | solution.py:30
  165.2 13.5 %collective-permute-start.29 = (bf16[128,2048]{1,0:T(8,128)(2,1)}, bf16[128,2048]{1,0:T(8,128)(2,1)S(1)}, u32[]{:S(2)}, u32[]{:S(2)}) collective-permute-start(bf16[128,2048]{1,0:T(8,128)(2,1)} %fusion.4), channel_id=1, source_target_pairs={{0,2},{2,0},{1,3},{3,1},{4,6},{6,4},{5,7},{7,5},{8,10},{10,8},{9,1... | collective-permute-start | bytes 1572872 | tf_op jit(solution)/shard_map/ppermute | solution.py:30
  167.1 22.8 %collective-permute-start.34 = (bf16[128,2048]{1,0:T(8,128)(2,1)S(1)}, bf16[128,2048]{1,0:T(8,128)(2,1)S(1)}, u32[]{:S(2)}, u32[]{:S(2)}) collective-permute-start(bf16[128,2048]{1,0:T(8,128)(2,1)S(1)} %copy.82.refs_4_), channel_id=1, source_target_pairs={{0,2},{2,0},{1,3},{3,1},{4,6},{6,4},{5,7},{7,5},{8,10},{10,8},{9,1... | collective-permute-start | bytes 1572872 | tf_op jit(solution)/shard_map/ppermute | solution.py:30
  180.4 20.6 %collective-permute-start.31 = (bf16[128,2048]{1,0:T(8,128)(2,1)S(1)}, bf16[128,2048]{1,0:T(8,128)(2,1)S(1)}, u32[]{:S(2)}, u32[]{:S(2)}) collective-permute-start(bf16[128,2048]{1,0:T(8,128)(2,1)S(1)} %fusion.47.refs_0_.refs_4_), channel_id=1, source_target_pairs={{0,2},{2,0},{1,3},{3,1},{4,6},{6,4},{5,7},{7,5},{8,10},{10,8},{9,1... | collective-permute-start | bytes 1572872 | tf_op jit(solution)/shard_map/ppermute | solution.py:30
  181.7 20.5 %collective-permute-start.33 = (bf16[128,2048]{1,0:T(8,128)(2,1)S(1)}, bf16[128,2048]{1,0:T(8,128)(2,1)S(1)}, u32[]{:S(2)}, u32[]{:S(2)}) collective-permute-start(bf16[128,2048]{1,0:T(8,128)(2,1)S(1)} %copy.82.refs_4_), channel_id=1, source_target_pairs={{0,1},{1,0},{2,3},{3,2},{4,5},{5,4},{6,7},{7,6},{8,9},{9,8},{10,11... | collective-permute-start | bytes 1572872 | tf_op jit(solution)/shard_map/ppermute | solution.py:30
  189.9 12.3 %collective-permute-start.35 = (bf16[128,2048]{1,0:T(8,128)(2,1)S(1)}, bf16[128,2048]{1,0:T(8,128)(2,1)S(1)}, u32[]{:S(2)}, u32[]{:S(2)}) collective-permute-start(bf16[128,2048]{1,0:T(8,128)(2,1)S(1)} %collective-permute-done.34.refs_6_), channel_id=1, source_target_pairs={{0,1},{1,0},{2,3},{3,2},{4,5},{5,4},{6,7},{7,6},{8,9},{9,8},{10,11... | collective-permute-start | bytes 1572872 | tf_op jit(solution)/shard_map/ppermute | solution.py:30
  191.8 10.5 %collective-permute-start.30 = (bf16[128,2048]{1,0:T(8,128)(2,1)S(1)}, bf16[128,2048]{1,0:T(8,128)(2,1)S(1)}, u32[]{:S(2)}, u32[]{:S(2)}) collective-permute-start(bf16[128,2048]{1,0:T(8,128)(2,1)S(1)} %fusion.47.refs_0_.refs_4_), channel_id=1, source_target_pairs={{0,1},{1,0},{2,3},{3,2},{4,5},{5,4},{6,7},{7,6},{8,9},{9,8},{10,11... | collective-permute-start | bytes 1572872 | tf_op jit(solution)/shard_map/ppermute | solution.py:30
  253.8 34.2 %collective-permute-start.38 = (bf16[128,2048]{1,0:T(8,128)(2,1)}, bf16[128,2048]{1,0:T(8,128)(2,1)}, u32[]{:S(2)}, u32[]{:S(2)}) collective-permute-start(bf16[128,2048]{1,0:T(8,128)(2,1)} %get-tuple-element.145), channel_id=1, source_target_pairs={{0,1},{1,0},{2,3},{3,2},{4,5},{5,4},{6,7},{7,6},{8,9},{9,8},{10,11... | collective-permute-start | bytes 1572872 | tf_op jit(solution)/shard_map/ppermute | solution.py:30
  282.8 15.4 %collective-permute-start.37 = (bf16[128,2048]{1,0:T(8,128)(2,1)}, bf16[128,2048]{1,0:T(8,128)(2,1)S(1)}, u32[]{:S(2)}, u32[]{:S(2)}) collective-permute-start(bf16[128,2048]{1,0:T(8,128)(2,1)} %get-tuple-element.144), channel_id=1, source_target_pairs={{0,1},{1,0},{2,3},{3,2},{4,5},{5,4},{6,7},{7,6},{8,9},{9,8},{10,11... | collective-permute-start | bytes 1572872 | tf_op jit(solution)/shard_map/ppermute | solution.py:30
  289.3 13.5 %collective-permute-start.39 = (bf16[128,2048]{1,0:T(8,128)(2,1)S(1)}, bf16[128,2048]{1,0:T(8,128)(2,1)S(1)}, u32[]{:S(2)}, u32[]{:S(2)}) collective-permute-start(bf16[128,2048]{1,0:T(8,128)(2,1)S(1)} %add_convert_fusion.5), channel_id=1, source_target_pairs={{0,2},{2,0},{1,3},{3,1},{4,6},{6,4},{5,7},{7,5},{8,10},{10,8},{9,1... | collective-permute-start | bytes 1572872 | tf_op jit(solution)/shard_map/ppermute | solution.py:30
  292.8 97.4 %collective-permute-start.67 = (bf16[512,1408]{1,0:T(8,128)(2,1)}, bf16[512,1408]{1,0:T(8,128)(2,1)}, u32[]{:S(2)}, u32[]{:S(2)}) collective-permute-start(bf16[512,1408]{1,0:T(8,128)(2,1)} %convolution_convert_fusion.1), channel_id=1, source_target_pairs={{0,32},{16,48},{32,0},{48,16},{1,33},{17,49},{33,1},{49,17},{2,34}... | collective-permute-start | bytes 4325384 | tf_op jit(solution)/shard_map/ppermute | solution.py:30
  295.0 97.6 %collective-permute-start.66 = (bf16[512,1408]{1,0:T(8,128)(2,1)}, bf16[512,1408]{1,0:T(8,128)(2,1)}, u32[]{:S(2)}, u32[]{:S(2)}) collective-permute-start(bf16[512,1408]{1,0:T(8,128)(2,1)} %convolution_convert_fusion), channel_id=1, source_target_pairs={{0,48},{16,0},{32,16},{48,32},{1,49},{17,1},{33,17},{49,33},{2,50}... | collective-permute-start | bytes 4325384 | tf_op jit(solution)/shard_map/ppermute | solution.py:30
  303.2 12.7 %collective-permute-start.41 = (bf16[128,2048]{1,0:T(8,128)(2,1)S(1)}, bf16[128,2048]{1,0:T(8,128)(2,1)S(1)}, u32[]{:S(2)}, u32[]{:S(2)}) collective-permute-start(bf16[128,2048]{1,0:T(8,128)(2,1)S(1)} %fusion.31), channel_id=1, source_target_pairs={{0,2},{2,0},{1,3},{3,1},{4,6},{6,4},{5,7},{7,5},{8,10},{10,8},{9,1... | collective-permute-start | bytes 1572872 | tf_op jit(solution)/shard_map/ppermute | solution.py:30
  306.7 85.9 %collective-permute-start.65 = (bf16[512,1408]{1,0:T(8,128)(2,1)}, bf16[512,1408]{1,0:T(8,128)(2,1)}, u32[]{:S(2)}, u32[]{:S(2)}) collective-permute-start(bf16[512,1408]{1,0:T(8,128)(2,1)} %convolution_convert_fusion.2), channel_id=1, source_target_pairs={{0,16},{16,32},{32,48},{48,0},{1,17},{17,33},{33,49},{49,1},{2,18}... | collective-permute-start | bytes 4325384 | tf_op jit(solution)/shard_map/ppermute | solution.py:30
  309.6 15.8 %collective-permute-start.40 = (bf16[128,2048]{1,0:T(8,128)(2,1)S(1)}, bf16[128,2048]{1,0:T(8,128)(2,1)S(1)}, u32[]{:S(2)}, u32[]{:S(2)}) collective-permute-start(bf16[128,2048]{1,0:T(8,128)(2,1)S(1)} %fusion.31), channel_id=1, source_target_pairs={{0,1},{1,0},{2,3},{3,2},{4,5},{5,4},{6,7},{7,6},{8,9},{9,8},{10,11... | collective-permute-start | bytes 1572872 | tf_op jit(solution)/shard_map/ppermute | solution.py:30
  316.0 9.4 %collective-permute-start.42 = (bf16[128,2048]{1,0:T(8,128)(2,1)S(1)}, bf16[128,2048]{1,0:T(8,128)(2,1)S(1)}, u32[]{:S(2)}, u32[]{:S(2)}) collective-permute-start(bf16[128,2048]{1,0:T(8,128)(2,1)S(1)} %collective-permute-done.41), channel_id=1, source_target_pairs={{0,1},{1,0},{2,3},{3,2},{4,5},{5,4},{6,7},{7,6},{8,9},{9,8},{10,11... | collective-permute-start | bytes 1572872 | tf_op jit(solution)/shard_map/ppermute | solution.py:30
  389.8 14.4 %collective-permute-start.48 = (bf16[512,128]{1,0:T(8,128)(2,1)S(1)}, bf16[512,128]{1,0:T(8,128)(2,1)S(1)}, u32[]{:S(2)}, u32[]{:S(2)}) collective-permute-start(bf16[512,128]{1,0:T(8,128)(2,1)S(1)} %get-tuple-element.164), channel_id=1, source_target_pairs={{0,4},{4,8},{8,12},{12,0},{1,5},{5,9},{9,13},{13,1},{2,6},{6,10},{... | collective-permute-start | bytes 393224 | tf_op jit(solution)/shard_map/ppermute | solution.py:30
  389.9 15.2 %collective-permute-start.47 = (bf16[512,128]{1,0:T(8,128)(2,1)S(1)}, bf16[512,128]{1,0:T(8,128)(2,1)S(1)}, u32[]{:S(2)}, u32[]{:S(2)}) collective-permute-start(bf16[512,128]{1,0:T(8,128)(2,1)S(1)} %get-tuple-element.165), channel_id=1, source_target_pairs={{0,8},{4,12},{8,0},{12,4},{1,9},{5,13},{9,1},{13,5},{2,10},{6,14},... | collective-permute-start | bytes 393224 | tf_op jit(solution)/shard_map/ppermute | solution.py:30
  390.2 14.9 %collective-permute-start.46 = (bf16[512,128]{1,0:T(8,128)(2,1)S(1)}, bf16[512,128]{1,0:T(8,128)(2,1)S(1)}, u32[]{:S(2)}, u32[]{:S(2)}) collective-permute-start(bf16[512,128]{1,0:T(8,128)(2,1)S(1)} %get-tuple-element.163), channel_id=1, source_target_pairs={{0,12},{4,0},{8,4},{12,8},{1,13},{5,1},{9,5},{13,9},{2,14},{6,2},{... | collective-permute-start | bytes 393224 | tf_op jit(solution)/shard_map/ppermute | solution.py:30
  396.7 26.8 %collective-permute-start.70 = (bf16[128,1408]{1,0:T(8,128)(2,1)}, bf16[128,1408]{1,0:T(8,128)(2,1)}, u32[]{:S(2)}, u32[]{:S(2)}) collective-permute-start(bf16[128,1408]{1,0:T(8,128)(2,1)} %get-tuple-element.153), channel_id=1, source_target_pairs={{0,8},{4,12},{8,0},{12,4},{1,9},{5,13},{9,1},{13,5},{2,10},{6,14},... | collective-permute-start | bytes 1081352 | tf_op jit(solution)/shard_map/ppermute | solution.py:30
  399.0 26.6 %collective-permute-start.69 = (bf16[128,1408]{1,0:T(8,128)(2,1)}, bf16[128,1408]{1,0:T(8,128)(2,1)}, u32[]{:S(2)}, u32[]{:S(2)}) collective-permute-start(bf16[128,1408]{1,0:T(8,128)(2,1)} %get-tuple-element.154), channel_id=1, source_target_pairs={{0,12},{4,0},{8,4},{12,8},{1,13},{5,1},{9,5},{13,9},{2,14},{6,2},{... | collective-permute-start | bytes 1081352 | tf_op jit(solution)/shard_map/ppermute | solution.py:30
  404.3 22.1 %collective-permute-start.68 = (bf16[128,1408]{1,0:T(8,128)(2,1)}, bf16[128,1408]{1,0:T(8,128)(2,1)}, u32[]{:S(2)}, u32[]{:S(2)}) collective-permute-start(bf16[128,1408]{1,0:T(8,128)(2,1)} %get-tuple-element.152), channel_id=1, source_target_pairs={{0,4},{4,8},{8,12},{12,0},{1,5},{5,9},{9,13},{13,1},{2,6},{6,10},{... | collective-permute-start | bytes 1081352 | tf_op jit(solution)/shard_map/ppermute | solution.py:30
  407.8 20.4 %collective-permute-start.60 = (bf16[512,256]{1,0:T(8,128)(2,1)}, bf16[512,256]{1,0:T(8,128)(2,1)S(1)}, u32[]{:S(2)}, u32[]{:S(2)}) collective-permute-start(bf16[512,256]{1,0:T(8,128)(2,1)} %convolution_convert_fusion.13), channel_id=1, source_target_pairs={{0,32},{16,48},{32,0},{48,16},{1,33},{17,49},{33,1},{49,17},{2,34}... | collective-permute-start | bytes 786440 | tf_op jit(solution)/shard_map/ppermute | solution.py:30
  408.8 19.7 %collective-permute-start.59 = (bf16[512,256]{1,0:T(8,128)(2,1)}, bf16[512,256]{1,0:T(8,128)(2,1)}, u32[]{:S(2)}, u32[]{:S(2)}) collective-permute-start(bf16[512,256]{1,0:T(8,128)(2,1)} %convolution_convert_fusion.14), channel_id=1, source_target_pairs={{0,48},{16,0},{32,16},{48,32},{1,49},{17,1},{33,17},{49,33},{2,50}... | collective-permute-start | bytes 786440 | tf_op jit(solution)/shard_map/ppermute | solution.py:30
  425.6 10.0 %collective-permute-start.54 = (bf16[512,384]{1,0:T(8,128)(2,1)S(1)}, bf16[512,384]{1,0:T(8,128)(2,1)S(1)}, u32[]{:S(2)}, u32[]{:S(2)}) collective-permute-start(bf16[512,384]{1,0:T(8,128)(2,1)S(1)} %copy-done.86), channel_id=1, source_target_pairs={{0,8},{4,12},{8,0},{12,4},{1,9},{5,13},{9,1},{13,5},{2,10},{6,14},... | collective-permute-start | bytes 1179656 | tf_op jit(solution)/shard_map/ppermute | solution.py:30
  426.3 20.6 %collective-permute-start.53 = (bf16[512,384]{1,0:T(8,128)(2,1)S(1)}, bf16[512,384]{1,0:T(8,128)(2,1)S(1)}, u32[]{:S(2)}, u32[]{:S(2)}) collective-permute-start(bf16[512,384]{1,0:T(8,128)(2,1)S(1)} %copy-done.85), channel_id=1, source_target_pairs={{0,12},{4,0},{8,4},{12,8},{1,13},{5,1},{9,5},{13,9},{2,14},{6,2},{... | collective-permute-start | bytes 1179656 | tf_op jit(solution)/shard_map/ppermute | solution.py:30
  428.1 21.2 %collective-permute-start.52 = (bf16[512,384]{1,0:T(8,128)(2,1)S(1)}, bf16[512,384]{1,0:T(8,128)(2,1)S(1)}, u32[]{:S(2)}, u32[]{:S(2)}) collective-permute-start(bf16[512,384]{1,0:T(8,128)(2,1)S(1)} %copy-done.84), channel_id=1, source_target_pairs={{0,4},{4,8},{8,12},{12,0},{1,5},{5,9},{9,13},{13,1},{2,6},{6,10},{... | collective-permute-start | bytes 1179656 | tf_op jit(solution)/shard_map/ppermute | solution.py:30
  428.6 43.5 %collective-permute-start.73 = (bf16[512,512]{1,0:T(8,128)(2,1)S(1)}, bf16[512,512]{1,0:T(8,128)(2,1)S(1)}, u32[]{:S(2)}, u32[]{:S(2)}) collective-permute-start(bf16[512,512]{1,0:T(8,128)(2,1)S(1)} %copy-done.52), channel_id=1, source_target_pairs={{0,8},{4,12},{8,0},{12,4},{1,9},{5,13},{9,1},{13,5},{2,10},{6,14},... | collective-permute-start | bytes 1572872 | tf_op jit(solution)/shard_map/ppermute | solution.py:30
  432.0 24.7 %collective-permute-start.63 = (bf16[128,256]{1,0:T(8,128)(2,1)S(1)}, bf16[128,256]{1,0:T(8,128)(2,1)S(1)}, u32[]{:S(2)}, u32[]{:S(2)}) collective-permute-start(bf16[128,256]{1,0:T(8,128)(2,1)S(1)} %get-tuple-element.169), channel_id=1, source_target_pairs={{0,8},{4,12},{8,0},{12,4},{1,9},{5,13},{9,1},{13,5},{2,10},{6,14},... | collective-permute-start | bytes 196616 | tf_op jit(solution)/shard_map/ppermute | solution.py:30
  435.6 23.4 %collective-permute-start.62 = (bf16[128,256]{1,0:T(8,128)(2,1)S(1)}, bf16[128,256]{1,0:T(8,128)(2,1)S(1)}, u32[]{:S(2)}, u32[]{:S(2)}) collective-permute-start(bf16[128,256]{1,0:T(8,128)(2,1)S(1)} %get-tuple-element.170), channel_id=1, source_target_pairs={{0,12},{4,0},{8,4},{12,8},{1,13},{5,1},{9,5},{13,9},{2,14},{6,2},{... | collective-permute-start | bytes 196616 | tf_op jit(solution)/shard_map/ppermute | solution.py:30
  446.9 13.8 %collective-permute-start.61 = (bf16[128,256]{1,0:T(8,128)(2,1)S(1)}, bf16[128,256]{1,0:T(8,128)(2,1)S(1)}, u32[]{:S(2)}, u32[]{:S(2)}) collective-permute-start(bf16[128,256]{1,0:T(8,128)(2,1)S(1)} %get-tuple-element.168), channel_id=1, source_target_pairs={{0,4},{4,8},{8,12},{12,0},{1,5},{5,9},{9,13},{13,1},{2,6},{6,10},{... | collective-permute-start | bytes 196616 | tf_op jit(solution)/shard_map/ppermute | solution.py:30
  449.9 13.5 %collective-permute-start.57 = (bf16[128,384]{1,0:T(8,128)(2,1)S(1)}, bf16[128,384]{1,0:T(8,128)(2,1)S(1)}, u32[]{:S(2)}, u32[]{:S(2)}) collective-permute-start(bf16[128,384]{1,0:T(8,128)(2,1)S(1)} %get-tuple-element.161), channel_id=1, source_target_pairs={{0,32},{16,48},{32,0},{48,16},{1,33},{17,49},{33,1},{49,17},{2,34}... | collective-permute-start | bytes 294920 | tf_op jit(solution)/shard_map/ppermute | solution.py:30
  456.7 15.5 %collective-permute-start.72 = (bf16[512,512]{1,0:T(8,128)(2,1)S(1)}, bf16[512,512]{1,0:T(8,128)(2,1)S(1)}, u32[]{:S(2)}, u32[]{:S(2)}) collective-permute-start(bf16[512,512]{1,0:T(8,128)(2,1)S(1)} %convolution_convert_fusion.4), channel_id=1, source_target_pairs={{0,12},{4,0},{8,4},{12,8},{1,13},{5,1},{9,5},{13,9},{2,14},{6,2},{... | collective-permute-start | bytes 1572872 | tf_op jit(solution)/shard_map/ppermute | solution.py:30
  459.0 15.5 %collective-permute-start.71 = (bf16[512,512]{1,0:T(8,128)(2,1)S(1)}, bf16[512,512]{1,0:T(8,128)(2,1)S(1)}, u32[]{:S(2)}, u32[]{:S(2)}) collective-permute-start(bf16[512,512]{1,0:T(8,128)(2,1)S(1)} %copy-done.51), channel_id=1, source_target_pairs={{0,4},{4,8},{8,12},{12,0},{1,5},{5,9},{9,13},{13,1},{2,6},{6,10},{... | collective-permute-start | bytes 1572872 | tf_op jit(solution)/shard_map/ppermute | solution.py:30
  465.1 9.9 %collective-permute-start.44 = (bf16[128,2048]{1,0:T(8,128)(2,1)S(1)}, bf16[128,2048]{1,0:T(8,128)(2,1)S(1)}, u32[]{:S(2)}, u32[]{:S(2)}) collective-permute-start(bf16[128,2048]{1,0:T(8,128)(2,1)S(1)} %copy-done.65), channel_id=1, source_target_pairs={{0,1},{1,0},{2,3},{3,2},{4,5},{5,4},{6,7},{7,6},{8,9},{9,8},{10,11... | collective-permute-start | bytes 1572872 | tf_op jit(solution)/shard_map/ppermute | solution.py:30
  468.4 36.7 %collective-permute-start.43 = (bf16[128,2048]{1,0:T(8,128)(2,1)S(1)}, bf16[128,2048]{1,0:T(8,128)(2,1)S(1)}, u32[]{:S(2)}, u32[]{:S(2)}) collective-permute-start(bf16[128,2048]{1,0:T(8,128)(2,1)S(1)} %copy-done.64), channel_id=1, source_target_pairs={{0,1},{1,0},{2,3},{3,2},{4,5},{5,4},{6,7},{7,6},{8,9},{9,8},{10,11... | collective-permute-start | bytes 1572872 | tf_op jit(solution)/shard_map/ppermute | solution.py:30
  472.1 14.4 %collective-permute-start.50 = (bf16[128,2048]{1,0:T(8,128)(2,1)S(1)}, bf16[128,2048]{1,0:T(8,128)(2,1)S(1)}, u32[]{:S(2)}, u32[]{:S(2)}) collective-permute-start(bf16[128,2048]{1,0:T(8,128)(2,1)S(1)} %get-tuple-element.137), channel_id=1, source_target_pairs={{0,1},{1,0},{2,3},{3,2},{4,5},{5,4},{6,7},{7,6},{8,9},{9,8},{10,11... | collective-permute-start | bytes 1572872 | tf_op jit(solution)/shard_map/ppermute | solution.py:30
  480.3 35.2 %collective-permute-start.49 = (bf16[128,2048]{1,0:T(8,128)(2,1)}, bf16[128,2048]{1,0:T(8,128)(2,1)}, u32[]{:S(2)}, u32[]{:S(2)}) collective-permute-start(bf16[128,2048]{1,0:T(8,128)(2,1)} %get-tuple-element.136), channel_id=1, source_target_pairs={{0,1},{1,0},{2,3},{3,2},{4,5},{5,4},{6,7},{7,6},{8,9},{9,8},{10,11... | collective-permute-start | bytes 1572872 | tf_op jit(solution)/shard_map/ppermute | solution.py:30
  483.5 21.6 %collective-permute-start.45 = (bf16[128,2048]{1,0:T(8,128)(2,1)S(1)}, bf16[128,2048]{1,0:T(8,128)(2,1)S(1)}, u32[]{:S(2)}, u32[]{:S(2)}) collective-permute-start(bf16[128,2048]{1,0:T(8,128)(2,1)S(1)} %add_convert_fusion.4), channel_id=1, source_target_pairs={{0,2},{2,0},{1,3},{3,1},{4,6},{6,4},{5,7},{7,5},{8,10},{10,8},{9,1... | collective-permute-start | bytes 1572872 | tf_op jit(solution)/shard_map/ppermute | solution.py:30
  484.9 18.8 %collective-permute-start.77 = (bf16[64,1920]{1,0:T(8,128)(2,1)S(1)}, bf16[64,1920]{1,0:T(8,128)(2,1)S(1)}, u32[]{:S(2)}, u32[]{:S(2)}) collective-permute-start(bf16[64,1920]{1,0:T(8,128)(2,1)S(1)} %dynamic-slice_bitcast_fusion.4), channel_id=1, source_target_pairs={{0,64},{64,0},{1,65},{65,1},{2,66},{66,2},{3,67},{67,3},{4,68},{68... | collective-permute-start | bytes 737288 | tf_op jit(solution)/shard_map/ppermute | solution.py:30
  487.5 28.0 %collective-permute-start.51 = (bf16[128,2048]{1,0:T(8,128)(2,1)}, bf16[128,2048]{1,0:T(8,128)(2,1)}, u32[]{:S(2)}, u32[]{:S(2)}) collective-permute-start(bf16[128,2048]{1,0:T(8,128)(2,1)} %add_convert_fusion.2), channel_id=1, source_target_pairs={{0,2},{2,0},{1,3},{3,1},{4,6},{6,4},{5,7},{7,5},{8,10},{10,8},{9,1... | collective-permute-start | bytes 1572872 | tf_op jit(solution)/shard_map/ppermute | solution.py:30
  514.8 10.4 %collective-permute-start.78 = (bf16[64,2816]{1,0:T(8,128)(2,1)S(1)}, bf16[64,2816]{1,0:T(8,128)(2,1)}, u32[]{:S(2)}, u32[]{:S(2)}) collective-permute-start(bf16[64,2816]{1,0:T(8,128)(2,1)S(1)} %dynamic-slice_bitcast_fusion), channel_id=1, source_target_pairs={{0,64},{64,0},{1,65},{65,1},{2,66},{66,2},{3,67},{67,3},{4,68},{68... | collective-permute-start | bytes 1081352 | tf_op jit(solution)/shard_map/ppermute | solution.py:30
  (107 other events, 892.0 us)
Sparse Core Ops, SparseCore 0:
  41.1 152.4 all-gather.1
  251.3 134.1 reduce-scatter.1

commit v2 on v1

--- a/solution.py
+++ b/solution.py
@@ -43,14 +43,31 @@
     return lax.dynamic_index_in_dim(array, index, dim, keepdims=False)
 
 
-def gather_stage(block, axis, dim, hold=()):
+def send_stage(block, axis):
     n = lax.axis_size(axis)
-    order = (0, 1, n - 1, *range(2, n - 1))
-    arrived = [block] + [after(shift(block, axis, d), *hold) for d in order[1:]]
+    return [block] + [shift(block, axis, d) for d in (1, n - 1, *range(2, n - 1))]
+
+
+def stack_stage(arrived, axis, dim):
+    n = len(arrived)
+    block = arrived[0]
     out = jnp.zeros(block.shape[:dim] + (n,) + block.shape[dim:], block.dtype)
-    for d, piece in zip(order, arrived):
+    for d, piece in zip((0, 1, n - 1, *range(2, n - 1)), arrived):
         out = lax.dynamic_update_index_in_dim(out, piece, place(axis, -d), dim)
     return out
+
+
+def gather_ring(block, axis, dim):
+    half = block.shape[0] // 2
+    left, right = shift(block, axis, 1), shift(block, axis, -1)
+    upper, lower = shift(left[:half], axis, 1), shift(right[half:], axis, -1)
+    out = jnp.zeros(block.shape[:dim] + (4,) + block.shape[dim:], block.dtype)
+    out = lax.dynamic_update_index_in_dim(out, block, place(axis), dim)
+    out = lax.dynamic_update_index_in_dim(out, left, place(axis, -1), dim)
+    out = lax.dynamic_update_index_in_dim(out, right, place(axis, 1), dim)
+    return lax.dynamic_update_index_in_dim(
+        out, jnp.concatenate([upper, lower], 0), place(axis, 2), dim
+    )
 
 
 def join_sides(shard, other):
@@ -67,38 +84,27 @@
     return rows.reshape(t, 2, 16, d // 32).transpose(0, 2, 1, 3).reshape(t, d)
 
 
-def from_inner(rows):
-    t, d = rows.shape
-    return rows.reshape(t, 16, 2, d // 32).transpose(0, 2, 1, 3).reshape(t, d)
-
-
 def gather_rows(rows):
     across = swap(rows, "yl")
     return [rows, swap(rows, "core"), across, swap(across, "core")]
 
 
+def scatter_cores(partial):
+    n = partial.shape[0] // 4
+    far = swap(partial[3 * n :], "core").astype(F32)
+    near = swap(partial[n : 2 * n], "core")
+    return partial[:n], near, (partial[2 * n : 3 * n].astype(F32) + far).astype(BF)
+
+
 def scatter_rows(partial):
-    n = partial.shape[0] // 4
-    low = partial.astype(BF)
-    far = swap(low[3 * n :], "core").astype(F32)
-    near = swap(low[n : 2 * n], "core").astype(F32)
-    other = partial[2 * n : 3 * n].astype(F32) + far
-    mine = partial[:n].astype(F32) + near
-    return mine + swap(other.astype(BF), "yl").astype(F32)
-
-
-def contract_last(left, right):
-    return lax.dot_general(left, right, (((1,), (1,)), ((), ())), preferred_element_type=F32)
-
-
-def contract_first(left, right):
-    return lax.dot_general(left, right, (((0,), (0,)), ((), ())), preferred_element_type=F32)
-
-
-def columns_of(rows, axis, index):
-    t, d = rows.shape
-    blocks = rows.reshape(t, 4, 4, d // 16)
-    return pick(blocks, index, {"z": 1, "x": 2}[axis]).reshape(t, d // 4)
+    own, near, other = scatter_cores(partial)
+    return [own, near, swap(other, "yl")]
+
+
+def total(first, parts):
+    for part in parts:
+        first = first + part.astype(F32)
+    return first
 
 
 def exchange_sum(parts, axis, hold=()):
@@ -114,13 +120,6 @@
     return exchange_sum([pick(half, place("yh"), 0), pick(half, place("yh", 1), 0)], "yh", hold)
 
 
-def wide_parts(left, right, axis):
-    return [
-        contract_first(columns_of(left, axis, place(axis, d)), right).astype(BF)
-        for d in range(lax.axis_size(axis))
-    ]
-
-
 def wide_sum_next(part, axis, hold=()):
     n = lax.axis_size(axis)
     part = part.reshape(n, part.shape[0] // n, part.shape[1])
@@ -150,12 +149,12 @@
             scaled_ref[rows : rows + 32, :] = (normed * gain).astype(BF)
 
 
-def project_kernel(*refs):
+def project_kernel(skip, *refs):
     piece_refs, (w_ref, last_ref, cos_ref, sin_ref, q_ref, kv_ref, scaled_ref, gains_ref) = refs[:4], refs[4:]
     width_q = q_ref.shape[0]
     half = HD // 2
     cos, sin = cos_ref[...], sin_ref[...]
-    tiles = [(w, at) for w in (w_ref, last_ref) for at in range(0, w.shape[1], 128)]
+    tiles = [(w, at) for w in (w_ref, last_ref) for at in range(skip, w.shape[1], 128)]
 
     def turned(block):
         a, b = block[:half], block[half:]
@@ -199,17 +198,21 @@
     dup_ref[...] = (grad * gated).astype(BF)
 
 
-def rows_grad_kernel(count, gain_row, *refs):
-    grads, weights, pieces = refs[:count], refs[count : 2 * count], refs[2 * count : 2 * count + 4]
-    gain_ref, out_ref, sum_ref = refs[2 * count + 4 :]
+def sum_of_products(terms, refs):
+    total = None
+    for left, (low, high), right, (first, last) in terms:
+        part = mm_last(refs[left][:, low:high], refs[right][:, first:last])
+        total = part if total is None else total + part
+    return total
+
+
+def rows_grad_kernel(terms, count, gain_row, *refs):
+    pieces = refs[count : count + 4]
+    gain_ref, out_ref, sum_ref = refs[count + 4 :]
     step = pl.program_id(0)
-    tile = weights[0].shape[0]
-    total = None
-    for g_ref, w_ref in zip(grads, weights):
-        part = mm_last(g_ref[...], w_ref[...])
-        total = part if total is None else total + part
+    tile = sum_ref.shape[1] // pl.num_programs(0)
     columns = pl.ds(pl.multiple_of(step * tile, tile), tile)
-    sum_ref[:, columns] = total * gain_ref[gain_row : gain_row + 1, columns]
+    sum_ref[:, columns] = sum_of_products(terms, refs) * gain_ref[gain_row : gain_row + 1, columns]
 
     @pl.when(step == pl.num_programs(0) - 1)
     def _():
@@ -220,6 +223,68 @@
                 scaled = sum_ref[rows, :]
                 inner = jnp.mean(scaled * normed, -1, keepdims=True)
                 out_ref[rows, :] = (factor * (scaled - normed * inner)).astype(BF)
+
+
+def rows_out_kernel(terms, *refs):
+    refs[-1][...] = sum_of_products(terms, refs).astype(BF)
+
+
+def write_parts(outs, turned_of, axis, me, right, base):
+    for d, out in enumerate(outs):
+        index = (me + d) & 3
+        if axis == "z":
+            turned = turned_of(pl.multiple_of(index * 512, 512), 512)
+        else:
+            turned = jnp.concatenate(
+                [turned_of(pl.multiple_of(z * 512 + index * 128, 128), 128) for z in range(4)], 0
+            )
+        out[:, base : base + right.shape[1]] = mm(turned, right).astype(BF)
+
+
+def parts_kernel(axis, columns, count, me_ref, *refs):
+    lefts, right_ref, outs = refs[:count], refs[count], refs[count + 1 :]
+
+    def turned_of(at, size):
+        return jnp.concatenate([left[:, pl.ds(at, size)] for left in lefts], 0).T
+
+    write_parts(outs, turned_of, axis, me_ref[0, 0], right_ref[:, columns[0] : columns[1]], 0)
+
+
+def last_parts_kernel(axis, cut, me_ref, left_ref, dq_ref, own_ref, one_ref, two_ref, three_ref,
+                      cos_ref, sin_ref, *outs):
+    half = HD // 2
+    cos, sin = cos_ref[...], sin_ref[...]
+    kv = own_ref[...]
+    for ref in (one_ref, two_ref, three_ref):
+        kv = kv + ref[...].astype(F32)
+    kv = kv.T
+    a, b = kv[:half], kv[half:HD]
+    kv = jnp.concatenate([a * cos + b * sin, b * cos - a * sin, kv[HD:]], 0).T.astype(BF)
+    outs[0][...] = kv
+    right = jnp.concatenate([dq_ref[:, cut:], kv], 1)
+
+    def turned_of(at, size):
+        return left_ref[:, pl.ds(at, size)].T
+
+    write_parts(outs[1:], turned_of, axis, me_ref[0, 0], right, 0)
+
+
+def settle_kernel(base_ref, *refs):
+    out_ref = refs[-1]
+    width = base_ref.shape[1]
+
+    def block(at):
+        value = base_ref[:, at : at + 128].astype(F32)
+        for ref in refs[:-1]:
+            value = value + ref[:, at : at + 128].astype(F32)
+        return value
+
+    for n in range(width // 256):
+        one, two = block(256 * n), block(256 * n + 128)
+        low = jnp.concatenate([one[:, :HD], two[:, :HD]], 1)
+        high = jnp.concatenate([one[:, HD:], two[:, HD:]], 1)
+        out_ref[:, 128 * n : 128 * n + 128] = low.astype(out_ref.dtype)
+        out_ref[:, width // 2 + 128 * n : width // 2 + 128 * n + 128] = high.astype(out_ref.dtype)
 
 
 def fill_bias(bias_ref, me_ref, pos_ref, span, distances):
@@ -288,7 +353,7 @@
     kv_refs = take(blocks)
     me_ref, pos_ref, lse_ref = take(3)
     if first:
-        mix_ref, grad_ref = take(2)
+        mix_ref, wa_ref, wb_ref, *piece_refs = take(7)
     else:
         gt_ref, delta_ref, part_ref = take(3)
     if last:
@@ -312,8 +377,11 @@
     dk_ref[...] = jnp.zeros_like(dk_ref)
     dv_ref[...] = jnp.zeros_like(dv_ref)
     if first:
+        rows_all = jnp.concatenate([ref[...] for ref in piece_refs], 0)
+        grads = [mm(rows_all, w_ref[:, : heads * HD // 2]).astype(BF) for w_ref in (wa_ref, wb_ref)]
         for at in range(0, heads * HD, 128):
-            gt = grad_ref[:, at : at + 128].T
+            where = at % (heads * HD // 2)
+            gt = grads[2 * at // (heads * HD)][:, where : where + 128].T
             mt = mix_ref[:, at : at + 128].T
             gt_ref[at : at + 128, :] = gt
             prod = gt.astype(F32) * mt.astype(F32)
@@ -355,15 +423,15 @@
         dkv_ref[rows, :] = jnp.concatenate([dk_ref[rows, :], dv_ref[rows, :]], 1).astype(dkv_ref.dtype)
 
 
-def weight_grads_kernel(left_ref, *refs):
-    out_ref = refs[-1]
-    turned = left_ref[...].T
+def weight_grads_kernel(left_ref, one_ref, two_ref, other_left_ref, other_ref, out_ref):
     at = 0
-    for ref in refs[:-1]:
-        for c in range(0, ref.shape[1], 256):
-            size = min(256, ref.shape[1] - c)
-            out_ref[:, at + c : at + c + size] = mm(turned, ref[:, c : c + size]).astype(BF)
-        at += ref.shape[1]
+    for lefts, rights in ((left_ref, (one_ref, two_ref)), (other_left_ref, (other_ref,))):
+        turned = lefts[...].T
+        for ref in rights:
+            for c in range(0, ref.shape[1], 256):
+                size = min(256, ref.shape[1] - c)
+                out_ref[:, at + c : at + c + size] = mm(turned, ref[:, c : c + size]).astype(BF)
+            at += ref.shape[1]
 
 
 def params():
@@ -378,10 +446,10 @@
     return pl.CostEstimate(flops=2 * products, bytes_accessed=moved, transcendentals=0)
 
 
-def project(pieces, w, last, cos, sin, width_q):
+def project(pieces, w, last, skip, cos, sin, width_q):
     span, d = 4 * pieces[0].shape[0], pieces[0].shape[1]
     return pl.pallas_call(
-        project_kernel,
+        functools.partial(project_kernel, skip),
         out_shape=(
             jax.ShapeDtypeStruct((width_q, span), BF),
             jax.ShapeDtypeStruct((span, 2 * HD), BF),
@@ -401,9 +469,6 @@
     tile = 128
     tiles = width // tile
 
-    def fixed(array):
-        return pl.BlockSpec(array.shape, lambda i: (0, 0))
-
     def columns(base):
         return pl.BlockSpec((d, tile), lambda i: (0, i + base))
 
@@ -422,29 +487,104 @@
     )(*pieces, *cots, gains, weights, weights, weights)
 
 
-def rows_grad(grads, weights, pieces, gains, gain_row):
+def feature_rows(weight, tile):
+    if not isinstance(weight, tuple):
+        return pl.BlockSpec((tile, weight.shape[1]), lambda i: (i, 0))
+    return pl.BlockSpec((tile, weight[2]), lambda i: (i, weight[1]))
+
+
+def array_of(weight):
+    return weight[0] if isinstance(weight, tuple) else weight
+
+
+def fixed(array):
+    return pl.BlockSpec(array.shape, lambda i: (0, 0))
+
+
+def rows_grad(grads, weights, terms, pieces, gains, gain_row):
     span, d = 4 * pieces[0].shape[0], pieces[0].shape[1]
     tile = 256
-
-    def fixed(array):
-        return pl.BlockSpec(array.shape, lambda i: (0, 0))
-
-    def rows(grad, index):
-        return pl.BlockSpec((tile, grad.shape[1]), lambda i: (i, index))
-
-    return pl.pallas_call(
-        functools.partial(rows_grad_kernel, len(grads), gain_row),
+    n = len(grads)
+    terms = [(g, c, n + w, e) for g, c, w, e in terms]
+    return pl.pallas_call(
+        functools.partial(rows_grad_kernel, terms, n + len(weights), gain_row),
         grid=(d // tile,),
         out_shape=jax.ShapeDtypeStruct((span, d), BF),
         in_specs=[fixed(g) for g in grads]
-        + [rows(g, w[1]) for g, w in zip(grads, weights)]
+        + [feature_rows(w, tile) for w in weights]
         + [fixed(a) for a in (*pieces, gains)],
         out_specs=pl.BlockSpec((span, d), lambda i: (0, 0)),
         scratch_shapes=[pltpu.VMEM((span, d), F32)],
         compiler_params=params(),
-        cost_estimate=cost(sum(span * d * g.shape[1] for g in grads), 8 << 20),
+        cost_estimate=cost(sum(span * d * (c[1] - c[0]) for _, c, _, _ in terms), 8 << 20),
         name="rows_grad",
-    )(*grads, *[w[0] for w in weights], *pieces, gains)
+    )(*grads, *map(array_of, weights), *pieces, gains)
+
+
+def rows_out(lefts, weights, terms):
+    span, d = lefts[0].shape[0], array_of(weights[0]).shape[0]
+    tile = 256
+    n = len(lefts)
+    terms = [(g, c, n + w, e) for g, c, w, e in terms]
+    return pl.pallas_call(
+        functools.partial(rows_out_kernel, terms),
+        grid=(d // tile,),
+        out_shape=jax.ShapeDtypeStruct((span, d), BF),
+        in_specs=[fixed(g) for g in lefts] + [feature_rows(w, tile) for w in weights],
+        out_specs=pl.BlockSpec((span, tile), lambda i: (0, i)),
+        compiler_params=params(),
+        cost_estimate=cost(sum(span * d * (c[1] - c[0]) for _, c, _, _ in terms), 6 << 20),
+        name="rows_out",
+    )(*lefts, *map(array_of, weights))
+
+
+def scalar():
+    return [pl.BlockSpec(memory_space=pltpu.SMEM)]
+
+
+def at_place(axis):
+    return place(axis).astype(jnp.int32).reshape(1, 1)
+
+
+def wide_parts(lefts, right, columns, axis):
+    span, d = right.shape[0], lefts[0].shape[1]
+    width = columns[1] - columns[0]
+    return pl.pallas_call(
+        functools.partial(parts_kernel, axis, columns, len(lefts)),
+        out_shape=(jax.ShapeDtypeStruct((d // 4, width), BF),) * 4,
+        in_specs=scalar() + whole(len(lefts) + 1),
+        out_specs=tuple(whole(4)),
+        compiler_params=params(),
+        cost_estimate=cost(span * d * width, 8 << 20),
+        name="wide_parts",
+    )(at_place(axis), *lefts, right)
+
+
+def last_parts(left, dq, cut, own, arrived, cos, sin, axis):
+    span, d = left.shape
+    width = dq.shape[1] - cut + 2 * HD
+    return pl.pallas_call(
+        functools.partial(last_parts_kernel, axis, cut),
+        out_shape=(jax.ShapeDtypeStruct((span, 2 * HD), BF),)
+        + (jax.ShapeDtypeStruct((d // 4, width), BF),) * 4,
+        in_specs=scalar() + whole(8),
+        out_specs=tuple(whole(5)),
+        compiler_params=params(),
+        cost_estimate=cost(span * d * width, 8 << 20),
+        name="last_parts",
+    )(at_place(axis), left, dq, own, *arrived, cos, sin)
+
+
+def settle(base, parts, kind):
+    return pl.pallas_call(
+        settle_kernel,
+        out_shape=jax.ShapeDtypeStruct(base.shape, kind),
+        in_specs=whole(1 + len(parts)),
+        out_specs=whole(1)[0],
+        compiler_params=params(),
+        cost_estimate=cost(0, 4 << 20),
+        name="settle",
+    )(base, *parts)
 
 
 def window_specs():
@@ -474,13 +614,13 @@
     )(q, *kvs, *window)
 
 
-def attend_back(distances, q, kvs, window, lse, prepared, mixed=None, grad=None, turn=None):
+def attend_back(distances, q, kvs, window, lse, prepared, mixed=None, out=None, turn=None):
     n = len(kvs)
     width, span = q.shape
     heads = width // HD
     first, last = prepared is None, turn is not None
     operands = [q, *kvs, *window, lse]
-    operands += [mixed, grad] if first else list(prepared)
+    operands += [mixed, *out] if first else list(prepared)
     shapes = []
     if last:
         operands += turn
@@ -509,21 +649,21 @@
     )(*operands)
 
 
-def weight_grads(left, *rights):
+def weight_grads(left, one, two, other_left, other):
     t, d = left.shape
     tile = 256
-    width = sum(right.shape[1] for right in rights)
+    rows = pl.BlockSpec((t, tile), lambda i: (0, i))
+    width = one.shape[1] + two.shape[1] + other.shape[1]
     return pl.pallas_call(
         weight_grads_kernel,
         grid=(d // tile,),
         out_shape=jax.ShapeDtypeStruct((d, width), BF),
-        in_specs=[pl.BlockSpec((t, tile), lambda i: (0, i))]
-        + [pl.BlockSpec(right.shape, lambda i: (0, 0)) for right in rights],
+        in_specs=[rows, fixed(one), fixed(two), rows, fixed(other)],
         out_specs=pl.BlockSpec((tile, width), lambda i: (i, 0)),
         compiler_params=params(),
         cost_estimate=cost(t * d * width, 2 * d * width + 4 * t * d),
         name="weight_grads",
-    )(left, *rights)
+    )(left, one, two, other_left, other)
 
 
 def per_device(
@@ -546,30 +686,31 @@
     span = positions.shape[0]
     quarter = span // 4
     cut = 3 * width_q // 4
+    skip = width_q // 2
 
     inputs = to_inner(inputs)
     cotangent = to_inner(cotangent)
 
     pad = jnp.zeros((attn_gain.shape[0], 126), BF)
-    shard_a = query_weight[:, :cut]
+    out_turned = out_weight.T
+    shard_a = jnp.concatenate([out_turned[:, :skip], query_weight[:, :cut]], 1)
     shard_b = jnp.concatenate(
-        [query_weight[:, cut:], key_weight, value_weight, attn_gain[:, None], mlp_gain[:, None], pad], 1
+        [out_turned[:, skip:], query_weight[:, cut:], key_weight, value_weight,
+         attn_gain[:, None], mlp_gain[:, None], pad], 1
     )
     width_b = width_q - cut + 2 * width_k
     shard_mlp = jnp.concatenate([gate_weight, up_weight, down_weight.T], 1)
     other_a, other_b = swap(shard_a, "yh"), swap(shard_b, "yh")
     other_mlp = swap(shard_mlp, "yh")
     rows_in = gather_rows(inputs)
-
-    part_b = gather_stage(join_sides(shard_b, other_b), "x", 0)
-    part_a = gather_stage(join_sides(shard_a, other_a), "z", 0)
-    out_turned = after(out_weight.T, part_a, part_b)
-    other_out = swap(out_turned, "yh")
-    mlp_pair = join_sides(shard_mlp, after(other_mlp, other_out))
+    along_b = send_stage(join_sides(shard_b, other_b), "x")
+    along_a = send_stage(join_sides(shard_a, other_a), "z")
+    mlp_pair = join_sides(shard_mlp, after(other_mlp, along_a[1:], along_b[1:]))
     mlp_whole = lax.all_gather(mlp_pair, ("z", "x"), axis=0, tiled=True)
-    whole_b = flat(gather_stage(part_b, "z", 0))
-    whole_a = flat(gather_stage(part_a, "x", 1))
-    pair_out = join_sides(out_turned, other_out)
+    part_b = stack_stage(along_b, "x", 0)
+    part_a = stack_stage(along_a, "z", 0)
+    whole_b = flat(gather_ring(part_b, "z", 0))
+    whole_a = flat(gather_ring(part_a, "x", 1))
 
     me = (lax.axis_index("yl") * 2 + lax.axis_index("core")).astype(jnp.int32)
     blocked = jnp.arange(4, dtype=jnp.int32) ^ me
@@ -579,75 +720,83 @@
     cos, sin = jnp.cos(angles), jnp.sin(angles)
     window = (me.reshape(1, 1), positions)
 
-    queries, kv_block, scaled_in, gains = project(rows_in, whole_a, whole_b, cos, sin, width_q)
+    queries, kv_block, scaled_in, gains = project(
+        rows_in, whole_a, whole_b, skip, cos, sin, width_q
+    )
     blocks = [kv_block] + [shift(kv_block, "x", d) for d in range(1, SEQ_DEVS)]
-    part_out = gather_stage(pair_out, "x", 0, hold=[kv_block])
     cotangents = gather_rows(after(cotangent, kv_block))
     mixed, log_total = attend(queries, blocks, window)
-    out_whole = flat(gather_stage(part_out, "z", 0, hold=[log_total]))
-
-    middle = inputs.astype(F32) + scatter_rows(contract_last(mixed, out_whole))
+
+    attn_rows = rows_out(
+        [mixed], [whole_a, whole_b],
+        [(0, (0, skip), 0, (0, skip)), (0, (skip, width_q), 1, (0, skip))],
+    )
+    middle = total(inputs.astype(F32), scatter_rows(attn_rows))
     rows_mid = gather_rows(middle.astype(BF))
     hidden, grad_gate, grad_up, scaled_mid, cotangent_all = hidden_units(
         rows_mid, cotangents, gains, mlp_whole, hidden_width
     )
+    every = (0, hidden_width)
     mid_partial = rows_grad(
-        [grad_gate, grad_up], [(mlp_whole, 0), (mlp_whole, 1)], rows_mid, gains, 1
-    )
-    mid_part = scatter_rows(mid_partial)
-    grad_middle = cotangent.astype(F32) + mid_part
-    grad_middle_all = jnp.concatenate(gather_rows(grad_middle.astype(BF)), 0)
-
-    gate_up_sum = weight_grads(after(scaled_mid, mid_partial), grad_gate, grad_up)
-    gate_up_sum = lax.psum_scatter(gate_up_sum, ("z", "x"), scatter_dimension=0, tiled=True)
-    down_parts = wide_parts(after(cotangent_all, mid_partial), hidden, "z")
-    mlp_partial = contract_last(after(hidden, down_parts), mlp_whole[:, 2 * hidden_width :])
-
-    grad_mixed = jnp.dot(grad_middle_all, out_whole, preferred_element_type=F32).astype(BF)
-    out_parts = wide_parts(grad_middle_all, mixed, "x")
-    down_sum = exchange_sum(down_parts, "z", hold=[grad_middle_all]).astype(BF)
+        [grad_gate, grad_up],
+        [(mlp_whole, 0, hidden_width), (mlp_whole, 1, hidden_width)],
+        [(0, every, 0, every), (1, every, 1, every)],
+        rows_mid, gains, 1,
+    )
+    grad_middle = total(cotangent.astype(F32), scatter_rows(mid_partial))
+    rows_grad_middle = gather_rows(grad_middle.astype(BF))
+
+    mlp_sum = weight_grads(
+        after(scaled_mid, mid_partial), grad_gate, grad_up, cotangent_all, hidden
+    )
+    mlp_rows = rows_out(
+        [after(hidden, mlp_sum)], [(mlp_whole, 2, hidden_width)], [(0, every, 0, every)]
+    )
+    mlp_sum = lax.psum_scatter(mlp_sum, ("z", "x"), scatter_dimension=0, tiled=True)
+
+    out_parts = wide_parts(rows_grad_middle, mixed, (0, width_q), "z")
+    mlp_own, mlp_near, mlp_other = scatter_cores(mlp_rows)
     query_part, far_grads, grad_turned, delta = attend_back(
-        (1, 2, 3), queries, blocks[1:], window, log_total, None, mixed, after(grad_mixed, out_parts)
-    )
-    mlp_rows = scatter_rows(after(mlp_partial, grad_middle_all))
-    output = (middle + mlp_rows).astype(BF)
+        (1, 2, 3), queries, blocks[1:], window, log_total, None, after(mixed, out_parts, mlp_other),
+        [whole_a, whole_b, *rows_grad_middle],
+    )
+    mlp_across = swap(after(mlp_other, rows_grad_middle), "yl")
+    output = settle(middle, [mlp_own, mlp_near, after(mlp_across, query_part)], BF)
     arriving = [
         shift(far_grads[(d - 1) * span : d * span], "x", -d) for d in range(1, SEQ_DEVS)
     ]
-    out_sum = exchange_sum(out_parts, "x", hold=[query_part]).astype(BF)
-    down_sum = wide_sum_next(down_sum, "x", hold=[query_part])
-    query_raw_grad, carried = attend_back(
-        (0,), queries, blocks[:1], window, log_total, (grad_turned, delta, query_part), turn=[cos, sin]
-    )
-    out_sum = wide_sum_next(out_sum, "z", hold=[query_raw_grad])
-    outer = jnp.concatenate([down_sum, out_sum], 1)
-    for piece in arriving:
-        carried = carried + piece.astype(F32)
-
-    a_sum = exchange_sum(wide_parts(scaled_in, query_raw_grad[:, :cut], "x"), "x").astype(BF)
-    turned = carried[:, :width_k]
-    first, second = turned[:, : HD // 2], turned[:, HD // 2 :]
-    key_raw_grad = jnp.concatenate(
-        [first * cos.T + second * sin.T, second * cos.T - first * sin.T], 1
-    ).astype(BF)
-    grad_b = jnp.concatenate(
-        [query_raw_grad[:, cut:], key_raw_grad, carried[:, width_k:].astype(BF)], 1
-    )
-    in_part = scatter_rows(
-        rows_grad([query_raw_grad[:, :cut], grad_b], [(whole_a, 0), (whole_b, 0)], rows_in, gains, 0)
-    )
-    input_grad = grad_middle + in_part
-    b_sum = exchange_sum(wide_parts(scaled_in, grad_b, "z"), "z").astype(BF)
-    a_sum, b_sum = wide_sum_next(a_sum, "z"), wide_sum_next(b_sum, "x")
+    out_sum = exchange_sum(out_parts, "z", hold=[query_part]).astype(BF)
+    query_raw_grad, own_grads = attend_back(
+        (0,), after(queries, out_sum, output), blocks[:1], window, log_total, (grad_turned, delta, query_part), turn=[cos, sin]
+    )
+
+    a_parts = wide_parts([scaled_in], query_raw_grad, (0, cut), "x")
+    kv_raw_grad, *b_parts = last_parts(
+        scaled_in, after(query_raw_grad, a_parts), cut, own_grads, arriving, cos, sin, "z"
+    )
+    in_partial = rows_grad(
+        [query_raw_grad, kv_raw_grad],
+        [whole_a, whole_b],
+        [
+            (0, (0, cut), 0, (skip, skip + cut)),
+            (0, (cut, width_q), 1, (skip, skip + width_q - cut)),
+            (1, (0, 2 * width_k), 1, (skip + width_q - cut, skip + width_b)),
+        ],
+        rows_in, gains, 0,
+    )
+    input_grad = settle(grad_middle, scatter_rows(in_partial), F32)
+    a_sum = wide_sum_next(exchange_sum(a_parts, "x").astype(BF), "z")
+    b_sum = exchange_sum(b_parts, "z").astype(BF)
+    b_sum = wide_sum_next(jnp.concatenate([b_sum, out_sum], 1), "x")
     attn_sum = sides_sum(jnp.concatenate([a_sum, b_sum], 1))
-    a_grad, b_grad = attn_sum[:, :cut], attn_sum[:, cut:]
-    outer_grad = sides_sum(outer, hold=[b_sum]).T
-    down_grad, out_grad = outer_grad[:hidden_width], outer_grad[hidden_width:]
-    mlp_grad = sides_sum(after(gate_up_sum, query_raw_grad))
-    gate_grad, up_grad = mlp_grad[:, :hidden_width], mlp_grad[:, hidden_width:]
-
-    attn_gain_part = jnp.sum(shard_a.astype(F32) * a_grad, 1) + jnp.sum(
-        shard_b[:, :width_b].astype(F32) * b_grad, 1
+    a_grad, b_grad = attn_sum[:, :cut], attn_sum[:, cut : cut + width_b]
+    out_grad = attn_sum[:, cut + width_b :].T
+    mlp_grad = sides_sum(after(mlp_sum, query_raw_grad))
+    gate_grad, up_grad = mlp_grad[:, :hidden_width], mlp_grad[:, hidden_width : 2 * hidden_width]
+    down_grad = mlp_grad[:, 2 * hidden_width :].T
+
+    attn_gain_part = jnp.sum(shard_a[:, skip:].astype(F32) * a_grad, 1) + jnp.sum(
+        shard_b[:, skip : skip + width_b].astype(F32) * b_grad, 1
     )
     mlp_gain_part = jnp.sum(
         gate_weight.astype(F32) * gate_grad + up_weight.astype(F32) * up_grad, 1
@@ -655,8 +804,8 @@
     attn_gain_grad, mlp_gain_grad = lax.psum((attn_gain_part, mlp_gain_part), TP)
     own = width_q - cut
     return (
-        from_inner(output),
-        from_inner(input_grad),
+        output,
+        input_grad,
         attn_gain_grad / attn_gain.astype(F32),
         jnp.concatenate([a_grad, b_grad[:, :own]], 1),
         b_grad[:, own : own + width_k],

time: 552 us -> 459 us (0.83)
  local copies, waits for them, and re-layouts: 90.7 us -> 28.7 us
  Pallas kernels: 113 us -> 155 us
  starting transfers between devices: 126 us -> 90 us
  matrix products: 31.9 us -> 0 us
  other arithmetic: 28.2 us -> 15.9 us
  waiting for transfers between devices: 129 us -> 135 us
    ppermute x79 -> x64, starting transfers between devices: 126 us -> 90 us  [shift(): lax.ppermute(block, axis, [(i, (i + distance) % n) for i in range(n)])]
    pallas_call x3 -> x10, Pallas kernels: 32.2 us -> 67.9 us  [the longest x2 25.2 us: rows_grad(): pl.pallas_call(functools.partial(rows_grad_kernel, terms, n + len(weights...]
    dot_general x19 -> x0, matrix products: 31.9 us -> none  [the longest x16 21 us: contract_first(): lax.dot_general(left, right, (((0,), (0,)), ((), ())), preferred_element_...]
    unnamed x192 -> x92, local copies, waits for them, and re-layouts: 37.6 us -> 8.62 us
    dynamic_slice x3 -> x0, local copies, waits for them, and re-layouts: 15.8 us -> none  [pick(): return lax.dynamic_index_in_dim(array, index, dim, keepdims=False)]
    reshape x3 -> x0, local copies, waits for them, and re-layouts: 11.1 us -> none  [columns_of(): blocks = rows.reshape(t, 4, 4, d // 16)]
    ppermute x79 -> x64, waiting for transfers between devices: 129 us -> 135 us  [shift(): lax.ppermute(block, axis, [(i, (i + distance) % n) for i in range(n)])]
  transfers between devices with their start and end apart: 81 -> 66, of which waited for: 26 -> 29; matrix products, arithmetic and copies ran while one was open for 25% -> 7% of each run, Pallas kernels for 12% -> 23%
where the time goes in v2:
time: 459 us; the launch traced here: 450 us
  Pallas kernels  155 us (34%)
  waiting for transfers between devices  135 us (29%)
  starting transfers between devices  90 us (20%)
  local copies, waits for them, and re-layouts  28.7 us (6%)
  other arithmetic  15.9 us (3%)
  between operations  15.4 us (3%)
  blocking collectives  9.68 us (2%)
    ppermute x64, waiting for transfers between devices, shift(): lax.ppermute(block, axis, [(i, (i + distance) % n) for i in range(n)])  135 us
    ppermute x64, starting transfers between devices, shift(): lax.ppermute(block, axis, [(i, (i + distance) % n) for i in range(n)])  90 us
    pallas_call x2, Pallas kernels, attend_back(): pl.pallas_call(functools.partial(attend_back_kernel, distances, first, la...  33.3 us
    pallas_call x2, Pallas kernels, rows_grad(): pl.pallas_call(functools.partial(rows_grad_kernel, terms, n + len(weights...  25.2 us
    pallas_call x1, Pallas kernels, hidden_units(): pl.pallas_call(hidden_kernel, grid=(tiles,), out_shape=(jax.ShapeDtypeStr...  20.1 us
    pallas_call x1, Pallas kernels, attend(): pl.pallas_call(attend_kernel, out_shape=(jax.ShapeDtypeStruct((span, widt...  18.4 us
    pallas_call x2, Pallas kernels, rows_out(): pl.pallas_call(functools.partial(rows_out_kernel, terms), grid=(d // tile...  16.9 us
    pallas_call x1, Pallas kernels, weight_grads(): pl.pallas_call(weight_grads_kernel, grid=(d // tile,), out_shape=jax.Shap...  15.3 us
  transfers between devices with their start and end apart: 66, of which 29 were waited for; matrix products, arithmetic and copies ran while one was open for 7% of the time, Pallas kernels for 23%

profile of v2, /device:TPU:1, one launch (start us, length us, event | category | flops | bytes accessed | tf_op | source)
XLA Modules:
  0.0 450.0 jit_solution(185494112600950497)
XLA Ops:
  9.0 3.8 collective-permute-start.3
  17.1 3.0 collective-permute-start.31
  21.9 2.2 collective-permute-start.5
  27.1 2.5 collective-permute-start.13
  31.8 1.7 collective-permute-done.13
  33.5 2.9 collective-permute-done.14
  40.8 2.7 collective-permute-start.8
  43.6 2.7 collective-permute-start.16
  47.1 1.9 collective-permute-done.1.refs_2_.refs_6_
  49.1 3.9 collective-permute-start
  52.9 4.0 collective-permute-done.8
  56.9 12.5 %collective-permute-start.2 = (bf16[128,2048]{1,0:T(8,128)(2,1)}, bf16[128,2048]{1,0:T(8,128)(2,1)}, u32[]{:S(2)}, u32[]{:S(2)}) collective-permute-start(bf16[128,2048]{1,0:T(8,128)(2,1)} %collective-permute-done.1.refs_2_.refs_6_), channel_id=1, source_target_pairs={{0,1},{1,0},{2,3},{3,2},{4,5},{5,4},{6,7},{7,6},{8,9},{9,8},{10,11... | collective-permute-start | bytes 1572872 | tf_op jit(solution)/shard_map/ppermute | solution.py:30
  69.4 3.5 collective-permute-start.10
  73.5 8.8 %collective-permute-done.10 = bf16[2,128,640]{2,1,0:T(8,128)(2,1)S(1)} collective-permute-done((bf16[2,128,640]{2,1,0:T(8,128)(2,1)S(1)}, bf16[2,128,640]{2,1,0:T(8,128)(2,1)S(1)}, u32[]{:S(2)}, u32[]{:S(2)}) %collective-permute-start.10) | collective-permute-done | bytes 327712 | tf_op jit(solution)/shard_map/ppermute | solution.py:30
  83.9 9.1 %collective-permute-done.17 = bf16[2,128,640]{2,1,0:T(8,128)(2,1)S(1)} collective-permute-done((bf16[2,128,640]{2,1,0:T(8,128)(2,1)S(1)}, bf16[2,128,640]{2,1,0:T(8,128)(2,1)S(1)}, u32[]{:S(2)}, u32[]{:S(2)}) %collective-permute-start.17) | collective-permute-done | bytes 327712 | tf_op jit(solution)/shard_map/ppermute | solution.py:30
  94.7 8.2 %project.1 = (bf16[512,512]{1,0:T(8,128)(2,1)}, bf16[512,128]{1,0:T(8,128)(2,1)}, bf16[512,2048]{1,0:T(8,128)(2,1)}, f32[8,2048]{1,0:T(8,128)}) custom-call(bf16[128,2048]{1,0:T(8,128)(2,1)} %copy-done.4, bf16[128,2048]{1,0:T(8,128)(2,1)} %copy-done.16, bf16[128,2048]{1,0:T(8,128)(2,1)} %collective-permute-done.1.refs_2_.refs_6_, ...), custom_call_target="tpu_custom_call" | custom-call | flops 1342177280 | bytes 8388608 | tf_op jit(solution)/shard_map/project/pallas_call | solution.py:451
  103.0 5.6 %collective-permute-start.20 = (bf16[512,128]{1,0:T(8,128)(2,1)}, bf16[512,128]{1,0:T(8,128)(2,1)S(1)}, u32[]{:S(2)}, u32[]{:S(2)}) collective-permute-start(bf16[512,128]{1,0:T(8,128)(2,1)} %get-tuple-element.55.refs_0_), channel_id=1, source_target_pairs={{0,8},{4,12},{8,0},{12,4},{1,9},{5,13},{9,1},{13,5},{2,10},{6,14},... | collective-permute-start | bytes 393224 | tf_op jit(solution)/shard_map/ppermute | solution.py:30
  108.6 4.8 %collective-permute-done.19.refs_1_.refs_0_ = bf16[512,128]{1,0:T(8,128)(2,1)S(1)} collective-permute-done((bf16[512,128]{1,0:T(8,128)(2,1)}, bf16[512,128]{1,0:T(8,128)(2,1)S(1)}, u32[]{:S(2)}, u32[]{:S(2)}) %collective-permute-start.19) | collective-permute-done | bytes 131104 | tf_op jit(solution)/shard_map/ppermute | solution.py:30
  113.3 6.6 %collective-permute-done.20.refs_2_.refs_1_ = bf16[512,128]{1,0:T(8,128)(2,1)S(1)} collective-permute-done((bf16[512,128]{1,0:T(8,128)(2,1)}, bf16[512,128]{1,0:T(8,128)(2,1)S(1)}, u32[]{:S(2)}, u32[]{:S(2)}) %collective-permute-start.20) | collective-permute-done | bytes 131104 | tf_op jit(solution)/shard_map/ppermute | solution.py:30
  120.6 18.4 %attend.1 = (bf16[512,512]{1,0:T(8,128)(2,1)}, f32[8,512]{1,0:T(8,128)}) custom-call(bf16[512,512]{1,0:T(8,128)(2,1)} %get-tuple-element.79.q_ref, bf16[512,128]{1,0:T(8,128)(2,1)} %get-tuple-element.55.refs_0_, bf16[512,128]{1,0:T(8,128)(2,1)} %copy-done.42, bf16[512,128]{1,0:T(8,128)(2,1)} %copy-done.43, bf16[512,128]{1,0:T(8,128)(2,1)} %copy-done.44, ...), custom_call_target="tpu_custom_call" | custom-call | flops 8589934592 | bytes 2097152 | tf_op jit(solution)/shard_map/attend/pallas_call | solution.py:598
  139.0 7.7 %rows_out.2 = bf16[512,2048]{1,0:T(8,128)(2,1)} custom-call(bf16[512,512]{1,0:T(8,128)(2,1)} %get-tuple-element.73.refs_0_.refs_4_.refs_6_, bf16[2048,640]{1,0:T(8,128)(2,1)} %bitcast.109, bf16[2048,640]{1,0:T(8,128)(2,1)} %bitcast.105), custom_call_target="tpu_custom_call" | custom-call | flops 1073741824 | bytes 6291456 | tf_op jit(solution)/shard_map/rows_out/pallas_call | solution.py:529
  146.7 2.2 fusion.15
  148.9 4.3 collective-permute-start.23
  153.2 2.2 collective-permute-done.23
  157.3 2.1 copy.43
  162.0 7.8 %collective-permute-done.24 = bf16[128,2048]{1,0:T(8,128)(2,1)} collective-permute-done((bf16[128,2048]{1,0:T(8,128)(2,1)}, bf16[128,2048]{1,0:T(8,128)(2,1)}, u32[]{:S(2)}, u32[]{:S(2)}) %collective-permute-start.24) | collective-permute-done | bytes 524320 | tf_op jit(solution)/shard_map/ppermute | solution.py:30
  169.8 2.5 fusion.11
  173.3 2.3 collective-permute-start.28
  175.6 5.4 %collective-permute-done.29.refs_6_ = bf16[128,2048]{1,0:T(8,128)(2,1)S(1)} collective-permute-done((bf16[128,2048]{1,0:T(8,128)(2,1)}, bf16[128,2048]{1,0:T(8,128)(2,1)S(1)}, u32[]{:S(2)}, u32[]{:S(2)}) %collective-permute-start.29) | collective-permute-done | bytes 524320 | tf_op jit(solution)/shard_map/ppermute | solution.py:30
  180.9 2.0 collective-permute-start.30
  182.9 9.2 %collective-permute-done.26.refs_2_.refs_6_ = bf16[128,2048]{1,0:T(8,128)(2,1)S(1)} collective-permute-done((bf16[128,2048]{1,0:T(8,128)(2,1)S(1)}, bf16[128,2048]{1,0:T(8,128)(2,1)S(1)}, u32[]{:S(2)}, u32[]{:S(2)}) %collective-permute-start.26) | collective-permute-done | bytes 524320 | tf_op jit(solution)/shard_map/ppermute | solution.py:30
  195.9 20.1 %hidden_units.1 = (bf16[512,1408]{1,0:T(8,128)(2,1)}, bf16[512,1408]{1,0:T(8,128)(2,1)}, bf16[512,1408]{1,0:T(8,128)(2,1)}, bf16[512,2048]{1,0:T(8,128)(2,1)}, bf16[512,2048]{1,0:T(8,128)(2,1)}) custom-call(bf16[128,2048]{1,0:T(8,128)(2,1)} %copy-done.9, bf16[128,2048]{1,0:T(8,128)(2,1)} %copy-done.13, bf16[128,2048]{1,0:T(8,128)(2,1)} %copy-done.12, ...), custom_call_target="tpu_custom_call" | custom-call | flops 8858370048 | bytes 17301504 | tf_op jit(solution)/shard_map/hidden_units/pallas_call | solution.py:476
  216.0 14.9 %rows_grad.2 = bf16[512,2048]{1,0:T(8,128)(2,1)} custom-call(bf16[512,1408]{1,0:T(8,128)(2,1)} %get-tuple-element.62.refs_0_.one_ref, bf16[512,1408]{1,0:T(8,128)(2,1)} %get-tuple-element.63.refs_1_.two_ref, bf16[2048,4224]{1,0:T(8,128)(2,1)} %all-gather.2.cloned.1.call-done.refs_9_.refs_10_.refs_11_.refs_2_.refs_3_.refs_1_, ...), custom_call_target="tpu_custom_call" | custom-call | flops 5905580032 | bytes 8388608 | tf_op jit(solution)/shard_map/rows_grad/pallas_call | solution.py:509
  230.9 15.3 %weight_grads.1 = bf16[2048,4224]{1,0:T(8,128)(2,1)} custom-call(bf16[512,2048]{1,0:T(8,128)(2,1)} %get-tuple-element.64.left_ref, bf16[512,1408]{1,0:T(8,128)(2,1)} %get-tuple-element.62.refs_0_.one_ref, bf16[512,1408]{1,0:T(8,128)(2,1)} %get-tuple-element.63.refs_1_.two_ref, bf16[512,2048]{1,0:T(8,128)(2,1)} %get-tuple-element.65.other_left_ref, ...), custom_call_target="tpu_custom_call" | custom-call | flops 8858370048 | bytes 21495808 | tf_op jit(solution)/shard_map/weight_grads/pallas_call | solution.py:657
  252.7 9.2 %rows_out.3 = bf16[512,2048]{1,0:T(8,128)(2,1)} custom-call(bf16[512,1408]{1,0:T(8,128)(2,1)} %get-tuple-element.66.other_ref.refs_0_, bf16[2048,4224]{1,0:T(8,128)(2,1)} %all-gather.2.cloned.1.call-done.refs_9_.refs_10_.refs_11_.refs_2_.refs_3_.refs_1_), custom_call_target="tpu_custom_call" | custom-call | flops 2952790016 | bytes 6291456 | tf_op jit(solution)/shard_map/rows_out/pallas_call | solution.py:529
  261.9 3.1 collective-permute-done.36
  265.0 2.7 fusion.10
  271.3 8.7 %collective-permute-done.38.refs_2_.refs_11_ = bf16[128,2048]{1,0:T(8,128)(2,1)} collective-permute-done((bf16[128,2048]{1,0:T(8,128)(2,1)S(1)}, bf16[128,2048]{1,0:T(8,128)(2,1)}, u32[]{:S(2)}, u32[]{:S(2)}) %collective-permute-start.38) | collective-permute-done | bytes 524320 | tf_op jit(solution)/shard_map/ppermute | solution.py:30
  280.0 2.1 collective-permute-start.39
  282.3 2.4 collective-permute-done.39.refs_3_.refs_12_
  285.7 4.1 wide_parts.2
  291.4 24.0 %attend_back.2 = (f32[512,512]{1,0:T(8,128)}, bf16[1536,128]{1,0:T(8,128)(2,1)}, bf16[512,512]{1,0:T(8,128)(2,1)}, f32[8,512]{1,0:T(8,128)}) custom-call(bf16[512,512]{1,0:T(8,128)(2,1)} %get-tuple-element.79.q_ref, bf16[512,128]{1,0:T(8,128)(2,1)} %copy-done.42, bf16[512,128]{1,0:T(8,128)(2,1)} %copy-done.43, bf16[512,128]{1,0:T(8,128)(2,1)} %copy-done.44, ...), custom_call_target="tpu_custom_call" | custom-call | flops 16106127360 | bytes 4194304 | tf_op jit(solution)/shard_map/attend_back/pallas_call | solution.py:634
  317.2 13.3 %collective-permute-done.42 = bf16[512,512]{1,0:T(8,128)(2,1)S(1)} collective-permute-done((bf16[512,512]{1,0:T(8,128)(2,1)}, bf16[512,512]{1,0:T(8,128)(2,1)S(1)}, u32[]{:S(2)}, u32[]{:S(2)}) %collective-permute-start.42) | collective-permute-done | bytes 524320 | tf_op jit(solution)/shard_map/ppermute | solution.py:30
  331.3 3.0 settle.2
  334.6 9.3 %attend_back.3 = (bf16[512,512]{1,0:T(8,128)(2,1)}, f32[512,128]{1,0:T(8,128)}) custom-call(bf16[512,512]{1,0:T(8,128)(2,1)} %get-tuple-element.79.q_ref, bf16[512,128]{1,0:T(8,128)(2,1)} %get-tuple-element.55.refs_0_, s32[1,1]{1,0:T(1,128)} %bitcast.31.refs_4_.refs_3_.refs_1_, s32[1,512]{1,0:T(1,128)} %bitcast.130, ...), custom_call_target="tpu_custom_call" | custom-call | flops 5368709120 | bytes 4194304 | tf_op jit(solution)/shard_map/attend_back/pallas_call | solution.py:634
  343.8 3.8 wide_parts.3
  347.8 2.4 collective-permute-start.51
  351.0 3.7 last_parts.1
  354.6 3.3 collective-permute-start.58
  359.6 10.3 %rows_grad.3 = bf16[512,2048]{1,0:T(8,128)(2,1)} custom-call(bf16[512,512]{1,0:T(8,128)(2,1)} %get-tuple-element.88.refs_1_.dq_ref.refs_0_, bf16[512,128]{1,0:T(8,128)(2,1)} %get-tuple-element.91.refs_1_, bf16[2048,640]{1,0:T(8,128)(2,1)} %bitcast.111, bf16[2048,640]{1,0:T(8,128)(2,1)} %bitcast.107, bf16[128,2048]{1,0:T(8,128)(2,1)} %copy-done.4, ...), custom_call_target="tpu_custom_call" | custom-call | flops 1342177280 | bytes 8388608 | tf_op jit(solution)/shard_map/rows_grad/pallas_call | solution.py:509
  370.0 2.6 fusion.12
  373.2 6.6 %collective-permute-done.57 = bf16[512,256]{1,0:T(8,128)(2,1)S(1)} collective-permute-done((bf16[512,256]{1,0:T(8,128)(2,1)}, bf16[512,256]{1,0:T(8,128)(2,1)S(1)}, u32[]{:S(2)}, u32[]{:S(2)}) %collective-permute-start.57) | collective-permute-done | bytes 262176 | tf_op jit(solution)/shard_map/ppermute | solution.py:30
  379.7 2.7 collective-permute-start.47
  382.7 2.1 collective-permute-start.61
  385.6 4.0 collective-permute-done.50
  389.9 4.2 collective-permute-done.61
  394.4 4.3 collective-permute-start.54
  400.4 4.1 collective-permute-done.53
  405.0 2.0 add_convert_fusion
  407.8 2.4 collective-permute-done.62
  413.5 5.1 %collective-permute-done.49.refs_2_ = bf16[128,2048]{1,0:T(8,128)(2,1)} collective-permute-done((bf16[128,2048]{1,0:T(8,128)(2,1)}, bf16[128,2048]{1,0:T(8,128)(2,1)}, u32[]{:S(2)}, u32[]{:S(2)}) %collective-permute-start.49) | collective-permute-done | bytes 524320 | tf_op jit(solution)/shard_map/ppermute | solution.py:30
  418.6 3.0 settle.3
  421.6 9.7 %collective-permute-done.63 = bf16[64,4224]{1,0:T(8,128)(2,1)S(1)} collective-permute-done((bf16[64,4224]{1,0:T(8,128)(2,1)S(1)}, bf16[64,4224]{1,0:T(8,128)(2,1)S(1)}, u32[]{:S(2)}, u32[]{:S(2)}) %collective-permute-start.63) | collective-permute-done | bytes 540704 | tf_op jit(solution)/shard_map/ppermute | solution.py:30
  432.6 9.7 %all-reduce = (f32[64]{0:T(128)S(1)}, f32[64]{0:T(128)S(1)}) all-reduce(f32[64]{0:T(128)S(1)} %add.202, f32[64]{0:T(128)S(1)} %get-tuple-element.99), channel_id=1, replica_groups=mesh['yh'=2,'z'=4,'x'=4,'yl'=2,'core'=2] {'yl','core'}, use_global_device_ids=true, to_apply=%region_2.3 | all-reduce | flops 128 | bytes 1024 | tf_op jit(solution)/shard_map/psum | solution.py:804
  (259 shorter events, 60.1 us)
Async XLA Ops:
  7.2 187.8 %all-gather.2.cloned.1.call-start = ((), (), s32[]{:S(2)}) async-start(), calls=%async_computation.1 | async-start | bytes 18382848 | tf_op jit(solution)/shard_map/all_gather | solution.py:709
  9.0 11.2 %collective-permute-start.3 = (bf16[64,640]{1,0:T(8,128)(2,1)S(1)}, bf16[64,640]{1,0:T(8,128)(2,1)S(1)}, u32[]{:S(2)}, u32[]{:S(2)}) collective-permute-start(bf16[64,640]{1,0:T(8,128)(2,1)S(1)} %pad_maximum_fusion.6), channel_id=1, source_target_pairs={{0,64},{64,0},{1,65},{65,1},{2,66},{66,2},{3,67},{67,3},{4,68},{68... | collective-permute-start | bytes 245768 | tf_op jit(solution)/shard_map/ppermute | solution.py:30
  15.9 9.5 %collective-permute-start.11 = (bf16[64,640]{1,0:T(8,128)(2,1)S(1)}, bf16[64,640]{1,0:T(8,128)(2,1)S(1)}, u32[]{:S(2)}, u32[]{:S(2)}) collective-permute-start(bf16[64,640]{1,0:T(8,128)(2,1)S(1)} %concatenate.39), channel_id=1, source_target_pairs={{0,64},{64,0},{1,65},{65,1},{2,66},{66,2},{3,67},{67,3},{4,68},{68... | collective-permute-start | bytes 245768 | tf_op jit(solution)/shard_map/ppermute | solution.py:30
  17.1 19.3 %collective-permute-start.31 = (bf16[64,4224]{1,0:T(8,128)(2,1)S(1)}, bf16[64,4224]{1,0:T(8,128)(2,1)S(1)}, u32[]{:S(2)}, u32[]{:S(2)}) collective-permute-start(bf16[64,4224]{1,0:T(8,128)(2,1)S(1)} %pad_maximum_fusion.2), channel_id=1, source_target_pairs={{0,64},{64,0},{1,65},{65,1},{2,66},{66,2},{3,67},{67,3},{4,68},{68... | collective-permute-start | bytes 1622024 | tf_op jit(solution)/shard_map/ppermute | solution.py:30
  20.2 6.8 %collective-permute-start.4 = (bf16[128,640]{1,0:T(8,128)(2,1)S(1)}, bf16[128,640]{1,0:T(8,128)(2,1)S(1)}, u32[]{:S(2)}, u32[]{:S(2)}) collective-permute-start(bf16[128,640]{1,0:T(8,128)(2,1)S(1)} %pad_maximum_fusion.4), channel_id=1, source_target_pairs={{0,16},{16,32},{32,48},{48,0},{1,17},{17,33},{33,49},{49,1},{2,18}... | collective-permute-start | bytes 491528 | tf_op jit(solution)/shard_map/ppermute | solution.py:30
  21.9 7.6 %collective-permute-start.5 = (bf16[128,640]{1,0:T(8,128)(2,1)S(1)}, bf16[128,640]{1,0:T(8,128)(2,1)S(1)}, u32[]{:S(2)}, u32[]{:S(2)}) collective-permute-start(bf16[128,640]{1,0:T(8,128)(2,1)S(1)} %pad_maximum_fusion.4), channel_id=1, source_target_pairs={{0,48},{16,0},{32,16},{48,32},{1,49},{17,1},{33,17},{49,33},{2,50}... | collective-permute-start | bytes 491528 | tf_op jit(solution)/shard_map/ppermute | solution.py:30
  24.1 7.6 %collective-permute-start.6 = (bf16[128,640]{1,0:T(8,128)(2,1)S(1)}, bf16[128,640]{1,0:T(8,128)(2,1)S(1)}, u32[]{:S(2)}, u32[]{:S(2)}) collective-permute-start(bf16[128,640]{1,0:T(8,128)(2,1)S(1)} %pad_maximum_fusion.4), channel_id=1, source_target_pairs={{0,32},{16,48},{32,0},{48,16},{1,33},{17,49},{33,1},{49,17},{2,34}... | collective-permute-start | bytes 491528 | tf_op jit(solution)/shard_map/ppermute | solution.py:30
  25.4 6.3 %collective-permute-start.12 = (bf16[128,640]{1,0:T(8,128)(2,1)S(1)}, bf16[128,640]{1,0:T(8,128)(2,1)S(1)}, u32[]{:S(2)}, u32[]{:S(2)}) collective-permute-start(bf16[128,640]{1,0:T(8,128)(2,1)S(1)} %pad_maximum_fusion.5), channel_id=1, source_target_pairs={{0,4},{4,8},{8,12},{12,0},{1,5},{5,9},{9,13},{13,1},{2,6},{6,10},{... | collective-permute-start | bytes 491528 | tf_op jit(solution)/shard_map/ppermute | solution.py:30
  27.1 6.4 %collective-permute-start.13 = (bf16[128,640]{1,0:T(8,128)(2,1)S(1)}, bf16[128,640]{1,0:T(8,128)(2,1)S(1)}, u32[]{:S(2)}, u32[]{:S(2)}) collective-permute-start(bf16[128,640]{1,0:T(8,128)(2,1)S(1)} %pad_maximum_fusion.5), channel_id=1, source_target_pairs={{0,12},{4,0},{8,4},{12,8},{1,13},{5,1},{9,5},{13,9},{2,14},{6,2},{... | collective-permute-start | bytes 491528 | tf_op jit(solution)/shard_map/ppermute | solution.py:30
  29.5 6.9 %collective-permute-start.14 = (bf16[128,640]{1,0:T(8,128)(2,1)S(1)}, bf16[128,640]{1,0:T(8,128)(2,1)S(1)}, u32[]{:S(2)}, u32[]{:S(2)}) collective-permute-start(bf16[128,640]{1,0:T(8,128)(2,1)S(1)} %pad_maximum_fusion.5), channel_id=1, source_target_pairs={{0,8},{4,12},{8,0},{12,4},{1,9},{5,13},{9,1},{13,5},{2,10},{6,14},... | collective-permute-start | bytes 491528 | tf_op jit(solution)/shard_map/ppermute | solution.py:30
  37.7 372.7 %reduce-scatter.2.cloned.1.call-start = ((), (), s32[]{:S(2)}) async-start(), calls=%async_computation.2 | async-start | bytes 18382848 | tf_op jit(solution)/shard_map/reduce_scatter | solution.py:755
  38.4 10.7 %collective-permute-start.1 = (bf16[128,2048]{1,0:T(8,128)(2,1)S(1)}, bf16[128,2048]{1,0:T(8,128)(2,1)}, u32[]{:S(2)}, u32[]{:S(2)}) collective-permute-start(bf16[128,2048]{1,0:T(8,128)(2,1)S(1)} %copy.33.refs_0_.refs_4_), channel_id=1, source_target_pairs={{0,2},{2,0},{1,3},{3,1},{4,6},{6,4},{5,7},{7,5},{8,10},{10,8},{9,1... | collective-permute-start | bytes 1572872 | tf_op jit(solution)/shard_map/ppermute | solution.py:30
  40.7 28.7 %collective-permute-start.7 = (bf16[4,128,640]{2,1,0:T(8,128)(2,1)S(1)}, bf16[4,128,640]{2,1,0:T(8,128)(2,1)S(1)}, u32[]{:S(2)}, u32[]{:S(2)}) collective-permute-start(bf16[4,128,640]{2,1,0:T(8,128)(2,1)S(1)} %bitcast_dynamic-update-slice_fusion.10), channel_id=1, source_target_pairs={{0,4},{4,8},{8,12},{12,0},{1,5},{5,9},{9,13},{13,1},{2,6},{6,10},{... | collective-permute-start | bytes 1966088 | tf_op jit(solution)/shard_map/ppermute | solution.py:30
  40.8 16.1 %collective-permute-start.8 = (bf16[4,128,640]{2,1,0:T(8,128)(2,1)S(1)}, bf16[4,128,640]{2,1,0:T(8,128)(2,1)S(1)}, u32[]{:S(2)}, u32[]{:S(2)}) collective-permute-start(bf16[4,128,640]{2,1,0:T(8,128)(2,1)S(1)} %bitcast_dynamic-update-slice_fusion.10), channel_id=1, source_target_pairs={{0,12},{4,0},{8,4},{12,8},{1,13},{5,1},{9,5},{13,9},{2,14},{6,2},{... | collective-permute-start | bytes 1966088 | tf_op jit(solution)/shard_map/ppermute | solution.py:30
  43.5 29.7 %collective-permute-start.15 = (bf16[4,128,640]{2,1,0:T(8,128)(2,1)S(1)}, bf16[4,128,640]{2,1,0:T(8,128)(2,1)S(1)}, u32[]{:S(2)}, u32[]{:S(2)}) collective-permute-start(bf16[4,128,640]{2,1,0:T(8,128)(2,1)S(1)} %bitcast_dynamic-update-slice_fusion.6), channel_id=1, source_target_pairs={{0,16},{16,32},{32,48},{48,0},{1,17},{17,33},{33,49},{49,1},{2,18}... | collective-permute-start | bytes 1966088 | tf_op jit(solution)/shard_map/ppermute | solution.py:30
  43.6 29.5 %collective-permute-start.16 = (bf16[4,128,640]{2,1,0:T(8,128)(2,1)S(1)}, bf16[4,128,640]{2,1,0:T(8,128)(2,1)S(1)}, u32[]{:S(2)}, u32[]{:S(2)}) collective-permute-start(bf16[4,128,640]{2,1,0:T(8,128)(2,1)S(1)} %bitcast_dynamic-update-slice_fusion.6), channel_id=1, source_target_pairs={{0,48},{16,0},{32,16},{48,32},{1,49},{17,1},{33,17},{49,33},{2,50}... | collective-permute-start | bytes 1966088 | tf_op jit(solution)/shard_map/ppermute | solution.py:30
  49.1 44.1 %collective-permute-start = (bf16[128,2048]{1,0:T(8,128)(2,1)S(1)}, bf16[128,2048]{1,0:T(8,128)(2,1)S(1)}, u32[]{:S(2)}, u32[]{:S(2)}) collective-permute-start(bf16[128,2048]{1,0:T(8,128)(2,1)S(1)} %copy.33.refs_0_.refs_4_), channel_id=1, source_target_pairs={{0,1},{1,0},{2,3},{3,2},{4,5},{5,4},{6,7},{7,6},{8,9},{9,8},{10,11... | collective-permute-start | bytes 1572872 | tf_op jit(solution)/shard_map/ppermute | solution.py:30
  56.9 36.2 %collective-permute-start.2 = (bf16[128,2048]{1,0:T(8,128)(2,1)}, bf16[128,2048]{1,0:T(8,128)(2,1)}, u32[]{:S(2)}, u32[]{:S(2)}) collective-permute-start(bf16[128,2048]{1,0:T(8,128)(2,1)} %collective-permute-done.1.refs_2_.refs_6_), channel_id=1, source_target_pairs={{0,1},{1,0},{2,3},{3,2},{4,5},{5,4},{6,7},{7,6},{8,9},{9,8},{10,11... | collective-permute-start | bytes 1572872 | tf_op jit(solution)/shard_map/ppermute | solution.py:30
  69.4 12.9 %collective-permute-start.10 = (bf16[2,128,640]{2,1,0:T(8,128)(2,1)S(1)}, bf16[2,128,640]{2,1,0:T(8,128)(2,1)S(1)}, u32[]{:S(2)}, u32[]{:S(2)}) collective-permute-start(bf16[2,128,640]{2,1,0:T(8,128)(2,1)S(1)} %slice.151), channel_id=1, source_target_pairs={{0,12},{4,0},{8,4},{12,8},{1,13},{5,1},{9,5},{13,9},{2,14},{6,2},{... | collective-permute-start | bytes 983048 | tf_op jit(solution)/shard_map/ppermute | solution.py:30
  73.1 9.7 %collective-permute-start.9 = (bf16[2,128,640]{2,1,0:T(8,128)(2,1)S(1)}, bf16[2,128,640]{2,1,0:T(8,128)(2,1)S(1)}, u32[]{:S(2)}, u32[]{:S(2)}) collective-permute-start(bf16[2,128,640]{2,1,0:T(8,128)(2,1)S(1)} %slice.150), channel_id=1, source_target_pairs={{0,4},{4,8},{8,12},{12,0},{1,5},{5,9},{9,13},{13,1},{2,6},{6,10},{... | collective-permute-start | bytes 983048 | tf_op jit(solution)/shard_map/ppermute | solution.py:30
  73.3 10.6 %collective-permute-start.18 = (bf16[2,128,640]{2,1,0:T(8,128)(2,1)S(1)}, bf16[2,128,640]{2,1,0:T(8,128)(2,1)S(1)}, u32[]{:S(2)}, u32[]{:S(2)}) collective-permute-start(bf16[2,128,640]{2,1,0:T(8,128)(2,1)S(1)} %slice.154), channel_id=1, source_target_pairs={{0,48},{16,0},{32,16},{48,32},{1,49},{17,1},{33,17},{49,33},{2,50}... | collective-permute-start | bytes 983048 | tf_op jit(solution)/shard_map/ppermute | solution.py:30
  82.3 10.7 %collective-permute-start.17 = (bf16[2,128,640]{2,1,0:T(8,128)(2,1)S(1)}, bf16[2,128,640]{2,1,0:T(8,128)(2,1)S(1)}, u32[]{:S(2)}, u32[]{:S(2)}) collective-permute-start(bf16[2,128,640]{2,1,0:T(8,128)(2,1)S(1)} %slice.153), channel_id=1, source_target_pairs={{0,16},{16,32},{32,48},{48,0},{1,17},{17,33},{33,49},{49,1},{2,18}... | collective-permute-start | bytes 983048 | tf_op jit(solution)/shard_map/ppermute | solution.py:30
  103.0 10.4 %collective-permute-start.19 = (bf16[512,128]{1,0:T(8,128)(2,1)}, bf16[512,128]{1,0:T(8,128)(2,1)S(1)}, u32[]{:S(2)}, u32[]{:S(2)}) collective-permute-start(bf16[512,128]{1,0:T(8,128)(2,1)} %get-tuple-element.55.refs_0_), channel_id=1, source_target_pairs={{0,4},{4,8},{8,12},{12,0},{1,5},{5,9},{9,13},{13,1},{2,6},{6,10},{... | collective-permute-start | bytes 393224 | tf_op jit(solution)/shard_map/ppermute | solution.py:30
  103.0 16.9 %collective-permute-start.20 = (bf16[512,128]{1,0:T(8,128)(2,1)}, bf16[512,128]{1,0:T(8,128)(2,1)S(1)}, u32[]{:S(2)}, u32[]{:S(2)}) collective-permute-start(bf16[512,128]{1,0:T(8,128)(2,1)} %get-tuple-element.55.refs_0_), channel_id=1, source_target_pairs={{0,8},{4,12},{8,0},{12,4},{1,9},{5,13},{9,1},{13,5},{2,10},{6,14},... | collective-permute-start | bytes 393224 | tf_op jit(solution)/shard_map/ppermute | solution.py:30
  108.6 11.4 %collective-permute-start.21 = (bf16[512,128]{1,0:T(8,128)(2,1)}, bf16[512,128]{1,0:T(8,128)(2,1)S(1)}, u32[]{:S(2)}, u32[]{:S(2)}) collective-permute-start(bf16[512,128]{1,0:T(8,128)(2,1)} %get-tuple-element.55.refs_0_), channel_id=1, source_target_pairs={{0,12},{4,0},{8,4},{12,8},{1,13},{5,1},{9,5},{13,9},{2,14},{6,2},{... | collective-permute-start | bytes 393224 | tf_op jit(solution)/shard_map/ppermute | solution.py:30
  148.9 6.5 %collective-permute-start.23 = (bf16[128,2048]{1,0:T(8,128)(2,1)S(1)}, bf16[128,2048]{1,0:T(8,128)(2,1)S(1)}, u32[]{:S(2)}, u32[]{:S(2)}) collective-permute-start(bf16[128,2048]{1,0:T(8,128)(2,1)S(1)} %get-tuple-element.115), channel_id=1, source_target_pairs={{0,1},{1,0},{2,3},{3,2},{4,5},{5,4},{6,7},{7,6},{8,9},{9,8},{10,11... | collective-permute-start | bytes 1572872 | tf_op jit(solution)/shard_map/ppermute | solution.py:30
  153.2 8.8 %collective-permute-start.22 = (bf16[128,2048]{1,0:T(8,128)(2,1)}, bf16[128,2048]{1,0:T(8,128)(2,1)}, u32[]{:S(2)}, u32[]{:S(2)}) collective-permute-start(bf16[128,2048]{1,0:T(8,128)(2,1)} %get-tuple-element.114), channel_id=1, source_target_pairs={{0,1},{1,0},{2,3},{3,2},{4,5},{5,4},{6,7},{7,6},{8,9},{9,8},{10,11... | collective-permute-start | bytes 1572872 | tf_op jit(solution)/shard_map/ppermute | solution.py:30
  156.3 13.5 %collective-permute-start.24 = (bf16[128,2048]{1,0:T(8,128)(2,1)}, bf16[128,2048]{1,0:T(8,128)(2,1)}, u32[]{:S(2)}, u32[]{:S(2)}) collective-permute-start(bf16[128,2048]{1,0:T(8,128)(2,1)} %add_convert_fusion.4), channel_id=1, source_target_pairs={{0,2},{2,0},{1,3},{3,1},{4,6},{6,4},{5,7},{7,5},{8,10},{10,8},{9,1... | collective-permute-start | bytes 1572872 | tf_op jit(solution)/shard_map/ppermute | solution.py:30
  161.4 19.5 %collective-permute-start.29 = (bf16[128,2048]{1,0:T(8,128)(2,1)}, bf16[128,2048]{1,0:T(8,128)(2,1)S(1)}, u32[]{:S(2)}, u32[]{:S(2)}) collective-permute-start(bf16[128,2048]{1,0:T(8,128)(2,1)} %copy.47.refs_4_), channel_id=1, source_target_pairs={{0,2},{2,0},{1,3},{3,1},{4,6},{6,4},{5,7},{7,5},{8,10},{10,8},{9,1... | collective-permute-start | bytes 1572872 | tf_op jit(solution)/shard_map/ppermute | solution.py:30
  172.4 19.8 %collective-permute-start.26 = (bf16[128,2048]{1,0:T(8,128)(2,1)S(1)}, bf16[128,2048]{1,0:T(8,128)(2,1)S(1)}, u32[]{:S(2)}, u32[]{:S(2)}) collective-permute-start(bf16[128,2048]{1,0:T(8,128)(2,1)S(1)} %get-tuple-element.104.refs_0_.refs_4_), channel_id=1, source_target_pairs={{0,2},{2,0},{1,3},{3,1},{4,6},{6,4},{5,7},{7,5},{8,10},{10,8},{9,1... | collective-permute-start | bytes 1572872 | tf_op jit(solution)/shard_map/ppermute | solution.py:30
  173.3 20.3 %collective-permute-start.28 = (bf16[128,2048]{1,0:T(8,128)(2,1)S(1)}, bf16[128,2048]{1,0:T(8,128)(2,1)S(1)}, u32[]{:S(2)}, u32[]{:S(2)}) collective-permute-start(bf16[128,2048]{1,0:T(8,128)(2,1)S(1)} %copy-done.15), channel_id=1, source_target_pairs={{0,1},{1,0},{2,3},{3,2},{4,5},{5,4},{6,7},{7,6},{8,9},{9,8},{10,11... | collective-permute-start | bytes 1572872 | tf_op jit(solution)/shard_map/ppermute | solution.py:30
  180.9 12.6 %collective-permute-start.30 = (bf16[128,2048]{1,0:T(8,128)(2,1)S(1)}, bf16[128,2048]{1,0:T(8,128)(2,1)S(1)}, u32[]{:S(2)}, u32[]{:S(2)}) collective-permute-start(bf16[128,2048]{1,0:T(8,128)(2,1)S(1)} %collective-permute-done.29.refs_6_), channel_id=1, source_target_pairs={{0,1},{1,0},{2,3},{3,2},{4,5},{5,4},{6,7},{7,6},{8,9},{9,8},{10,11... | collective-permute-start | bytes 1572872 | tf_op jit(solution)/shard_map/ppermute | solution.py:30
  182.9 10.6 %collective-permute-start.25 = (bf16[128,2048]{1,0:T(8,128)(2,1)S(1)}, bf16[128,2048]{1,0:T(8,128)(2,1)S(1)}, u32[]{:S(2)}, u32[]{:S(2)}) collective-permute-start(bf16[128,2048]{1,0:T(8,128)(2,1)S(1)} %get-tuple-element.104.refs_0_.refs_4_), channel_id=1, source_target_pairs={{0,1},{1,0},{2,3},{3,2},{4,5},{5,4},{6,7},{7,6},{8,9},{9,8},{10,11... | collective-permute-start | bytes 1572872 | tf_op jit(solution)/shard_map/ppermute | solution.py:30
  249.0 12.9 %collective-permute-start.34 = (bf16[128,2048]{1,0:T(8,128)(2,1)}, bf16[128,2048]{1,0:T(8,128)(2,1)}, u32[]{:S(2)}, u32[]{:S(2)}) collective-permute-start(bf16[128,2048]{1,0:T(8,128)(2,1)} %get-tuple-element.109), channel_id=1, source_target_pairs={{0,1},{1,0},{2,3},{3,2},{4,5},{5,4},{6,7},{7,6},{8,9},{9,8},{10,11... | collective-permute-start | bytes 1572872 | tf_op jit(solution)/shard_map/ppermute | solution.py:30
  251.5 13.5 %collective-permute-start.36 = (bf16[128,2048]{1,0:T(8,128)(2,1)}, bf16[128,2048]{1,0:T(8,128)(2,1)}, u32[]{:S(2)}, u32[]{:S(2)}) collective-permute-start(bf16[128,2048]{1,0:T(8,128)(2,1)} %add_convert_fusion.2), channel_id=1, source_target_pairs={{0,2},{2,0},{1,3},{3,1},{4,6},{6,4},{5,7},{7,5},{8,10},{10,8},{9,1... | collective-permute-start | bytes 1572872 | tf_op jit(solution)/shard_map/ppermute | solution.py:30
  267.7 12.3 %collective-permute-start.38 = (bf16[128,2048]{1,0:T(8,128)(2,1)S(1)}, bf16[128,2048]{1,0:T(8,128)(2,1)}, u32[]{:S(2)}, u32[]{:S(2)}) collective-permute-start(bf16[128,2048]{1,0:T(8,128)(2,1)S(1)} %get-tuple-element.102.refs_0_.refs_9_), channel_id=1, source_target_pairs={{0,2},{2,0},{1,3},{3,1},{4,6},{6,4},{5,7},{7,5},{8,10},{10,8},{9,1... | collective-permute-start | bytes 1572872 | tf_op jit(solution)/shard_map/ppermute | solution.py:30
  269.8 12.3 %collective-permute-start.33 = (bf16[128,2048]{1,0:T(8,128)(2,1)}, bf16[128,2048]{1,0:T(8,128)(2,1)S(1)}, u32[]{:S(2)}, u32[]{:S(2)}) collective-permute-start(bf16[128,2048]{1,0:T(8,128)(2,1)} %get-tuple-element.111), channel_id=1, source_target_pairs={{0,1},{1,0},{2,3},{3,2},{4,5},{5,4},{6,7},{7,6},{8,9},{9,8},{10,11... | collective-permute-start | bytes 1572872 | tf_op jit(solution)/shard_map/ppermute | solution.py:30
  271.3 11.0 %collective-permute-start.37 = (bf16[128,2048]{1,0:T(8,128)(2,1)S(1)}, bf16[128,2048]{1,0:T(8,128)(2,1)}, u32[]{:S(2)}, u32[]{:S(2)}) collective-permute-start(bf16[128,2048]{1,0:T(8,128)(2,1)S(1)} %get-tuple-element.102.refs_0_.refs_9_), channel_id=1, source_target_pairs={{0,1},{1,0},{2,3},{3,2},{4,5},{5,4},{6,7},{7,6},{8,9},{9,8},{10,11... | collective-permute-start | bytes 1572872 | tf_op jit(solution)/shard_map/ppermute | solution.py:30
  280.0 4.7 %collective-permute-start.39 = (bf16[128,2048]{1,0:T(8,128)(2,1)}, bf16[128,2048]{1,0:T(8,128)(2,1)}, u32[]{:S(2)}, u32[]{:S(2)}) collective-permute-start(bf16[128,2048]{1,0:T(8,128)(2,1)} %collective-permute-done.38.refs_2_.refs_11_), channel_id=1, source_target_pairs={{0,1},{1,0},{2,3},{3,2},{4,5},{5,4},{6,7},{7,6},{8,9},{9,8},{10,11... | collective-permute-start | bytes 1572872 | tf_op jit(solution)/shard_map/ppermute | solution.py:30
  282.1 48.4 %collective-permute-start.32 = (bf16[128,2048]{1,0:T(8,128)(2,1)}, bf16[128,2048]{1,0:T(8,128)(2,1)S(1)}, u32[]{:S(2)}, u32[]{:S(2)}) collective-permute-start(bf16[128,2048]{1,0:T(8,128)(2,1)} %get-tuple-element.112), channel_id=1, source_target_pairs={{0,1},{1,0},{2,3},{3,2},{4,5},{5,4},{6,7},{7,6},{8,9},{9,8},{10,11... | collective-permute-start | bytes 1572872 | tf_op jit(solution)/shard_map/ppermute | solution.py:30
  284.7 31.8 %collective-permute-start.40 = (bf16[128,2048]{1,0:T(8,128)(2,1)S(1)}, bf16[128,2048]{1,0:T(8,128)(2,1)S(1)}, u32[]{:S(2)}, u32[]{:S(2)}) collective-permute-start(bf16[128,2048]{1,0:T(8,128)(2,1)S(1)} %add_convert_fusion.3), channel_id=1, source_target_pairs={{0,2},{2,0},{1,3},{3,1},{4,6},{6,4},{5,7},{7,5},{8,10},{10,8},{9,1... | collective-permute-start | bytes 1572872 | tf_op jit(solution)/shard_map/ppermute | solution.py:30
  289.7 26.9 %collective-permute-start.43 = (bf16[512,512]{1,0:T(8,128)(2,1)}, bf16[512,512]{1,0:T(8,128)(2,1)S(1)}, u32[]{:S(2)}, u32[]{:S(2)}) collective-permute-start(bf16[512,512]{1,0:T(8,128)(2,1)} %get-tuple-element.71), channel_id=1, source_target_pairs={{0,32},{16,48},{32,0},{48,16},{1,33},{17,49},{33,1},{49,17},{2,34}... | collective-permute-start | bytes 1572872 | tf_op jit(solution)/shard_map/ppermute | solution.py:30
  289.7 40.8 %collective-permute-start.42 = (bf16[512,512]{1,0:T(8,128)(2,1)}, bf16[512,512]{1,0:T(8,128)(2,1)S(1)}, u32[]{:S(2)}, u32[]{:S(2)}) collective-permute-start(bf16[512,512]{1,0:T(8,128)(2,1)} %get-tuple-element.72), channel_id=1, source_target_pairs={{0,48},{16,0},{32,16},{48,32},{1,49},{17,1},{33,17},{49,33},{2,50}... | collective-permute-start | bytes 1572872 | tf_op jit(solution)/shard_map/ppermute | solution.py:30
  290.8 39.7 %collective-permute-start.41 = (bf16[512,512]{1,0:T(8,128)(2,1)}, bf16[512,512]{1,0:T(8,128)(2,1)S(1)}, u32[]{:S(2)}, u32[]{:S(2)}) collective-permute-start(bf16[512,512]{1,0:T(8,128)(2,1)} %get-tuple-element.70), channel_id=1, source_target_pairs={{0,16},{16,32},{32,48},{48,0},{1,17},{17,33},{33,49},{49,1},{2,18}... | collective-permute-start | bytes 1572872 | tf_op jit(solution)/shard_map/ppermute | solution.py:30
  316.5 33.7 %collective-permute-start.44 = (bf16[512,128]{1,0:T(8,128)(2,1)S(1)}, bf16[512,128]{1,0:T(8,128)(2,1)S(1)}, u32[]{:S(2)}, u32[]{:S(2)}) collective-permute-start(bf16[512,128]{1,0:T(8,128)(2,1)S(1)} %get-tuple-element.127), channel_id=1, source_target_pairs={{0,12},{4,0},{8,4},{12,8},{1,13},{5,1},{9,5},{13,9},{2,14},{6,2},{... | collective-permute-start | bytes 393224 | tf_op jit(solution)/shard_map/ppermute | solution.py:30
  316.6 33.6 %collective-permute-start.45 = (bf16[512,128]{1,0:T(8,128)(2,1)S(1)}, bf16[512,128]{1,0:T(8,128)(2,1)S(1)}, u32[]{:S(2)}, u32[]{:S(2)}) collective-permute-start(bf16[512,128]{1,0:T(8,128)(2,1)S(1)} %get-tuple-element.126), channel_id=1, source_target_pairs={{0,8},{4,12},{8,0},{12,4},{1,9},{5,13},{9,1},{13,5},{2,10},{6,14},... | collective-permute-start | bytes 393224 | tf_op jit(solution)/shard_map/ppermute | solution.py:30
  330.5 19.8 %collective-permute-start.46 = (bf16[512,128]{1,0:T(8,128)(2,1)S(1)}, bf16[512,128]{1,0:T(8,128)(2,1)S(1)}, u32[]{:S(2)}, u32[]{:S(2)}) collective-permute-start(bf16[512,128]{1,0:T(8,128)(2,1)S(1)} %get-tuple-element.125), channel_id=1, source_target_pairs={{0,4},{4,8},{8,12},{12,0},{1,5},{5,9},{9,13},{13,1},{2,6},{6,10},{... | collective-permute-start | bytes 393224 | tf_op jit(solution)/shard_map/ppermute | solution.py:30
  347.7 35.1 %collective-permute-start.52 = (bf16[512,384]{1,0:T(8,128)(2,1)}, bf16[512,384]{1,0:T(8,128)(2,1)S(1)}, u32[]{:S(2)}, u32[]{:S(2)}) collective-permute-start(bf16[512,384]{1,0:T(8,128)(2,1)} %get-tuple-element.86), channel_id=1, source_target_pairs={{0,8},{4,12},{8,0},{12,4},{1,9},{5,13},{9,1},{13,5},{2,10},{6,14},... | collective-permute-start | bytes 1179656 | tf_op jit(solution)/shard_map/ppermute | solution.py:30
  347.8 37.0 %collective-permute-start.51 = (bf16[512,384]{1,0:T(8,128)(2,1)}, bf16[512,384]{1,0:T(8,128)(2,1)S(1)}, u32[]{:S(2)}, u32[]{:S(2)}) collective-permute-start(bf16[512,384]{1,0:T(8,128)(2,1)} %get-tuple-element.87), channel_id=1, source_target_pairs={{0,12},{4,0},{8,4},{12,8},{1,13},{5,1},{9,5},{13,9},{2,14},{6,2},{... | collective-permute-start | bytes 1179656 | tf_op jit(solution)/shard_map/ppermute | solution.py:30
  354.6 17.9 %collective-permute-start.58 = (bf16[512,256]{1,0:T(8,128)(2,1)}, bf16[512,256]{1,0:T(8,128)(2,1)S(1)}, u32[]{:S(2)}, u32[]{:S(2)}) collective-permute-start(bf16[512,256]{1,0:T(8,128)(2,1)} %get-tuple-element.95), channel_id=1, source_target_pairs={{0,32},{16,48},{32,0},{48,16},{1,33},{17,49},{33,1},{49,17},{2,34}... | collective-permute-start | bytes 786440 | tf_op jit(solution)/shard_map/ppermute | solution.py:30
  357.9 21.8 %collective-permute-start.57 = (bf16[512,256]{1,0:T(8,128)(2,1)}, bf16[512,256]{1,0:T(8,128)(2,1)S(1)}, u32[]{:S(2)}, u32[]{:S(2)}) collective-permute-start(bf16[512,256]{1,0:T(8,128)(2,1)} %get-tuple-element.94), channel_id=1, source_target_pairs={{0,48},{16,0},{32,16},{48,32},{1,49},{17,1},{33,17},{49,33},{2,50}... | collective-permute-start | bytes 786440 | tf_op jit(solution)/shard_map/ppermute | solution.py:30
  358.2 24.3 %collective-permute-start.56 = (bf16[512,256]{1,0:T(8,128)(2,1)}, bf16[512,256]{1,0:T(8,128)(2,1)S(1)}, u32[]{:S(2)}, u32[]{:S(2)}) collective-permute-start(bf16[512,256]{1,0:T(8,128)(2,1)} %get-tuple-element.93), channel_id=1, source_target_pairs={{0,16},{16,32},{32,48},{48,0},{1,17},{17,33},{33,49},{49,1},{2,18}... | collective-permute-start | bytes 786440 | tf_op jit(solution)/shard_map/ppermute | solution.py:30
  372.6 17.0 %collective-permute-start.50 = (bf16[512,384]{1,0:T(8,128)(2,1)S(1)}, bf16[512,384]{1,0:T(8,128)(2,1)S(1)}, u32[]{:S(2)}, u32[]{:S(2)}) collective-permute-start(bf16[512,384]{1,0:T(8,128)(2,1)S(1)} %copy-done.41), channel_id=1, source_target_pairs={{0,4},{4,8},{8,12},{12,0},{1,5},{5,9},{9,13},{13,1},{2,6},{6,10},{... | collective-permute-start | bytes 1179656 | tf_op jit(solution)/shard_map/ppermute | solution.py:30
  379.7 33.8 %collective-permute-start.47 = (bf16[128,2048]{1,0:T(8,128)(2,1)}, bf16[128,2048]{1,0:T(8,128)(2,1)S(1)}, u32[]{:S(2)}, u32[]{:S(2)}) collective-permute-start(bf16[128,2048]{1,0:T(8,128)(2,1)} %get-tuple-element.107), channel_id=1, source_target_pairs={{0,1},{1,0},{2,3},{3,2},{4,5},{5,4},{6,7},{7,6},{8,9},{9,8},{10,11... | collective-permute-start | bytes 1572872 | tf_op jit(solution)/shard_map/ppermute | solution.py:30
  382.5 22.6 %collective-permute-start.48 = (bf16[128,2048]{1,0:T(8,128)(2,1)S(1)}, bf16[128,2048]{1,0:T(8,128)(2,1)S(1)}, u32[]{:S(2)}, u32[]{:S(2)}) collective-permute-start(bf16[128,2048]{1,0:T(8,128)(2,1)S(1)} %get-tuple-element.106), channel_id=1, source_target_pairs={{0,1},{1,0},{2,3},{3,2},{4,5},{5,4},{6,7},{7,6},{8,9},{9,8},{10,11... | collective-permute-start | bytes 1572872 | tf_op jit(solution)/shard_map/ppermute | solution.py:30
  382.7 11.3 %collective-permute-start.61 = (bf16[128,768]{1,0:T(8,128)(2,1)S(1)}, bf16[128,768]{1,0:T(8,128)(2,1)S(1)}, u32[]{:S(2)}, u32[]{:S(2)}) collective-permute-start(bf16[128,768]{1,0:T(8,128)(2,1)S(1)} %get-tuple-element.120), channel_id=1, source_target_pairs={{0,8},{4,12},{8,0},{12,4},{1,9},{5,13},{9,1},{13,5},{2,10},{6,14},... | collective-permute-start | bytes 589832 | tf_op jit(solution)/shard_map/ppermute | solution.py:30
  384.8 9.6 %collective-permute-start.60 = (bf16[128,768]{1,0:T(8,128)(2,1)S(1)}, bf16[128,768]{1,0:T(8,128)(2,1)S(1)}, u32[]{:S(2)}, u32[]{:S(2)}) collective-permute-start(bf16[128,768]{1,0:T(8,128)(2,1)S(1)} %get-tuple-element.121), channel_id=1, source_target_pairs={{0,12},{4,0},{8,4},{12,8},{1,13},{5,1},{9,5},{13,9},{2,14},{6,2},{... | collective-permute-start | bytes 589832 | tf_op jit(solution)/shard_map/ppermute | solution.py:30
  389.6 9.2 %collective-permute-start.59 = (bf16[128,768]{1,0:T(8,128)(2,1)S(1)}, bf16[128,768]{1,0:T(8,128)(2,1)S(1)}, u32[]{:S(2)}, u32[]{:S(2)}) collective-permute-start(bf16[128,768]{1,0:T(8,128)(2,1)S(1)} %get-tuple-element.119), channel_id=1, source_target_pairs={{0,4},{4,8},{8,12},{12,0},{1,5},{5,9},{9,13},{13,1},{2,6},{6,10},{... | collective-permute-start | bytes 589832 | tf_op jit(solution)/shard_map/ppermute | solution.py:30
  394.1 5.0 %collective-permute-start.55 = (bf16[128,384]{1,0:T(8,128)(2,1)S(1)}, bf16[128,384]{1,0:T(8,128)(2,1)S(1)}, u32[]{:S(2)}, u32[]{:S(2)}) collective-permute-start(bf16[128,384]{1,0:T(8,128)(2,1)S(1)} %get-tuple-element.123), channel_id=1, source_target_pairs={{0,32},{16,48},{32,0},{48,16},{1,33},{17,49},{33,1},{49,17},{2,34}... | collective-permute-start | bytes 294920 | tf_op jit(solution)/shard_map/ppermute | solution.py:30
  394.4 6.0 %collective-permute-start.54 = (bf16[128,384]{1,0:T(8,128)(2,1)S(1)}, bf16[128,384]{1,0:T(8,128)(2,1)S(1)}, u32[]{:S(2)}, u32[]{:S(2)}) collective-permute-start(bf16[128,384]{1,0:T(8,128)(2,1)S(1)} %get-tuple-element.124), channel_id=1, source_target_pairs={{0,48},{16,0},{32,16},{48,32},{1,49},{17,1},{33,17},{49,33},{2,50}... | collective-permute-start | bytes 294920 | tf_op jit(solution)/shard_map/ppermute | solution.py:30
  398.8 5.7 %collective-permute-start.53 = (bf16[128,384]{1,0:T(8,128)(2,1)S(1)}, bf16[128,384]{1,0:T(8,128)(2,1)S(1)}, u32[]{:S(2)}, u32[]{:S(2)}) collective-permute-start(bf16[128,384]{1,0:T(8,128)(2,1)S(1)} %get-tuple-element.122), channel_id=1, source_target_pairs={{0,16},{16,32},{32,48},{48,0},{1,17},{17,33},{33,49},{49,1},{2,18}... | collective-permute-start | bytes 294920 | tf_op jit(solution)/shard_map/ppermute | solution.py:30
  404.6 5.6 %collective-permute-start.62 = (bf16[64,1152]{1,0:T(8,128)(2,1)S(1)}, bf16[64,1152]{1,0:T(8,128)(2,1)S(1)}, u32[]{:S(2)}, u32[]{:S(2)}) collective-permute-start(bf16[64,1152]{1,0:T(8,128)(2,1)S(1)} %dynamic-slice_bitcast_fusion.4), channel_id=1, source_target_pairs={{0,64},{64,0},{1,65},{65,1},{2,66},{66,2},{3,67},{67,3},{4,68},{68... | collective-permute-start | bytes 442376 | tf_op jit(solution)/shard_map/ppermute | solution.py:30
  407.1 11.5 %collective-permute-start.49 = (bf16[128,2048]{1,0:T(8,128)(2,1)}, bf16[128,2048]{1,0:T(8,128)(2,1)}, u32[]{:S(2)}, u32[]{:S(2)}) collective-permute-start(bf16[128,2048]{1,0:T(8,128)(2,1)} %add_convert_fusion), channel_id=1, source_target_pairs={{0,2},{2,0},{1,3},{3,1},{4,6},{6,4},{5,7},{7,5},{8,10},{10,8},{9,1... | collective-permute-start | bytes 1572872 | tf_op jit(solution)/shard_map/ppermute | solution.py:30
  411.5 19.8 %collective-permute-start.63 = (bf16[64,4224]{1,0:T(8,128)(2,1)S(1)}, bf16[64,4224]{1,0:T(8,128)(2,1)S(1)}, u32[]{:S(2)}, u32[]{:S(2)}) collective-permute-start(bf16[64,4224]{1,0:T(8,128)(2,1)S(1)} %dynamic-slice_bitcast_fusion), channel_id=1, source_target_pairs={{0,64},{64,0},{1,65},{65,1},{2,66},{66,2},{3,67},{67,3},{4,68},{68... | collective-permute-start | bytes 1622024 | tf_op jit(solution)/shard_map/ppermute | solution.py:30
  (47 other events, 457.4 us)
Sparse Core Ops, SparseCore 0:
  37.8 129.4 all-gather.1
  246.3 146.9 reduce-scatter.1
